TPU v7x, 32 devices: a whole 2x2x4 slice. The times are simulated.
32 devices in a mesh: dp: 16 (over z, x, core), seq: 2 (over y).
Axes of the slice: x: 2, y: 2, z: 4, core: 2. Of those that a mesh axis runs over, the one named last changes fastest.
Arguments:
- queries: bfloat16 [4096, 3072], P(('dp', 'seq')), may hold values from -6 to 6
- key_states: bfloat16 [4096, 3072], P(('dp', 'seq')), may hold values from -6 to 6
- value_states: bfloat16 [4096, 3072], P(('dp', 'seq')), may hold values from -6 to 6
- grad_out: bfloat16 [4096, 2560], P(('dp', 'seq')), may hold values from -6 to 6
- out_weight: bfloat16 [3072, 2560], P('seq', 'dp'), may hold values from -0.109375 to 0.109375
- key_blocks: int32 [24, 4, 4], replicated, may hold values from 0 to 3, as said below
- key_count: int32 [24, 4], replicated, may hold values from 4 to 4
Outputs:
- grad_queries: bfloat16 [4096, 3072], P(('dp', 'seq'))
- grad_keys: bfloat16 [4096, 3072], P(('dp', 'seq'))
- grad_weight: float32 [3072, 2560], P('seq', 'dp')
Inputs may be any that keep to these rules, and one draw needn't show every extreme that they name: The first key_count[h, b] entries of key_blocks[h, b] name distinct key blocks; later entries name the other blocks and are not used. Query blocks 0 and 3 attend all 4 blocks; every other query block attends at most 4 blocks, and some reach 4 for every head.
All inputs are finite; a program needn't handle non-finite values.
Results may differ from a plain program's by a relative error of at most 0.0079.
Values may be sent and summed in bfloat16 or wider, within the bound.
No kernel may reach another device: no remote copies, remote signals or barrier semaphores. Data moves between devices by JAX's collectives and lax.ppermute only.
A program may use at most 128 MiB of HBM per device.

v0:
```python
import jax
import jax.numpy as jnp
from jax import lax
from jax.sharding import PartitionSpec as P

HEADS = 24
HD = 128
BLK = 64
RANDB = 3


def forward_rows(query_rows, key_rows, value_rows, live_keys):
    scores = jnp.einsum(
        "rqd,rkd->rqk", query_rows, key_rows, preferred_element_type=jnp.float32
    ) * HD ** (-0.5)
    if live_keys is not None:
        scores = jnp.where(live_keys[:, None, :], scores, -jnp.inf)
    row_max = jnp.max(scores, axis=-1, keepdims=True)
    expo = jnp.exp(scores - row_max)
    probs = expo / jnp.sum(expo, axis=-1, keepdims=True)
    head_out = jnp.einsum(
        "rqk,rkd->rqd", probs.astype(jnp.bfloat16), value_rows, preferred_element_type=jnp.float32
    )
    return (probs, head_out.astype(jnp.bfloat16))


def backward_rows(query_rows, key_rows, value_rows, grad_rows, probs):
    dprob = jnp.einsum("rqd,rkd->rqk", grad_rows, value_rows, preferred_element_type=jnp.float32)
    row_delta = jnp.sum(probs * dprob, axis=-1, keepdims=True)
    dscore = (probs * (dprob - row_delta) * HD ** (-0.5)).astype(jnp.bfloat16)
    grad_q = jnp.einsum("rqk,rkd->rqd", dscore, key_rows, preferred_element_type=jnp.float32)
    grad_k = jnp.einsum("rqk,rqd->rkd", dscore, query_rows, preferred_element_type=jnp.float32)
    return (grad_q, grad_k)


def arrange(head_item):
    query_head, key_head, value_head, grad_head, block_list, block_count = head_item
    seq_length = query_head.shape[0]
    block_total = seq_length // BLK
    slot_count = min(block_total, 5 + RANDB)
    middle = block_total - 2
    query_blocks = query_head.reshape(block_total, BLK, HD)
    key_blocks_here = key_head.reshape(block_total, BLK, HD)
    value_blocks = value_head.reshape(block_total, BLK, HD)
    grad_blocks = grad_head.reshape(block_total, BLK, HD)
    chosen = block_list[1 : block_total - 1, :slot_count]
    live_keys = jnp.repeat(
        jnp.arange(slot_count)[None, :] < block_count[1 : block_total - 1, None], BLK, axis=1
    )
    mid_keys = key_blocks_here[chosen].reshape(middle, slot_count * BLK, HD)
    mid_values = value_blocks[chosen].reshape(middle, slot_count * BLK, HD)
    middle_group = (
        query_blocks[1 : block_total - 1],
        mid_keys,
        mid_values,
        grad_blocks[1 : block_total - 1],
        live_keys,
    )
    edge_queries = jnp.stack((query_blocks[0], query_blocks[block_total - 1]))
    edge_grads = jnp.stack((grad_blocks[0], grad_blocks[block_total - 1]))
    edge_keys = jnp.broadcast_to(key_head[None], (2, seq_length, HD))
    edge_values = jnp.broadcast_to(value_head[None], (2, seq_length, HD))
    edge_group = (edge_queries, edge_keys, edge_values, edge_grads, None)
    return (middle_group, edge_group, chosen)


def join_rows(edge_part, middle_part):
    return jnp.concatenate((edge_part[:1], middle_part, edge_part[1:]), axis=0).reshape(-1, HD)


def attend_forward(head_item):
    middle_group, edge_group, chosen = arrange(head_item)
    mid_probs, mid_out = forward_rows(
        middle_group[0], middle_group[1], middle_group[2], middle_group[4]
    )
    edge_probs, edge_out = forward_rows(edge_group[0], edge_group[1], edge_group[2], None)
    return join_rows(edge_out, mid_out)


def attend_full(head_item):
    middle_group, edge_group, chosen = arrange(head_item)
    mid_probs, mid_out = forward_rows(
        middle_group[0], middle_group[1], middle_group[2], middle_group[4]
    )
    edge_probs, edge_out = forward_rows(edge_group[0], edge_group[1], edge_group[2], None)
    mid_dq, mid_dk = backward_rows(
        middle_group[0], middle_group[1], middle_group[2], middle_group[3], mid_probs
    )
    edge_dq, edge_dk = backward_rows(
        edge_group[0], edge_group[1], edge_group[2], edge_group[3], edge_probs
    )
    block_total = head_item[0].shape[0] // BLK
    slot_count = chosen.shape[1]
    spread = (chosen[:, :, None] == jnp.arange(block_total)[None, None, :]).astype(jnp.float32)
    key_sum = jnp.einsum(
        "msn,msbd->nbd",
        spread,
        mid_dk.reshape(chosen.shape[0], slot_count, BLK, HD),
        precision=lax.Precision.HIGHEST,
    ).reshape(-1, HD)
    key_sum = key_sum + jnp.sum(edge_dk, axis=0)
    grad_query = join_rows(edge_dq, mid_dq).astype(jnp.bfloat16)
    return (join_rows(edge_out, mid_out), grad_query, key_sum.astype(jnp.bfloat16))


def project_back(whole_grad, out_weight):
    whole_rows = lax.all_gather(out_weight, "dp", axis=1, tiled=True)
    return lax.dot_general(
        whole_grad, whole_rows, (((1,), (1,)), ((), ())), preferred_element_type=jnp.float32
    )


def reduce_grads(head_outputs, whole_grad):
    local_count = head_outputs.shape[0]
    local_sum = jnp.einsum(
        "hld,lc->hdc", head_outputs, whole_grad, preferred_element_type=jnp.float32
    )
    local_sum = local_sum.reshape(local_count * HD, whole_grad.shape[1])
    return lax.psum_scatter(local_sum, "dp", scatter_dimension=1, tiled=True)


def per_device(queries, key_states, value_states, grad_out, out_weight, key_blocks, key_count):
    group_size = lax.axis_size("seq")
    local_heads = HEADS // group_size
    query_all, key_all, value_all = (
        lax.all_to_all(queries, "seq", split_axis=1, concat_axis=0, tiled=True),
        lax.all_to_all(key_states, "seq", split_axis=1, concat_axis=0, tiled=True),
        lax.all_to_all(value_states, "seq", split_axis=1, concat_axis=0, tiled=True),
    )
    whole_grad = lax.all_gather(grad_out, "seq", axis=0, tiled=True)
    seq_length = query_all.shape[0]
    first_head = lax.axis_index("seq") * local_heads
    lists_here = lax.dynamic_slice_in_dim(key_blocks, first_head, local_heads, 0)
    counts_here = lax.dynamic_slice_in_dim(key_count, first_head, local_heads, 0)
    grad_heads = project_back(whole_grad, out_weight).astype(jnp.bfloat16)

    def split_heads(array_in):
        return array_in.reshape(seq_length, local_heads, HD).transpose(1, 0, 2)

    def merge_heads(array_in):
        return array_in.transpose(1, 0, 2).reshape(seq_length, local_heads * HD)

    stacked = (
        split_heads(query_all),
        split_heads(key_all),
        split_heads(value_all),
        split_heads(grad_heads),
        lists_here,
        counts_here,
    )
    head_outputs = lax.map(attend_forward, stacked)
    weight_part = reduce_grads(head_outputs, whole_grad)
    head_outputs, grad_q, grad_k = lax.map(attend_full, stacked)
    grad_queries, grad_keys = (
        lax.all_to_all(merge_heads(grad_q), "seq", split_axis=0, concat_axis=1, tiled=True),
        lax.all_to_all(merge_heads(grad_k), "seq", split_axis=0, concat_axis=1, tiled=True),
    )
    return (grad_queries, grad_keys, weight_part)


def solution(mesh):
    return jax.shard_map(
        per_device,
        mesh=mesh,
        in_specs=(
            P(("dp", "seq"), None),
            P(("dp", "seq"), None),
            P(("dp", "seq"), None),
            P(("dp", "seq"), None),
            P("seq", "dp"),
            P(),
            P(),
        ),
        out_specs=(P(("dp", "seq"), None), P(("dp", "seq"), None), P("seq", "dp")),
        check_vma=False,
    )
```

profile of v0, /device:TPU:0, one launch (start us, length us, event | category | flops | bytes accessed | tf_op | source)
XLA Modules:
  0.0 315.8 jit_solution(18360061737972834253)
XLA Ops:
  7.9 2.4 copy.60
  10.3 4.2 %all-to-all-start = ((bf16[128,2,1536]{0,2,1:T(8,128)(2,1)}), bf16[128,2,1536]{0,2,1:T(8,128)(2,1)S(1)}, u32[]{:S(2)}, u32[]{:S(2)}) async-start(bf16[128,2,1536]{0,2,1:T(8,128)(2,1)} %bitcast.29), calls=%async_computation | async-start | bytes 1572864 | tf_op jit(solution)/shard_map/all_to_all | solution.py:126
  14.5 1.2 copy.62
  15.7 15.0 %all-to-all-done = bf16[128,2,1536]{0,2,1:T(8,128)(2,1)S(1)} async-done(((bf16[128,2,1536]{0,2,1:T(8,128)(2,1)}), bf16[128,2,1536]{0,2,1:T(8,128)(2,1)S(1)}, u32[]{:S(2)}, u32[]{:S(2)}) %all-to-all-start) | async-done | bytes 786464 | tf_op jit(solution)/shard_map/all_to_all | solution.py:126
  30.6 3.5 %all-to-all-start.1 = ((bf16[128,2,1536]{0,2,1:T(8,128)(2,1)}), bf16[128,2,1536]{0,2,1:T(8,128)(2,1)S(1)}, u32[]{:S(2)}, u32[]{:S(2)}) async-start(bf16[128,2,1536]{0,2,1:T(8,128)(2,1)} %bitcast.32), calls=%async_computation.1 | async-start | bytes 1572864 | tf_op jit(solution)/shard_map/all_to_all | solution.py:127
  34.2 1.2 copy.65
  35.4 13.2 %all-to-all-done.1 = bf16[128,2,1536]{0,2,1:T(8,128)(2,1)S(1)} async-done(((bf16[128,2,1536]{0,2,1:T(8,128)(2,1)}), bf16[128,2,1536]{0,2,1:T(8,128)(2,1)S(1)}, u32[]{:S(2)}, u32[]{:S(2)}) %all-to-all-start.1) | async-done | bytes 786464 | tf_op jit(solution)/shard_map/all_to_all | solution.py:127
  48.6 3.5 %all-to-all-start.2 = ((bf16[128,2,1536]{0,2,1:T(8,128)(2,1)}), bf16[128,2,1536]{0,2,1:T(8,128)(2,1)S(1)}, u32[]{:S(2)}, u32[]{:S(2)}) async-start(bf16[128,2,1536]{0,2,1:T(8,128)(2,1)} %bitcast.37), calls=%async_computation.2 | async-start | bytes 1572864 | tf_op jit(solution)/shard_map/all_to_all | solution.py:128
  53.3 6.5 %copy.61 = bf16[2,128,1536]{1,0,2:T(2,128)(2,1)S(1)} copy(bf16[2,128,1536]{1,2,0:T(8,128)(2,1)S(1)} %bitcast.210) | data formatting | bytes 1572864 | tf_op jit(solution)/shard_map/all_to_all | solution.py:126
  60.7 6.5 %copy.63 = bf16[2,128,1536]{1,0,2:T(2,128)(2,1)S(1)} copy(bf16[2,128,1536]{1,2,0:T(8,128)(2,1)S(1)} %bitcast.211) | data formatting | bytes 1572864 | tf_op jit(solution)/shard_map/all_to_all | solution.py:127
  67.7 1.2 copy.70
  68.9 6.7 %copy.66 = bf16[2,128,1536]{1,0,2:T(2,128)(2,1)S(1)} copy(bf16[2,128,1536]{1,2,0:T(8,128)(2,1)S(1)} %bitcast.212) | data formatting | bytes 1572864 | tf_op jit(solution)/shard_map/all_to_all | solution.py:128
  76.6 48.6 %while.23 = (s32[]{:T(128)}, bf16[12,256,128]{2,1,0:T(8,128)(2,1)S(1)}, bf16[12,256,128]{2,1,0:T(8,128)(2,1)S(1)}, bf16[12,256,128]{2,1,0:T(8,128)(2,1)}, bf16[1...) while((s32[]{:T(128)}, ...), condition=%wide.region_13.14_spmd, body=%wide.region_8.0_spmd.sunk | while | flops 42535200 | bytes 2531925 | solution.py:151
  125.2 9.4 %fusion.102 = f32[12,128,2560]{2,1,0:T(8,128)} fusion(bf16[12,256,128]{2,1,0:T(8,128)(2,1)S(1)} %get-tuple-element.90, bf16[256,2560]{1,0:T(8,128)(2,1)} %all-gather.3.cloned.1.call-done), kind=kOutput, calls=%fused_computation.131 | convolution fusion | flops 2013265920 | bytes 17825792 | tf_op jit(solution)/shard_map/hld,lc->hdc/dot_general | solution.py:115
  134.6 15.6 %copy.81 = f32[1536,2560]{0,1:T(8,128)} copy(f32[1536,2560]{1,0:T(8,128)} %bitcast.186) | data formatting | bytes 31457280 | tf_op jit(solution)/shard_map/reshape | solution.py:118
  150.3 1.3 copy-done.3
  151.5 5.4 %convolution_convert_fusion.4 = bf16[256,1536]{1,0:T(8,128)(2,1)S(1)} fusion(bf16[256,2560]{1,0:T(8,128)(2,1)S(1)} %copy-done.3, bf16[1536,2560]{0,1:T(8,128)(2,1)} %all-gather.5.cloned.1.call-done), kind=kOutput, calls=%fused_computation.130 | convolution fusion | flops 2013659136 | bytes 9961472 | tf_op jit(solution)/shard_map/dot_general | solution.py:108
  157.0 1.2 copy.64
  158.4 88.3 %while.22 = (s32[]{:T(128)}, bf16[12,256,128]{2,1,0:T(8,128)(2,1)S(1)}, bf16[12,256,128]{2,1,0:T(8,128)(2,1)S(1)}, bf16[12,256,128]{2,1,0:T(8,128)(2,1)S(1)}, bf...) while((s32[]{:T(128)}, ...), condition=%wide.region_7.8_spmd, body=%wide.region_0.7_spmd.sunk | while | flops 71356480 | bytes 5315289 | solution.py:153
  166.2 0.9 constant_dynamic-slice_fusion.37
  173.6 0.9 constant_dynamic-slice_fusion.37
  181.0 0.9 constant_dynamic-slice_fusion.37
  188.3 1.0 constant_dynamic-slice_fusion.37
  247.2 1.0 copy.74
  248.2 3.5 %all-to-all-start.3 = ((bf16[2,128,1536]{1,2,0:T(8,128)(2,1)}), bf16[2,128,1536]{1,2,0:T(8,128)(2,1)S(1)}, u32[]{:S(2)}, u32[]{:S(2)}) async-start(bf16[2,128,1536]{1,2,0:T(8,128)(2,1)} %copy.74), calls=%async_computation.3 | async-start | bytes 1572864 | tf_op jit(solution)/shard_map/all_to_all | solution.py:155
  252.2 1.0 copy.76
  253.2 8.8 %all-to-all-done.3 = bf16[2,128,1536]{1,2,0:T(8,128)(2,1)S(1)} async-done(((bf16[2,128,1536]{1,2,0:T(8,128)(2,1)}), bf16[2,128,1536]{1,2,0:T(8,128)(2,1)S(1)}, u32[]{:S(2)}, u32[]{:S(2)}) %all-to-all-start.3) | async-done | bytes 786464 | tf_op jit(solution)/shard_map/all_to_all | solution.py:155
  262.1 3.5 %all-to-all-start.4 = ((bf16[2,128,1536]{1,2,0:T(8,128)(2,1)}), bf16[2,128,1536]{1,2,0:T(8,128)(2,1)S(1)}, u32[]{:S(2)}, u32[]{:S(2)}) async-start(bf16[2,128,1536]{1,2,0:T(8,128)(2,1)} %copy.76), calls=%async_computation.4 | async-start | bytes 1572864 | tf_op jit(solution)/shard_map/all_to_all | solution.py:156
  265.6 1.2 copy.82
  266.8 8.3 %all-to-all-done.4 = bf16[2,128,1536]{1,2,0:T(8,128)(2,1)S(1)} async-done(((bf16[2,128,1536]{1,2,0:T(8,128)(2,1)}), bf16[2,128,1536]{1,2,0:T(8,128)(2,1)S(1)}, u32[]{:S(2)}, u32[]{:S(2)}) %all-to-all-start.4) | async-done | bytes 786464 | tf_op jit(solution)/shard_map/all_to_all | solution.py:156
  275.1 1.2 copy.83
  276.3 33.0 %reduce-scatter.2.cloned.1.call-done = f32[1536,160]{0,1:T(8,128)} async-done(((f32[1536,2560]{0,1:T(8,128)}), f32[1536,160]{0,1:T(8,128)}) %reduce-scatter.2.cloned.1.call-update) | async-done | bytes 983056 | tf_op jit(solution)/shard_map/reduce_scatter | solution.py:119
  (706 shorter events, 135.7 us)
Async XLA Ops:
  7.2 45.9 %copy-start = (s32[24,4,4]{0,2,1:T(4,128)S(1)}, s32[24,4,4]{0,2,1:T(4,128)}, u32[]{:S(2)}) copy-start(s32[24,4,4]{0,2,1:T(4,128)} %param.16) | copy-start | bytes 4612
  7.2 118.0 %all-gather.3.cloned.1.call-start = ((), (), s32[]{:S(2)}) async-start(), calls=%async_computation.6 | async-start | bytes 1966080 | tf_op jit(solution)/shard_map/all_gather | solution.py:130
  7.9 6.6 %copy-start.4 = (bf16[128,3072]{1,0:T(8,128)(2,1)S(1)}, bf16[128,3072]{1,0:T(8,128)(2,1)}, u32[]{:S(2)}) copy-start(bf16[128,3072]{1,0:T(8,128)(2,1)} %param.12) | copy-start | bytes 2359300
  10.3 20.4 %all-to-all-start = ((bf16[128,2,1536]{0,2,1:T(8,128)(2,1)}), bf16[128,2,1536]{0,2,1:T(8,128)(2,1)S(1)}, u32[]{:S(2)}, u32[]{:S(2)}) async-start(bf16[128,2,1536]{0,2,1:T(8,128)(2,1)} %bitcast.29), calls=%async_computation | async-start | bytes 1572864 | tf_op jit(solution)/shard_map/all_to_all | solution.py:126
  14.5 19.7 %copy-start.5 = (bf16[128,3072]{1,0:T(8,128)(2,1)S(1)}, bf16[128,3072]{1,0:T(8,128)(2,1)}, u32[]{:S(2)}) copy-start(bf16[128,3072]{1,0:T(8,128)(2,1)} %param.13) | copy-start | bytes 2359300
  30.6 17.9 %all-to-all-start.1 = ((bf16[128,2,1536]{0,2,1:T(8,128)(2,1)}), bf16[128,2,1536]{0,2,1:T(8,128)(2,1)S(1)}, u32[]{:S(2)}, u32[]{:S(2)}) async-start(bf16[128,2,1536]{0,2,1:T(8,128)(2,1)} %bitcast.32), calls=%async_computation.1 | async-start | bytes 1572864 | tf_op jit(solution)/shard_map/all_to_all | solution.py:127
  34.2 18.7 %copy-start.6 = (s32[24,4]{0,1:T(4,128)S(1)}, s32[24,4]{0,1:T(4,128)}, u32[]{:S(2)}) copy-start(s32[24,4]{0,1:T(4,128)} %param.17) | copy-start | bytes 1156
  48.6 20.3 %all-to-all-start.2 = ((bf16[128,2,1536]{0,2,1:T(8,128)(2,1)}), bf16[128,2,1536]{0,2,1:T(8,128)(2,1)S(1)}, u32[]{:S(2)}, u32[]{:S(2)}) async-start(bf16[128,2,1536]{0,2,1:T(8,128)(2,1)} %bitcast.37), calls=%async_computation.2 | async-start | bytes 1572864 | tf_op jit(solution)/shard_map/all_to_all | solution.py:128
  52.1 98.1 %all-gather.5.cloned.1.call-start = ((), (), s32[]{:S(2)}) async-start(), calls=%async_computation.7 | async-start | bytes 8355840 | tf_op jit(solution)/shard_map/all_gather | solution.py:107
  52.9 256.4 %reduce-scatter.2.cloned.1.call-start = ((), (), s32[]{:S(2)}) async-start(), calls=%async_computation.8 | async-start | bytes 16711680 | tf_op jit(solution)/shard_map/reduce_scatter | solution.py:119
  125.2 9.4 %copy-start.2 = (bf16[12,256,128]{2,1,0:T(8,128)(2,1)}, bf16[12,256,128]{2,1,0:T(8,128)(2,1)S(1)}, u32[]{:S(2)}) copy-start(bf16[12,256,128]{2,1,0:T(8,128)(2,1)S(1)} %get-tuple-element.401) | copy-start | bytes 2359300
  150.2 1.3 copy-start.3
  248.2 13.9 %all-to-all-start.3 = ((bf16[2,128,1536]{1,2,0:T(8,128)(2,1)}), bf16[2,128,1536]{1,2,0:T(8,128)(2,1)S(1)}, u32[]{:S(2)}, u32[]{:S(2)}) async-start(bf16[2,128,1536]{1,2,0:T(8,128)(2,1)} %copy.74), calls=%async_computation.3 | async-start | bytes 1572864 | tf_op jit(solution)/shard_map/all_to_all | solution.py:155
  262.1 13.0 %all-to-all-start.4 = ((bf16[2,128,1536]{1,2,0:T(8,128)(2,1)}), bf16[2,128,1536]{1,2,0:T(8,128)(2,1)S(1)}, u32[]{:S(2)}, u32[]{:S(2)}) async-start(bf16[2,128,1536]{1,2,0:T(8,128)(2,1)} %copy.76), calls=%async_computation.4 | async-start | bytes 1572864 | tf_op jit(solution)/shard_map/all_to_all | solution.py:156
  265.6 43.6 %copy-start.1 = (s32[24,4,4]{0,2,1:T(4,128)S(1)}, s32[24,4,4]{0,2,1:T(4,128)}, u32[]{:S(2)}) copy-start(s32[24,4,4]{0,2,1:T(4,128)} %param.16) | copy-start | bytes 4612
Sparse Core Ops, SparseCore 0:
  9.6 35.1 all-gather.2
  55.3 73.9 all-gather.4
  150.4 158.8 reduce-scatter.1
where the time goes:
time: 319 us; the launch traced here: 316 us
  local copies, waits for them, and re-layouts  135 us (42%)
  waiting for transfers between devices  79.7 us (25%)
  matrix products  60.9 us (19%)
  starting transfers between devices  18.5 us (6%)
  between operations  14 us (4%)
  other arithmetic  4.67 us (1%)
    reduce_scatter x1, waiting for transfers between devices, reduce_grads(): return lax.psum_scatter(local_sum, 'dp', scatter_dimension=1, tiled=True)  33 us
    dynamic_slice x72, local copies, waits for them, and re-layouts, per_device(): head_outputs = lax.map(attend_forward, stacked)  21.4 us
    reshape x1, local copies, waits for them, and re-layouts, reduce_grads(): local_sum = local_sum.reshape(local_count * HD, whole_grad.shape[1])  15.6 us
    all_to_all x1, waiting for transfers between devices, per_device(): lax.all_to_all(queries, 'seq', split_axis=1, concat_axis=0, tiled=True)  15 us
    gather x24, local copies, waits for them, and re-layouts, arrange(): mid_keys = key_blocks_here[chosen].reshape(middle, slot_count * BLK, HD)  13.9 us
    gather x24, local copies, waits for them, and re-layouts, arrange(): mid_values = value_blocks[chosen].reshape(middle, slot_count * BLK, HD)  13.8 us
    all_to_all x1, waiting for transfers between devices, per_device(): lax.all_to_all(key_states, 'seq', split_axis=1, concat_axis=0, tiled=True)  13.2 us
    slice x12, local copies, waits for them, and re-layouts, arrange(): grad_blocks[1:block_total - 1]  11.1 us
  transfers between devices with their start and end apart: 8, of which 5 were waited for; matrix products, arithmetic and copies ran while one was open for 63% of the time, Pallas kernels for 0%

commit v1 on v0

v1 whole, which is shorter than its diff:
```python
import functools

import jax
import jax.numpy as jnp
from jax import lax
from jax.experimental import pallas as pl
from jax.experimental.pallas import tpu as pltpu
from jax.sharding import PartitionSpec as P

HEADS = 24
HD = 128
BLK = 64
SCALE = HD ** (-0.5)
QUERY_TILE = 256
VMEM_LIMIT = 48 * 1024 * 1024
GROUP = 4


def dot(left, right, left_dim, right_dim):
    return lax.dot_general(
        left, right, (((left_dim,), (right_dim,)), ((), ())), preferred_element_type=jnp.float32
    )


def softmax_rows(query_rows, key_rows, bias_ref, head, first_block, block_count):
    scores = dot(query_rows, key_rows, 1, 1) * SCALE
    length = key_rows.shape[0]
    bias = jnp.concatenate(
        [
            jnp.broadcast_to(bias_ref[head, block : block + 1, :], (BLK, length))
            for block in range(first_block, first_block + block_count)
        ],
        axis=0,
    )
    scores = scores + bias
    row_max = jnp.max(scores, axis=-1, keepdims=True)
    expo = jnp.exp(scores - row_max)
    return expo * (1.0 / jnp.sum(expo, axis=-1, keepdims=True))


def take_tokens(own_ref, recv_refs, slot, columns):
    return jnp.concatenate(
        [own_ref[:, columns]] + [recv_ref[slot, :, columns] for recv_ref in recv_refs], axis=0
    )


def forward_kernel(heads_step, recv_count, pos_ref, *refs):
    query_ref, key_ref, value_ref = refs[:3]
    recv_refs = refs[3 : 3 + recv_count]
    bias_ref, out_ref = refs[3 + recv_count :]
    length = out_ref.shape[0]
    tile = min(QUERY_TILE, length)
    for head in range(heads_step):
        columns = slice(head * HD, (head + 1) * HD)
        query = take_tokens(query_ref, recv_refs, 0, columns)
        key = take_tokens(key_ref, recv_refs, 1, columns)
        value = take_tokens(value_ref, recv_refs, 2, columns)
        for start in range(0, length, tile):
            rows = slice(start, start + tile)
            probs = softmax_rows(query[rows], key, bias_ref, head, start // BLK, tile // BLK)
            out_ref[rows, columns] = dot(probs.astype(jnp.bfloat16), value, 1, 0).astype(
                jnp.bfloat16
            )


def backward_kernel(heads_step, recv_count, pos_ref, *refs):
    query_ref, key_ref, value_ref = refs[:3]
    recv_refs = refs[3 : 3 + recv_count]
    bias_ref, grad_ref, grad_recv_ref = refs[3 + recv_count : 6 + recv_count]
    out_refs = refs[6 + recv_count :]
    tokens = query_ref.shape[0]
    length = grad_ref.shape[0]
    tile = min(QUERY_TILE, length)
    for head in range(heads_step):
        columns = slice(head * HD, (head + 1) * HD)
        query = take_tokens(query_ref, recv_refs, 0, columns)
        key = take_tokens(key_ref, recv_refs, 1, columns)
        value = take_tokens(value_ref, recv_refs, 2, columns)
        grad_key = None
        for start in range(0, length, tile):
            rows = slice(start, start + tile)
            probs = softmax_rows(query[rows], key, bias_ref, head, start // BLK, tile // BLK)
            grad = grad_ref[rows, columns] + grad_recv_ref[rows, columns].astype(jnp.float32)
            dprob = dot(grad.astype(jnp.bfloat16), value, 1, 1)
            delta = jnp.sum(probs * dprob, axis=-1, keepdims=True)
            dscore = (probs * (dprob - delta) * SCALE).astype(jnp.bfloat16)
            grad_query = dot(dscore, key, 1, 0).astype(jnp.bfloat16)
            for piece in range(tile // tokens):
                out_refs[start // tokens + piece][0, :, columns] = grad_query[
                    piece * tokens : (piece + 1) * tokens
                ]
            part = dot(dscore, query[rows], 0, 0)
            grad_key = part if grad_key is None else grad_key + part
        grad_key = grad_key.astype(jnp.bfloat16)
        for piece in range(length // tokens):
            out_refs[piece][1, :, columns] = grad_key[piece * tokens : (piece + 1) * tokens]


def attention_specs(tokens, seq_size, local_heads, first, heads_step, bias):
    width = heads_step * HD
    own = pl.BlockSpec(
        (tokens, width), lambda h, pos: (0, (pos[0] * local_heads + first) // heads_step + h)
    )
    recv = pl.BlockSpec((3, tokens, width), lambda h, pos: (0, 0, h))
    bias_spec = pl.BlockSpec(
        (heads_step,) + bias.shape[1:], lambda h, pos: (first // heads_step + h, 0, 0)
    )
    return [own] * 3 + [recv] * (seq_size - 1) + [bias_spec]


def attention_cost(count, length, matmuls):
    return pl.CostEstimate(
        flops=count * matmuls * 2 * length * length * HD,
        bytes_accessed=count * length * HD * 2 * 5,
        transcendentals=count * length * length,
    )


def attend_forward(pos, own, recv, bias, first, count, local_heads, heads_step):
    tokens = own[0].shape[0]
    length = bias.shape[2]
    return pl.pallas_call(
        functools.partial(forward_kernel, heads_step, len(recv)),
        grid_spec=pltpu.PrefetchScalarGridSpec(
            num_scalar_prefetch=1,
            grid=(count // heads_step,),
            in_specs=attention_specs(
                tokens, len(recv) + 1, local_heads, first, heads_step, bias
            ),
            out_specs=pl.BlockSpec((length, heads_step * HD), lambda h, pos: (0, h)),
        ),
        out_shape=jax.ShapeDtypeStruct((length, count * HD), jnp.bfloat16),
        compiler_params=pltpu.CompilerParams(vmem_limit_bytes=VMEM_LIMIT),
        cost_estimate=attention_cost(count, length, 2),
        name="attend_forward",
    )(pos, *own, *recv, bias)


def attend_backward(pos, own, recv, bias, grad, grad_recv, first, count, local_heads, heads_step):
    tokens = own[0].shape[0]
    length = bias.shape[2]
    width = heads_step * HD
    grad_spec = pl.BlockSpec((length, width), lambda h, pos: (0, h))
    return pl.pallas_call(
        functools.partial(backward_kernel, heads_step, len(recv)),
        grid_spec=pltpu.PrefetchScalarGridSpec(
            num_scalar_prefetch=1,
            grid=(count // heads_step,),
            in_specs=attention_specs(tokens, len(recv) + 1, local_heads, first, heads_step, bias)
            + [grad_spec, grad_spec],
            out_specs=[
                pl.BlockSpec((2, tokens, width), lambda h, pos: (0, 0, h))
                for _ in range(len(recv) + 1)
            ],
        ),
        out_shape=[
            jax.ShapeDtypeStruct((2, tokens, count * HD), jnp.bfloat16)
            for _ in range(len(recv) + 1)
        ],
        compiler_params=pltpu.CompilerParams(vmem_limit_bytes=VMEM_LIMIT),
        cost_estimate=attention_cost(count, length, 5),
        name="attend_backward",
    )(pos, *own, *recv, bias, grad, grad_recv)


def bit_reversed(count):
    order = [0]
    while len(order) < count:
        order = [2 * value for value in order] + [2 * value + 1 for value in order]
    return order


def swap_with(array_in, axis_name, distance):
    size = lax.axis_size(axis_name)
    return lax.ppermute(array_in, axis_name, [(i, i ^ distance) for i in range(size)])


def mask_bias(lists_here, counts_here, place, seq_size, length):
    block_total = length // BLK
    per_part = block_total // seq_size
    lists_rel = jnp.concatenate(
        [
            lax.dynamic_slice_in_dim(lists_here, (place ^ k) * per_part, per_part, 1)
            for k in range(seq_size)
        ],
        axis=1,
    )
    counts_rel = jnp.concatenate(
        [
            lax.dynamic_slice_in_dim(counts_here, (place ^ k) * per_part, per_part, 1)
            for k in range(seq_size)
        ],
        axis=1,
    )
    token = jnp.arange(length)
    part_tokens = per_part * BLK
    token_block = (place ^ (token // part_tokens)) * per_part + (token % part_tokens) // BLK
    live = jnp.arange(block_total)[None, None, :] < counts_rel[:, :, None]
    hits = (lists_rel[:, :, :, None] == token_block) & live[:, :, :, None]
    return jnp.where(jnp.any(hits, axis=2), 0.0, -jnp.inf).astype(jnp.float32)


def per_device(queries, key_states, value_states, grad_out, out_weight, key_blocks, key_count):
    seq_size = lax.axis_size("seq")
    dp_size = lax.axis_size("dp")
    layers = dp_size // GROUP
    place = lax.axis_index("seq")
    row = lax.axis_index("dp")
    tokens = queries.shape[0]
    length = tokens * seq_size
    local_heads = HEADS // seq_size
    cols = out_weight.shape[1]
    own = (queries, key_states, value_states)
    pos = place.astype(jnp.int32).reshape(1)
    parts = 2 if local_heads % 2 == 0 else 1
    count = local_heads // parts
    heads_step = 2 if count % 2 == 0 else 1
    width = count * HD
    layer_order = bit_reversed(layers)

    def send_heads(part):
        received = []
        for k in range(1, seq_size):
            start = ((place ^ k) * local_heads + part * count) * HD
            sent = jnp.stack([lax.dynamic_slice_in_dim(a, start, width, 1) for a in own])
            received.append(swap_with(sent, "seq", k))
        return received

    def gather_rows(part):
        held = {0: out_weight[part * width : (part + 1) * width].T}
        bit = layers // 2
        while bit:
            for known in sorted(held):
                held[known ^ bit] = swap_with(held[known], "dp", bit * GROUP)
            bit //= 2
        return jnp.concatenate([held[k] for k in layer_order], axis=0)

    def gather_grad():
        turned = grad_out.T.reshape(dp_size, cols, tokens)
        order = jnp.array(
            [
                (layer << 2) | (dx << 1) | dc
                for dx in range(2)
                for dc in range(2)
                for layer in layer_order
            ],
            jnp.int32,
        )
        turned = jnp.take(turned, row ^ order, axis=0, mode="clip")
        turned = turned.reshape(2, 2, layers * cols, tokens)
        from_x = swap_with(turned[1], "dp", 2)
        from_c = swap_with(jnp.stack([turned[0, 1], from_x[1]]), "dp", 1)
        held = jnp.stack([turned[0, 0], from_x[0], from_c[0], from_c[1]])
        pieces = [held] + [swap_with(held, "seq", k) for k in range(1, seq_size)]
        return jnp.concatenate(pieces, axis=2)

    received = [send_heads(part) for part in range(parts)]
    rows_all = [gather_rows(part) for part in range(parts)]
    grad_cols = gather_grad()
    grad_wide = jnp.concatenate([grad_cols[i] for i in range(GROUP)], axis=1)

    first_head = place * local_heads
    bias = mask_bias(
        lax.dynamic_slice_in_dim(key_blocks, first_head, local_heads, 0),
        lax.dynamic_slice_in_dim(key_count, first_head, local_heads, 0),
        place,
        seq_size,
        length,
    )

    weight_parts = []
    own_parts = []
    back_parts = []
    for part in range(parts):
        first = part * count
        outs = attend_forward(
            pos, own, received[part], bias, first, count, local_heads, heads_step
        )
        outs_x = swap_with(outs, "dp", 2)
        outs_c = swap_with(outs, "dp", 1)
        outs_xc = swap_with(outs_x, "dp", 1)
        outs_wide = jnp.concatenate([outs, outs_x, outs_c, outs_xc], axis=0)
        block = grad_wide
        bit = 1
        half = block.shape[0] // 2
        sent = dot(block[half:], outs_wide, 1, 0).astype(jnp.bfloat16)
        kept = dot(block[:half], outs_wide, 1, 0)
        while True:
            kept = kept + swap_with(sent, "dp", bit * GROUP).astype(jnp.float32)
            bit *= 2
            if bit >= layers:
                break
            half = kept.shape[0] // 2
            sent = kept[half:].astype(jnp.bfloat16)
            kept = kept[:half]
        weight_parts.append(kept.T)

        def partial(sequence):
            return dot(grad_cols[sequence], rows_all[part], 0, 0)

        sent = jnp.stack([partial(2), partial(3)]).astype(jnp.bfloat16)
        got = swap_with(sent, "dp", 1).astype(jnp.float32)
        sent = (partial(1) + got[1]).astype(jnp.bfloat16)
        kept = partial(0) + got[0]
        got = swap_with(sent, "dp", 2)
        grads = attend_backward(
            pos, own, received[part], bias, kept, got, first, count, local_heads, heads_step
        )
        own_parts.append(grads[0])
        back_parts.append([swap_with(grads[k], "seq", k) for k in range(1, seq_size)])

    sections = [jnp.concatenate(own_parts, axis=2)] + [
        jnp.concatenate([back_parts[part][k] for part in range(parts)], axis=2)
        for k in range(seq_size - 1)
    ]
    if seq_size == 2:
        both = jnp.where(
            place == 0,
            jnp.concatenate(sections, axis=2),
            jnp.concatenate(sections[::-1], axis=2),
        )
    else:
        stacked = jnp.take(jnp.stack(sections), place ^ jnp.arange(seq_size), axis=0, mode="clip")
        both = stacked.transpose(1, 2, 0, 3).reshape(2, tokens, HEADS * HD)
    return (both[0], both[1], jnp.concatenate(weight_parts, axis=0))


def solution(mesh):
    return jax.shard_map(
        per_device,
        mesh=mesh,
        in_specs=(
            P(("dp", "seq"), None),
            P(("dp", "seq"), None),
            P(("dp", "seq"), None),
            P(("dp", "seq"), None),
            P("seq", "dp"),
            P(),
            P(),
        ),
        out_specs=(P(("dp", "seq"), None), P(("dp", "seq"), None), P("seq", "dp")),
        check_vma=False,
    )
```

time: 319 us -> 137 us (0.43)
  local copies, waits for them, and re-layouts: 135 us -> 8.4 us
  matrix products: 60.9 us -> 15.3 us
  waiting for transfers between devices: 79.7 us -> 62.5 us
  Pallas kernels: 0 us -> 14.3 us
  between operations: 14 us -> 1.15 us
  starting transfers between devices: 18.5 us -> 27.3 us
    ppermute x0 -> x27, waiting for transfers between devices: none -> 62.5 us  [swap_with(): lax.ppermute(array_in, axis_name, [(i, i ^ distance) for i in range(size)])]
    all_to_all x5 -> x0, waiting for transfers between devices: 45.3 us -> none  [the longest x1 15 us: per_device(): lax.all_to_all(queries, 'seq', split_axis=1, concat_axis=0, tiled=True)]
    dot_general x134 -> x12, matrix products: 48.7 us -> 15.3 us  [dot(): lax.dot_general(left, right, (((left_dim,), (right_dim,)), ((), ())), pre...]
    reduce_scatter x1 -> x0, waiting for transfers between devices: 33 us -> none  [reduce_grads(): return lax.psum_scatter(local_sum, 'dp', scatter_dimension=1, tiled=True)]
    ppermute x0 -> x27, starting transfers between devices: none -> 27.3 us  [swap_with(): lax.ppermute(array_in, axis_name, [(i, i ^ distance) for i in range(size)])]
    gather x48 -> x1, local copies, waits for them, and re-layouts: 27.7 us -> 0.67 us  [gather_grad(): turned = jnp.take(turned, row ^ order, axis=0, mode='clip')]
    all_to_all x7 -> x0, local copies, waits for them, and re-layouts: 22.1 us -> none  [the longest x1 6.67 us: per_device(): lax.all_to_all(value_states, 'seq', split_axis=1, concat_axis=0, tiled=True)]
    dynamic_slice x74 -> x2, local copies, waits for them, and re-layouts: 21.5 us -> 0.16 us  [the longest x1 0.08 us: mask_bias(): lax.dynamic_slice_in_dim(lists_here, (place ^ k) * per_part, per_part, 1)]
  transfers between devices with their start and end apart: 8 -> 27, of which waited for: 5 -> 13; matrix products, arithmetic and copies ran while one was open for 63% -> 19% of each run, Pallas kernels for 0% -> 10%
where the time goes in v1:
time: 137 us; the launch traced here: 136 us
  waiting for transfers between devices  62.5 us (46%)
  starting transfers between devices  27.3 us (20%)
  matrix products  15.3 us (11%)
  Pallas kernels  14.3 us (10%)
  local copies, waits for them, and re-layouts  8.4 us (6%)
  other arithmetic  7.14 us (5%)
    ppermute x27, waiting for transfers between devices, swap_with(): lax.ppermute(array_in, axis_name, [(i, i ^ distance) for i in range(size)])  62.5 us
    ppermute x27, starting transfers between devices, swap_with(): lax.ppermute(array_in, axis_name, [(i, i ^ distance) for i in range(size)])  27.3 us
    dot_general x12, matrix products, dot(): lax.dot_general(left, right, (((left_dim,), (right_dim,)), ((), ())), pre...  15.3 us
    pallas_call x2, Pallas kernels, attend_backward(): pl.pallas_call(functools.partial(backward_kernel, heads_step, len(recv)),...  8.03 us
    pallas_call x2, Pallas kernels, attend_forward(): pl.pallas_call(functools.partial(forward_kernel, heads_step, len(recv)),...  6.24 us
  transfers between devices with their start and end apart: 27, of which 13 were waited for; matrix products, arithmetic and copies ran while one was open for 19% of the time, Pallas kernels for 10%

profile of v1, /device:TPU:0, one launch (start us, length us, event | category | flops | bytes accessed | tf_op | source)
XLA Modules:
  0.0 136.1 jit_solution(14814047635200681644)
XLA Ops:
  4.0 3.0 %collective-permute-start.9 = (bf16[3,128,768]{2,1,0:T(8,128)(2,1)}, bf16[3,128,768]{2,1,0:T(8,128)(2,1)S(1)}, u32[]{:S(2)}, u32[]{:S(2)}) collective-permute-start(bf16[3,128,768]{2,1,0:T(8,128)(2,1)} %pad_maximum_fusion.11), channel_id=1, source_target_pairs={{0,1},{1,0},{2,3},{3,2},{4,5},{5,4},{6,7},{7,6},{8,9},{9,8},{10,11... | collective-permute-start | bytes 1769480 | tf_op jit(solution)/shard_map/ppermute | solution.py:175
  11.0 2.6 %collective-permute-start.10 = (bf16[160,768]{1,0:T(8,128)(2,1)}, bf16[160,768]{1,0:T(8,128)(2,1)}, u32[]{:S(2)}, u32[]{:S(2)}) collective-permute-start(bf16[160,768]{1,0:T(8,128)(2,1)} %get-tuple-element.26), channel_id=1, source_target_pairs={{0,16},{2,18},{4,20},{6,22},{8,24},{10,26},{12,28},{14,30},{16,0},... | collective-permute-start | bytes 737288 | tf_op jit(solution)/shard_map/ppermute | solution.py:175
  15.5 2.7 %collective-permute-done.1 = bf16[2,640,128]{2,1,0:T(8,128)(2,1)} collective-permute-done((bf16[2,640,128]{2,1,0:T(8,128)(2,1)}, bf16[2,640,128]{2,1,0:T(8,128)(2,1)}, u32[]{:S(2)}, u32[]{:S(2)}) %collective-permute-start.1) | collective-permute-done | bytes 327712 | tf_op jit(solution)/shard_map/ppermute | solution.py:175
  24.1 1.9 %collective-permute-start.11 = (bf16[160,768]{1,0:T(8,128)(2,1)}, bf16[160,768]{1,0:T(8,128)(2,1)S(1)}, u32[]{:S(2)}, u32[]{:S(2)}) collective-permute-start(bf16[160,768]{1,0:T(8,128)(2,1)} %get-tuple-element.26), channel_id=1, source_target_pairs={{0,8},{2,10},{4,12},{6,14},{8,0},{10,2},{12,4},{14,6},{16,24},{18,... | collective-permute-start | bytes 737288 | tf_op jit(solution)/shard_map/ppermute | solution.py:175
  26.0 3.1 %attend_forward.3 = bf16[256,768]{1,0:T(8,128)(2,1)S(1)} custom-call(s32[1]{0:T(128)} %bitcast.pos_ref, bf16[128,3072]{1,0:T(8,128)(2,1)S(1)} %copy-done, bf16[128,3072]{1,0:T(8,128)(2,1)S(1)} %copy-done.1, bf16[128,3072]{1,0:T(8,128)(2,1)S(1)} %copy-done.2, bf16[3,128,768]{2,1,0:T(8,128)(2,1)S(1)} %collective-permute-done.9.refs_3_, ...), custom_call_target="tpu_custom_call" | custom-call | flops 201326592 | bytes 1966080 | tf_op jit(solution)/shard_map/attend_forward/pallas_call | solution.py:122
  29.2 2.0 %collective-permute-done.10 = bf16[160,768]{1,0:T(8,128)(2,1)} collective-permute-done((bf16[160,768]{1,0:T(8,128)(2,1)}, bf16[160,768]{1,0:T(8,128)(2,1)}, u32[]{:S(2)}, u32[]{:S(2)}) %collective-permute-start.10) | collective-permute-done | bytes 245792 | tf_op jit(solution)/shard_map/ppermute | solution.py:175
  31.2 4.1 %collective-permute-done.4 = bf16[160,768]{1,0:T(8,128)(2,1)} collective-permute-done((bf16[160,768]{1,0:T(8,128)(2,1)}, bf16[160,768]{1,0:T(8,128)(2,1)}, u32[]{:S(2)}, u32[]{:S(2)}) %collective-permute-start.4) | collective-permute-done | bytes 245792 | tf_op jit(solution)/shard_map/ppermute | solution.py:175
  37.3 3.1 %attend_forward.2 = bf16[256,768]{1,0:T(8,128)(2,1)S(1)} custom-call(s32[1]{0:T(128)} %bitcast.pos_ref, bf16[128,3072]{1,0:T(8,128)(2,1)S(1)} %copy-done, bf16[128,3072]{1,0:T(8,128)(2,1)S(1)} %copy-done.1, bf16[128,3072]{1,0:T(8,128)(2,1)S(1)} %copy-done.2, bf16[3,128,768]{2,1,0:T(8,128)(2,1)S(1)} %collective-permute-done.refs_3_, ...), custom_call_target="tpu_custom_call" | custom-call | flops 201326592 | bytes 1966080 | tf_op jit(solution)/shard_map/attend_forward/pallas_call | solution.py:122
  40.4 6.8 %collective-permute-done.3 = bf16[4,640,128]{2,1,0:T(8,128)(2,1)} collective-permute-done((bf16[4,640,128]{2,1,0:T(8,128)(2,1)}, bf16[4,640,128]{2,1,0:T(8,128)(2,1)}, u32[]{:S(2)}, u32[]{:S(2)}) %collective-permute-start.3) | collective-permute-done | bytes 655392 | tf_op jit(solution)/shard_map/ppermute | solution.py:175
  47.2 1.7 %collective-permute-start.22 = (bf16[256,768]{1,0:T(8,128)(2,1)S(1)}, bf16[256,768]{1,0:T(8,128)(2,1)S(1)}, u32[]{:S(2)}, u32[]{:S(2)}) collective-permute-start(bf16[256,768]{1,0:T(8,128)(2,1)S(1)} %attend_forward.3), channel_id=1, source_target_pairs={{0,4},{2,6},{4,0},{6,2},{8,12},{10,14},{12,8},{14,10},{16,20},{18,... | collective-permute-start | bytes 1179656 | tf_op jit(solution)/shard_map/ppermute | solution.py:175
  51.5 7.8 %collective-permute-done.22 = bf16[256,768]{1,0:T(8,128)(2,1)S(1)} collective-permute-done((bf16[256,768]{1,0:T(8,128)(2,1)S(1)}, bf16[256,768]{1,0:T(8,128)(2,1)S(1)}, u32[]{:S(2)}, u32[]{:S(2)}) %collective-permute-start.22) | collective-permute-done | bytes 393248 | tf_op jit(solution)/shard_map/ppermute | solution.py:175
  59.3 1.6 %fusion.5 = bf16[1,256,768]{2,1,0:T(8,128)(2,1)S(1)} fusion(bf16[4,640,256]{2,1,0:T(8,128)(2,1)S(1)} %pad_maximum_fusion.2, bf16[160,768]{1,0:T(8,128)(2,1)S(1)} %collective-permute-done.12, bf16[160,768]{1,0:T(8,128)(2,1)S(1)} %collective-permute-done.11, bf16[160,768]{1,0:T(8,128)(2,1)} %collective-permute-done.10, bf16[160,768]{1,0:T(8,128)(2,1)} %get-tuple-element.26), kind=kOutput, calls=%fused_computation.23 | convolution fusion | flops 255787008 | bytes 1703936 | tf_op jit(solution)/shard_map/dot_general | solution.py:20
  60.9 1.6 %fusion.4 = bf16[1,256,768]{2,1,0:T(8,128)(2,1)S(1)} fusion(bf16[4,640,256]{2,1,0:T(8,128)(2,1)S(1)} %pad_maximum_fusion.2, bf16[160,768]{1,0:T(8,128)(2,1)S(1)} %collective-permute-done.12, bf16[160,768]{1,0:T(8,128)(2,1)S(1)} %collective-permute-done.11, bf16[160,768]{1,0:T(8,128)(2,1)} %collective-permute-done.10, bf16[160,768]{1,0:T(8,128)(2,1)} %get-tuple-element.26), kind=kOutput, calls=%fused_computation.22 | convolution fusion | flops 255787008 | bytes 1703936 | tf_op jit(solution)/shard_map/dot_general | solution.py:20
  63.1 2.9 %collective-permute-done.17 = bf16[256,768]{1,0:T(8,128)(2,1)S(1)} collective-permute-done((bf16[256,768]{1,0:T(8,128)(2,1)S(1)}, bf16[256,768]{1,0:T(8,128)(2,1)S(1)}, u32[]{:S(2)}, u32[]{:S(2)}) %collective-permute-start.17) | collective-permute-done | bytes 393248 | tf_op jit(solution)/shard_map/ppermute | solution.py:175
  66.5 1.6 %fusion.3 = bf16[1,256,768]{2,1,0:T(8,128)(2,1)S(1)} fusion(bf16[4,640,256]{2,1,0:T(8,128)(2,1)S(1)} %pad_maximum_fusion.2, bf16[160,768]{1,0:T(8,128)(2,1)S(1)} %collective-permute-done.6, bf16[160,768]{1,0:T(8,128)(2,1)S(1)} %collective-permute-done.5, bf16[160,768]{1,0:T(8,128)(2,1)} %collective-permute-done.4, bf16[160,768]{1,0:T(8,128)(2,1)} %get-tuple-element.25), kind=kOutput, calls=%fused_computation.21 | convolution fusion | flops 255787008 | bytes 1703936 | tf_op jit(solution)/shard_map/dot_general | solution.py:20
  69.0 1.5 %collective-permute-start.25 = (bf16[320,768]{1,0:T(8,128)(2,1)S(1)}, bf16[320,768]{1,0:T(8,128)(2,1)S(1)}, u32[]{:S(2)}, u32[]{:S(2)}) collective-permute-start(bf16[320,768]{1,0:T(8,128)(2,1)S(1)} %convolution_convert_fusion), channel_id=1, source_target_pairs={{0,8},{2,10},{4,12},{6,14},{8,0},{10,2},{12,4},{14,6},{16,24},{18,... | collective-permute-start | bytes 1474568 | tf_op jit(solution)/shard_map/ppermute | solution.py:175
  71.8 1.6 %fusion.2 = bf16[1,256,768]{2,1,0:T(8,128)(2,1)S(1)} fusion(bf16[4,640,256]{2,1,0:T(8,128)(2,1)S(1)} %pad_maximum_fusion.2, bf16[160,768]{1,0:T(8,128)(2,1)S(1)} %collective-permute-done.6, bf16[160,768]{1,0:T(8,128)(2,1)S(1)} %collective-permute-done.5, bf16[160,768]{1,0:T(8,128)(2,1)} %collective-permute-done.4, bf16[160,768]{1,0:T(8,128)(2,1)} %get-tuple-element.25), kind=kOutput, calls=%fused_computation.20 | convolution fusion | flops 255787008 | bytes 1703936 | tf_op jit(solution)/shard_map/dot_general | solution.py:20
  73.5 9.6 %collective-permute-done.25 = bf16[320,768]{1,0:T(8,128)(2,1)S(1)} collective-permute-done((bf16[320,768]{1,0:T(8,128)(2,1)S(1)}, bf16[320,768]{1,0:T(8,128)(2,1)S(1)}, u32[]{:S(2)}, u32[]{:S(2)}) %collective-permute-start.25) | collective-permute-done | bytes 491552 | tf_op jit(solution)/shard_map/ppermute | solution.py:175
  83.8 2.6 %collective-permute-start.26 = (bf16[160,768]{1,0:T(8,128)(2,1)S(1)}, bf16[160,768]{1,0:T(8,128)(2,1)S(1)}, u32[]{:S(2)}, u32[]{:S(2)}) collective-permute-start(bf16[160,768]{1,0:T(8,128)(2,1)S(1)} %slice.177), channel_id=1, source_target_pairs={{0,16},{2,18},{4,20},{6,22},{8,24},{10,26},{12,28},{14,30},{16,0},... | collective-permute-start | bytes 737288 | tf_op jit(solution)/shard_map/ppermute | solution.py:175
  86.4 11.6 %collective-permute-done.20 = bf16[320,768]{1,0:T(8,128)(2,1)S(1)} collective-permute-done((bf16[320,768]{1,0:T(8,128)(2,1)S(1)}, bf16[320,768]{1,0:T(8,128)(2,1)S(1)}, u32[]{:S(2)}, u32[]{:S(2)}) %collective-permute-start.20) | collective-permute-done | bytes 491552 | tf_op jit(solution)/shard_map/ppermute | solution.py:175
  98.7 1.7 %collective-permute-start.21 = (bf16[160,768]{1,0:T(8,128)(2,1)S(1)}, bf16[160,768]{1,0:T(8,128)(2,1)S(1)}, u32[]{:S(2)}, u32[]{:S(2)}) collective-permute-start(bf16[160,768]{1,0:T(8,128)(2,1)S(1)} %slice.178), channel_id=1, source_target_pairs={{0,16},{2,18},{4,20},{6,22},{8,24},{10,26},{12,28},{14,30},{16,0},... | collective-permute-start | bytes 737288 | tf_op jit(solution)/shard_map/ppermute | solution.py:175
  100.4 1.6 %fusion.1 = bf16[256,768]{1,0:T(8,128)(2,1)S(1)} fusion(f32[2,256,768]{2,1,0:T(8,128)S(1)} %convert_element_type.36, bf16[4,640,256]{2,1,0:T(8,128)(2,1)S(1)} %pad_maximum_fusion.2, bf16[160,768]{1,0:T(8,128)(2,1)S(1)} %collective-permute-done.12, bf16[160,768]{1,0:T(8,128)(2,1)S(1)} %collective-permute-done.11, ...), kind=kOutput, calls=%fused_computation.15 | convolution fusion | flops 255983616 | bytes 2490368 | tf_op jit(solution)/shard_map/dot_general | solution.py:20
  102.0 1.6 %collective-permute-start.14 = (bf16[256,768]{1,0:T(8,128)(2,1)S(1)}, bf16[256,768]{1,0:T(8,128)(2,1)S(1)}, u32[]{:S(2)}, u32[]{:S(2)}) collective-permute-start(bf16[256,768]{1,0:T(8,128)(2,1)S(1)} %fusion.1), channel_id=1, source_target_pairs={{0,4},{2,6},{4,0},{6,2},{8,12},{10,14},{12,8},{14,10},{16,20},{18,... | collective-permute-start | bytes 1179656 | tf_op jit(solution)/shard_map/ppermute | solution.py:175
  103.7 1.6 %fusion = bf16[256,768]{1,0:T(8,128)(2,1)S(1)} fusion(f32[2,256,768]{2,1,0:T(8,128)S(1)} %convert_element_type.34, bf16[4,640,256]{2,1,0:T(8,128)(2,1)S(1)} %pad_maximum_fusion.2, bf16[160,768]{1,0:T(8,128)(2,1)S(1)} %collective-permute-done.6, bf16[160,768]{1,0:T(8,128)(2,1)S(1)} %collective-permute-done.5, bf16[160,768]{1,0:T(8,128)(2,1)} %collective-permute-done.4, ...), kind=kOutput, calls=%fused_computation.14 | convolution fusion | flops 255983616 | bytes 2490368 | tf_op jit(solution)/shard_map/dot_general | solution.py:20
  105.9 1.6 %convolution_add_fusion.3.refs_5_ = f32[256,768]{1,0:T(8,128)S(1)} fusion(f32[2,256,768]{2,1,0:T(8,128)S(1)} %convert_element_type.36, bf16[4,640,256]{2,1,0:T(8,128)(2,1)S(1)} %pad_maximum_fusion.2, bf16[160,768]{1,0:T(8,128)(2,1)S(1)} %collective-permute-done.12, bf16[160,768]{1,0:T(8,128)(2,1)S(1)} %collective-permute-done.11, ...), kind=kOutput, calls=%fused_computation.9 | convolution fusion | flops 255787008 | bytes 2883584 | tf_op jit(solution)/shard_map/dot_general | solution.py:20
  107.5 1.6 %convolution_add_fusion.5.refs_5_ = f32[256,768]{1,0:T(8,128)S(1)} fusion(f32[2,256,768]{2,1,0:T(8,128)S(1)} %convert_element_type.34, bf16[4,640,256]{2,1,0:T(8,128)(2,1)S(1)} %pad_maximum_fusion.2, bf16[160,768]{1,0:T(8,128)(2,1)S(1)} %collective-permute-done.6, bf16[160,768]{1,0:T(8,128)(2,1)S(1)} %collective-permute-done.5, ...), kind=kOutput, calls=%fused_computation.11 | convolution fusion | flops 255787008 | bytes 2883584 | tf_op jit(solution)/shard_map/dot_general | solution.py:20
  109.1 5.0 %collective-permute-done.14.refs_6_ = bf16[256,768]{1,0:T(8,128)(2,1)S(1)} collective-permute-done((bf16[256,768]{1,0:T(8,128)(2,1)S(1)}, bf16[256,768]{1,0:T(8,128)(2,1)S(1)}, u32[]{:S(2)}, u32[]{:S(2)}) %collective-permute-start.14) | collective-permute-done | bytes 393248 | tf_op jit(solution)/shard_map/ppermute | solution.py:175
  114.1 4.0 %attend_backward.3 = (bf16[2,128,768]{2,1,0:T(8,128)(2,1)S(1)}, bf16[2,128,768]{2,1,0:T(8,128)(2,1)S(1)}) custom-call(s32[1]{0:T(128)} %bitcast.pos_ref, bf16[128,3072]{1,0:T(8,128)(2,1)S(1)} %copy-done, bf16[128,3072]{1,0:T(8,128)(2,1)S(1)} %copy-done.1, bf16[128,3072]{1,0:T(8,128)(2,1)S(1)} %copy-done.2, ...), custom_call_target="tpu_custom_call" | custom-call | flops 503316480 | bytes 1966080 | tf_op jit(solution)/shard_map/attend_backward/pallas_call | solution.py:144
  118.2 1.6 %collective-permute-start.16 = (bf16[2,128,768]{2,1,0:T(8,128)(2,1)S(1)}, bf16[2,128,768]{2,1,0:T(8,128)(2,1)S(1)}, u32[]{:S(2)}, u32[]{:S(2)}) collective-permute-start(bf16[2,128,768]{2,1,0:T(8,128)(2,1)S(1)} %get-tuple-element.10), channel_id=1, source_target_pairs={{0,1},{1,0},{2,3},{3,2},{4,5},{5,4},{6,7},{7,6},{8,9},{9,8},{10,11... | collective-permute-start | bytes 1179656 | tf_op jit(solution)/shard_map/ppermute | solution.py:175
  120.4 4.0 %attend_backward.2 = (bf16[2,128,768]{2,1,0:T(8,128)(2,1)S(1)}, bf16[2,128,768]{2,1,0:T(8,128)(2,1)S(1)}) custom-call(s32[1]{0:T(128)} %bitcast.pos_ref, bf16[128,3072]{1,0:T(8,128)(2,1)S(1)} %copy-done, bf16[128,3072]{1,0:T(8,128)(2,1)S(1)} %copy-done.1, bf16[128,3072]{1,0:T(8,128)(2,1)S(1)} %copy-done.2, ...), custom_call_target="tpu_custom_call" | custom-call | flops 503316480 | bytes 1966080 | tf_op jit(solution)/shard_map/attend_backward/pallas_call | solution.py:144
  124.4 1.6 %collective-permute-start.15 = (bf16[2,128,768]{2,1,0:T(8,128)(2,1)S(1)}, bf16[2,128,768]{2,1,0:T(8,128)(2,1)S(1)}, u32[]{:S(2)}, u32[]{:S(2)}) collective-permute-start(bf16[2,128,768]{2,1,0:T(8,128)(2,1)S(1)} %get-tuple-element.9), channel_id=1, source_target_pairs={{0,1},{1,0},{2,3},{3,2},{4,5},{5,4},{6,7},{7,6},{8,9},{9,8},{10,11... | collective-permute-start | bytes 1179656 | tf_op jit(solution)/shard_map/ppermute | solution.py:175
  127.1 7.3 %collective-permute-done.15 = bf16[2,128,768]{2,1,0:T(8,128)(2,1)S(1)} collective-permute-done((bf16[2,128,768]{2,1,0:T(8,128)(2,1)S(1)}, bf16[2,128,768]{2,1,0:T(8,128)(2,1)S(1)}, u32[]{:S(2)}, u32[]{:S(2)}) %collective-permute-start.15) | collective-permute-done | bytes 393248 | tf_op jit(solution)/shard_map/ppermute | solution.py:175
  (104 shorter events, 28.8 us)
Async XLA Ops:
  4.0 20.2 %collective-permute-start.9 = (bf16[3,128,768]{2,1,0:T(8,128)(2,1)}, bf16[3,128,768]{2,1,0:T(8,128)(2,1)S(1)}, u32[]{:S(2)}, u32[]{:S(2)}) collective-permute-start(bf16[3,128,768]{2,1,0:T(8,128)(2,1)} %pad_maximum_fusion.11), channel_id=1, source_target_pairs={{0,1},{1,0},{2,3},{3,2},{4,5},{5,4},{6,7},{7,6},{8,9},{9,8},{10,11... | collective-permute-start | bytes 1769480 | tf_op jit(solution)/shard_map/ppermute | solution.py:175
  8.7 9.5 %collective-permute-start.1 = (bf16[2,640,128]{2,1,0:T(8,128)(2,1)}, bf16[2,640,128]{2,1,0:T(8,128)(2,1)}, u32[]{:S(2)}, u32[]{:S(2)}) collective-permute-start(bf16[2,640,128]{2,1,0:T(8,128)(2,1)} %bitcast.8), channel_id=1, source_target_pairs={{0,4},{2,6},{4,0},{6,2},{8,12},{10,14},{12,8},{14,10},{16,20},{18,... | collective-permute-start | bytes 983048 | tf_op jit(solution)/shard_map/ppermute | solution.py:175
  11.0 20.2 %collective-permute-start.10 = (bf16[160,768]{1,0:T(8,128)(2,1)}, bf16[160,768]{1,0:T(8,128)(2,1)}, u32[]{:S(2)}, u32[]{:S(2)}) collective-permute-start(bf16[160,768]{1,0:T(8,128)(2,1)} %get-tuple-element.26), channel_id=1, source_target_pairs={{0,16},{2,18},{4,20},{6,22},{8,24},{10,26},{12,28},{14,30},{16,0},... | collective-permute-start | bytes 737288 | tf_op jit(solution)/shard_map/ppermute | solution.py:175
  14.5 21.4 %collective-permute-start = (bf16[3,128,768]{2,1,0:T(8,128)(2,1)}, bf16[3,128,768]{2,1,0:T(8,128)(2,1)S(1)}, u32[]{:S(2)}, u32[]{:S(2)}) collective-permute-start(bf16[3,128,768]{2,1,0:T(8,128)(2,1)} %pad_maximum_fusion.10), channel_id=1, source_target_pairs={{0,1},{1,0},{2,3},{3,2},{4,5},{5,4},{6,7},{7,6},{8,9},{9,8},{10,11... | collective-permute-start | bytes 1769480 | tf_op jit(solution)/shard_map/ppermute | solution.py:175
  15.0 20.3 %collective-permute-start.4 = (bf16[160,768]{1,0:T(8,128)(2,1)}, bf16[160,768]{1,0:T(8,128)(2,1)}, u32[]{:S(2)}, u32[]{:S(2)}) collective-permute-start(bf16[160,768]{1,0:T(8,128)(2,1)} %get-tuple-element.25), channel_id=1, source_target_pairs={{0,16},{2,18},{4,20},{6,22},{8,24},{10,26},{12,28},{14,30},{16,0},... | collective-permute-start | bytes 737288 | tf_op jit(solution)/shard_map/ppermute | solution.py:175
  15.5 10.5 %copy-start = (bf16[128,3072]{1,0:T(8,128)(2,1)S(1)}, bf16[128,3072]{1,0:T(8,128)(2,1)}, u32[]{:S(2)}) copy-start(bf16[128,3072]{1,0:T(8,128)(2,1)} %refs_0_.7) | copy-start | bytes 2359300
  15.5 10.5 %copy-start.1 = (bf16[128,3072]{1,0:T(8,128)(2,1)S(1)}, bf16[128,3072]{1,0:T(8,128)(2,1)}, u32[]{:S(2)}) copy-start(bf16[128,3072]{1,0:T(8,128)(2,1)} %refs_1_.7) | copy-start | bytes 2359300
  19.3 1.7 %collective-permute-start.2 = (bf16[2,640,128]{2,1,0:T(8,128)(2,1)S(1)}, bf16[2,640,128]{2,1,0:T(8,128)(2,1)S(1)}, u32[]{:S(2)}, u32[]{:S(2)}) collective-permute-start(bf16[2,640,128]{2,1,0:T(8,128)(2,1)S(1)} %pad_maximum_fusion.12), channel_id=1, source_target_pairs={{0,2},{2,0},{4,6},{6,4},{8,10},{10,8},{12,14},{14,12},{16,18},{18,... | collective-permute-start | bytes 983048 | tf_op jit(solution)/shard_map/ppermute | solution.py:175
  21.9 25.3 %collective-permute-start.3 = (bf16[4,640,128]{2,1,0:T(8,128)(2,1)}, bf16[4,640,128]{2,1,0:T(8,128)(2,1)}, u32[]{:S(2)}, u32[]{:S(2)}) collective-permute-start(bf16[4,640,128]{2,1,0:T(8,128)(2,1)} %pad_maximum_fusion.9), channel_id=1, source_target_pairs={{0,1},{1,0},{2,3},{3,2},{4,5},{5,4},{6,7},{7,6},{8,9},{9,8},{10,11... | collective-permute-start | bytes 1966088 | tf_op jit(solution)/shard_map/ppermute | solution.py:175
  24.1 26.2 %collective-permute-start.11 = (bf16[160,768]{1,0:T(8,128)(2,1)}, bf16[160,768]{1,0:T(8,128)(2,1)S(1)}, u32[]{:S(2)}, u32[]{:S(2)}) collective-permute-start(bf16[160,768]{1,0:T(8,128)(2,1)} %get-tuple-element.26), channel_id=1, source_target_pairs={{0,8},{2,10},{4,12},{6,14},{8,0},{10,2},{12,4},{14,6},{16,24},{18,... | collective-permute-start | bytes 737288 | tf_op jit(solution)/shard_map/ppermute | solution.py:175
  29.1 19.8 %copy-start.4 = (bf16[1,640,128]{2,1,0:T(8,128)(2,1)S(1)}, bf16[1,640,128]{2,1,0:T(8,128)(2,1)}, u32[]{:S(2)}) copy-start(bf16[1,640,128]{2,1,0:T(8,128)(2,1)} %copy-done.3) | copy-start | bytes 491524
  29.2 19.8 %copy-start.6 = (bf16[1,640,128]{2,1,0:T(8,128)(2,1)S(1)}, bf16[1,640,128]{2,1,0:T(8,128)(2,1)}, u32[]{:S(2)}) copy-start(bf16[1,640,128]{2,1,0:T(8,128)(2,1)} %copy-done.5) | copy-start | bytes 491524
  29.2 19.8 %copy-start.8 = (bf16[2,640,128]{2,1,0:T(8,128)(2,1)S(1)}, bf16[2,640,128]{2,1,0:T(8,128)(2,1)}, u32[]{:S(2)}) copy-start(bf16[2,640,128]{2,1,0:T(8,128)(2,1)} %copy-done.7) | copy-start | bytes 983044
  31.2 31.3 %collective-permute-start.5 = (bf16[160,768]{1,0:T(8,128)(2,1)}, bf16[160,768]{1,0:T(8,128)(2,1)S(1)}, u32[]{:S(2)}, u32[]{:S(2)}) collective-permute-start(bf16[160,768]{1,0:T(8,128)(2,1)} %get-tuple-element.25), channel_id=1, source_target_pairs={{0,8},{2,10},{4,12},{6,14},{8,0},{10,2},{12,4},{14,6},{16,24},{18,... | collective-permute-start | bytes 737288 | tf_op jit(solution)/shard_map/ppermute | solution.py:175
  35.3 15.7 %collective-permute-start.12 = (bf16[160,768]{1,0:T(8,128)(2,1)}, bf16[160,768]{1,0:T(8,128)(2,1)S(1)}, u32[]{:S(2)}, u32[]{:S(2)}) collective-permute-start(bf16[160,768]{1,0:T(8,128)(2,1)} %collective-permute-done.10), channel_id=1, source_target_pairs={{0,8},{2,10},{4,12},{6,14},{8,0},{10,2},{12,4},{14,6},{16,24},{18,... | collective-permute-start | bytes 737288 | tf_op jit(solution)/shard_map/ppermute | solution.py:175
  35.9 30.1 %collective-permute-start.6 = (bf16[160,768]{1,0:T(8,128)(2,1)}, bf16[160,768]{1,0:T(8,128)(2,1)S(1)}, u32[]{:S(2)}, u32[]{:S(2)}) collective-permute-start(bf16[160,768]{1,0:T(8,128)(2,1)} %collective-permute-done.4), channel_id=1, source_target_pairs={{0,8},{2,10},{4,12},{6,14},{8,0},{10,2},{12,4},{14,6},{16,24},{18,... | collective-permute-start | bytes 737288 | tf_op jit(solution)/shard_map/ppermute | solution.py:175
  47.2 12.1 %collective-permute-start.22 = (bf16[256,768]{1,0:T(8,128)(2,1)S(1)}, bf16[256,768]{1,0:T(8,128)(2,1)S(1)}, u32[]{:S(2)}, u32[]{:S(2)}) collective-permute-start(bf16[256,768]{1,0:T(8,128)(2,1)S(1)} %attend_forward.3), channel_id=1, source_target_pairs={{0,4},{2,6},{4,0},{6,2},{8,12},{10,14},{12,8},{14,10},{16,20},{18,... | collective-permute-start | bytes 1179656 | tf_op jit(solution)/shard_map/ppermute | solution.py:175
  50.3 17.9 %collective-permute-start.23 = (bf16[256,768]{1,0:T(8,128)(2,1)S(1)}, bf16[256,768]{1,0:T(8,128)(2,1)S(1)}, u32[]{:S(2)}, u32[]{:S(2)}) collective-permute-start(bf16[256,768]{1,0:T(8,128)(2,1)S(1)} %attend_forward.3), channel_id=1, source_target_pairs={{0,2},{2,0},{4,6},{6,4},{8,10},{10,8},{12,14},{14,12},{16,18},{18,... | collective-permute-start | bytes 1179656 | tf_op jit(solution)/shard_map/ppermute | solution.py:175
  51.0 15.0 %collective-permute-start.17 = (bf16[256,768]{1,0:T(8,128)(2,1)S(1)}, bf16[256,768]{1,0:T(8,128)(2,1)S(1)}, u32[]{:S(2)}, u32[]{:S(2)}) collective-permute-start(bf16[256,768]{1,0:T(8,128)(2,1)S(1)} %attend_forward.2), channel_id=1, source_target_pairs={{0,4},{2,6},{4,0},{6,2},{8,12},{10,14},{12,8},{14,10},{16,20},{18,... | collective-permute-start | bytes 1179656 | tf_op jit(solution)/shard_map/ppermute | solution.py:175
  59.3 9.0 %collective-permute-start.24 = (bf16[256,768]{1,0:T(8,128)(2,1)S(1)}, bf16[256,768]{1,0:T(8,128)(2,1)S(1)}, u32[]{:S(2)}, u32[]{:S(2)}) collective-permute-start(bf16[256,768]{1,0:T(8,128)(2,1)S(1)} %collective-permute-done.22), channel_id=1, source_target_pairs={{0,2},{2,0},{4,6},{6,4},{8,10},{10,8},{12,14},{14,12},{16,18},{18,... | collective-permute-start | bytes 1179656 | tf_op jit(solution)/shard_map/ppermute | solution.py:175
  62.5 8.0 %collective-permute-start.18 = (bf16[256,768]{1,0:T(8,128)(2,1)S(1)}, bf16[256,768]{1,0:T(8,128)(2,1)S(1)}, u32[]{:S(2)}, u32[]{:S(2)}) collective-permute-start(bf16[256,768]{1,0:T(8,128)(2,1)S(1)} %attend_forward.2), channel_id=1, source_target_pairs={{0,2},{2,0},{4,6},{6,4},{8,10},{10,8},{12,14},{14,12},{16,18},{18,... | collective-permute-start | bytes 1179656 | tf_op jit(solution)/shard_map/ppermute | solution.py:175
  66.0 4.5 %collective-permute-start.19 = (bf16[256,768]{1,0:T(8,128)(2,1)S(1)}, bf16[256,768]{1,0:T(8,128)(2,1)S(1)}, u32[]{:S(2)}, u32[]{:S(2)}) collective-permute-start(bf16[256,768]{1,0:T(8,128)(2,1)S(1)} %collective-permute-done.17), channel_id=1, source_target_pairs={{0,2},{2,0},{4,6},{6,4},{8,10},{10,8},{12,14},{14,12},{16,18},{18,... | collective-permute-start | bytes 1179656 | tf_op jit(solution)/shard_map/ppermute | solution.py:175
  66.0 34.4 %collective-permute-start.13 = (bf16[2,256,768]{2,1,0:T(8,128)(2,1)S(1)}, bf16[2,256,768]{2,1,0:T(8,128)(2,1)S(1)}, u32[]{:S(2)}, u32[]{:S(2)}) collective-permute-start(bf16[2,256,768]{2,1,0:T(8,128)(2,1)S(1)} %pad_maximum_fusion.8), channel_id=1, source_target_pairs={{0,2},{2,0},{4,6},{6,4},{8,10},{10,8},{12,14},{14,12},{16,18},{18,... | collective-permute-start | bytes 2359304 | tf_op jit(solution)/shard_map/ppermute | solution.py:175
  69.0 14.2 %collective-permute-start.25 = (bf16[320,768]{1,0:T(8,128)(2,1)S(1)}, bf16[320,768]{1,0:T(8,128)(2,1)S(1)}, u32[]{:S(2)}, u32[]{:S(2)}) collective-permute-start(bf16[320,768]{1,0:T(8,128)(2,1)S(1)} %convolution_convert_fusion), channel_id=1, source_target_pairs={{0,8},{2,10},{4,12},{6,14},{8,0},{10,2},{12,4},{14,6},{16,24},{18,... | collective-permute-start | bytes 1474568 | tf_op jit(solution)/shard_map/ppermute | solution.py:175
  71.2 26.8 %collective-permute-start.20 = (bf16[320,768]{1,0:T(8,128)(2,1)S(1)}, bf16[320,768]{1,0:T(8,128)(2,1)S(1)}, u32[]{:S(2)}, u32[]{:S(2)}) collective-permute-start(bf16[320,768]{1,0:T(8,128)(2,1)S(1)} %convolution_convert_fusion.1), channel_id=1, source_target_pairs={{0,8},{2,10},{4,12},{6,14},{8,0},{10,2},{12,4},{14,6},{16,24},{18,... | collective-permute-start | bytes 1474568 | tf_op jit(solution)/shard_map/ppermute | solution.py:175
  73.5 30.1 %collective-permute-start.7 = (bf16[2,256,768]{2,1,0:T(8,128)(2,1)S(1)}, bf16[2,256,768]{2,1,0:T(8,128)(2,1)S(1)}, u32[]{:S(2)}, u32[]{:S(2)}) collective-permute-start(bf16[2,256,768]{2,1,0:T(8,128)(2,1)S(1)} %pad_maximum_fusion.7), channel_id=1, source_target_pairs={{0,2},{2,0},{4,6},{6,4},{8,10},{10,8},{12,14},{14,12},{16,18},{18,... | collective-permute-start | bytes 2359304 | tf_op jit(solution)/shard_map/ppermute | solution.py:175
  83.8 25.2 %collective-permute-start.26 = (bf16[160,768]{1,0:T(8,128)(2,1)S(1)}, bf16[160,768]{1,0:T(8,128)(2,1)S(1)}, u32[]{:S(2)}, u32[]{:S(2)}) collective-permute-start(bf16[160,768]{1,0:T(8,128)(2,1)S(1)} %slice.177), channel_id=1, source_target_pairs={{0,16},{2,18},{4,20},{6,22},{8,24},{10,26},{12,28},{14,30},{16,0},... | collective-permute-start | bytes 737288 | tf_op jit(solution)/shard_map/ppermute | solution.py:175
  98.7 27.4 %collective-permute-start.21 = (bf16[160,768]{1,0:T(8,128)(2,1)S(1)}, bf16[160,768]{1,0:T(8,128)(2,1)S(1)}, u32[]{:S(2)}, u32[]{:S(2)}) collective-permute-start(bf16[160,768]{1,0:T(8,128)(2,1)S(1)} %slice.178), channel_id=1, source_target_pairs={{0,16},{2,18},{4,20},{6,22},{8,24},{10,26},{12,28},{14,30},{16,0},... | collective-permute-start | bytes 737288 | tf_op jit(solution)/shard_map/ppermute | solution.py:175
  102.0 12.1 %collective-permute-start.14 = (bf16[256,768]{1,0:T(8,128)(2,1)S(1)}, bf16[256,768]{1,0:T(8,128)(2,1)S(1)}, u32[]{:S(2)}, u32[]{:S(2)}) collective-permute-start(bf16[256,768]{1,0:T(8,128)(2,1)S(1)} %fusion.1), channel_id=1, source_target_pairs={{0,4},{2,6},{4,0},{6,2},{8,12},{10,14},{12,8},{14,10},{16,20},{18,... | collective-permute-start | bytes 1179656 | tf_op jit(solution)/shard_map/ppermute | solution.py:175
  105.3 15.1 %collective-permute-start.8 = (bf16[256,768]{1,0:T(8,128)(2,1)S(1)}, bf16[256,768]{1,0:T(8,128)(2,1)S(1)}, u32[]{:S(2)}, u32[]{:S(2)}) collective-permute-start(bf16[256,768]{1,0:T(8,128)(2,1)S(1)} %fusion), channel_id=1, source_target_pairs={{0,4},{2,6},{4,0},{6,2},{8,12},{10,14},{12,8},{14,10},{16,20},{18,... | collective-permute-start | bytes 1179656 | tf_op jit(solution)/shard_map/ppermute | solution.py:175
  118.2 9.0 %collective-permute-start.16 = (bf16[2,128,768]{2,1,0:T(8,128)(2,1)S(1)}, bf16[2,128,768]{2,1,0:T(8,128)(2,1)S(1)}, u32[]{:S(2)}, u32[]{:S(2)}) collective-permute-start(bf16[2,128,768]{2,1,0:T(8,128)(2,1)S(1)} %get-tuple-element.10), channel_id=1, source_target_pairs={{0,1},{1,0},{2,3},{3,2},{4,5},{5,4},{6,7},{7,6},{8,9},{9,8},{10,11... | collective-permute-start | bytes 1179656 | tf_op jit(solution)/shard_map/ppermute | solution.py:175
  124.4 10.0 %collective-permute-start.15 = (bf16[2,128,768]{2,1,0:T(8,128)(2,1)S(1)}, bf16[2,128,768]{2,1,0:T(8,128)(2,1)S(1)}, u32[]{:S(2)}, u32[]{:S(2)}) collective-permute-start(bf16[2,128,768]{2,1,0:T(8,128)(2,1)S(1)} %get-tuple-element.9), channel_id=1, source_target_pairs={{0,1},{1,0},{2,3},{3,2},{4,5},{5,4},{6,7},{7,6},{8,9},{9,8},{10,11... | collective-permute-start | bytes 1179656 | tf_op jit(solution)/shard_map/ppermute | solution.py:175
  (9 other events, 45.8 us)

commit v2 on v0

v2 whole, which is shorter than its diff:
```python
import functools
import math

import jax
import jax.numpy as jnp
from jax import lax
from jax.experimental import pallas as pl
from jax.experimental.pallas import tpu as pltpu
from jax.sharding import PartitionSpec as P

HEADS = 24
HD = 128
BLK = 64
SCALE = HD ** (-0.5)
QUERY_TILE = 256
VMEM_LIMIT = 16 * 1024 * 1024
COLLECT_VMEM = 63 * 1024 * 1024
GROUP = 4
SMALL_COST = pl.CostEstimate(flops=0, bytes_accessed=0, transcendentals=0)
PARTS = (6, 6)


def dot(left, right, left_dim, right_dim):
    return lax.dot_general(
        left, right, (((left_dim,), (right_dim,)), ((), ())), preferred_element_type=jnp.float32
    )


def whole(count, space=pltpu.VMEM):
    return [pl.BlockSpec(memory_space=space)] * count


def mask_rows(mask_ref, place, head, block_total, per_part):
    blocks = [
        (place ^ (block // per_part)) * per_part + block % per_part for block in range(block_total)
    ]
    bits = [mask_ref[head, block] for block in blocks]
    lane = lax.div(lax.broadcasted_iota(jnp.int32, (1, block_total * BLK), 1), jnp.int32(BLK))
    rows = []
    for block in blocks:
        row = jnp.zeros(lane.shape, jnp.float32)
        for query_block in range(block_total):
            allowed = lax.shift_right_logical(bits[query_block], block) & 1
            value = jnp.where(allowed == 1, 0.0, -jnp.inf).astype(jnp.float32)
            row = jnp.where(lane == query_block, value, row)
        rows.append(row)
    return rows


def softmax_columns(key_rows, query_rows, mask, queries):
    scores = dot(key_rows, query_rows, 1, 1) * SCALE
    bias = jnp.concatenate(
        [jnp.broadcast_to(row[:, queries], (BLK, scores.shape[1])) for row in mask], axis=0
    )
    scores = scores + bias
    column_max = jnp.max(scores, axis=0, keepdims=True)
    expo = jnp.exp(scores - column_max)
    return expo * (1.0 / jnp.sum(expo, axis=0, keepdims=True))


def each_head(count, body):
    step = 4 if count % 4 == 0 else 3 if count % 3 == 0 else 2 if count % 2 == 0 else 1

    def run(index, carry):
        for offset in range(step):
            body(index * step + offset)
        return carry

    lax.fori_loop(0, count // step, run, 0)


def head_tokens(piece_refs, columns):
    return [
        jnp.concatenate([piece_ref[slot, :, columns] for piece_ref in piece_refs], axis=0)
        for slot in range(3)
    ]


def lanes(head):
    return pl.ds(pl.multiple_of(head * HD, HD), HD)


def forward_kernel(first, count, local_heads, pos_ref, mask_ref, *refs):
    piece_refs, (out_ref, probs_ref) = refs[:-2], refs[-2:]
    length = out_ref.shape[1]
    tokens = length // len(piece_refs)
    tile = min(QUERY_TILE, length)
    place = pos_ref[0]

    def one(head):
        query, key, value = head_tokens(piece_refs, lanes(head))
        mask = mask_rows(
            mask_ref, place, place * local_heads + first + head, length // BLK, tokens // BLK
        )
        for start in range(0, length, tile):
            rows = slice(start, start + tile)
            probs = softmax_columns(key, query[rows], mask, rows)
            probs_ref[head, :, rows] = probs
            out_ref[lanes(head), rows] = dot(value, probs.astype(jnp.bfloat16), 0, 0).astype(
                jnp.bfloat16
            )

    each_head(count, one)


def backward_kernel(count, pieces, *refs):
    piece_refs, (probs_ref, grad_ref, grad_recv_ref) = refs[:pieces], refs[pieces : pieces + 3]
    out_refs = refs[pieces + 3 :]
    length = grad_ref.shape[0]
    tokens = length // pieces
    tile = min(QUERY_TILE, length)

    def one(head):
        columns = lanes(head)
        query, key, value = head_tokens(piece_refs, columns)
        grad_key = None
        for start in range(0, length, tile):
            rows = slice(start, start + tile)
            probs = probs_ref[head, :, rows]
            grad = grad_ref[rows, columns] + grad_recv_ref[rows, columns].astype(jnp.float32)
            dprob = dot(value, grad.astype(jnp.bfloat16), 1, 1)
            delta = jnp.sum(probs * dprob, axis=0, keepdims=True)
            dscore = (probs * (dprob - delta) * SCALE).astype(jnp.bfloat16)
            grad_query = dot(dscore, key, 0, 0).astype(jnp.bfloat16)
            for piece in range(tile // tokens):
                out_refs[start // tokens + piece][0, :, columns] = grad_query[
                    piece * tokens : (piece + 1) * tokens
                ]
            part = dot(dscore, query[rows], 1, 0)
            grad_key = part if grad_key is None else grad_key + part
        grad_key = grad_key.astype(jnp.bfloat16)
        for piece in range(length // tokens):
            out_refs[piece][1, :, columns] = grad_key[piece * tokens : (piece + 1) * tokens]

    each_head(count, one)


def attend_forward(pos, mask, pieces, first, count, local_heads):
    length = pieces[0].shape[1] * len(pieces)
    return pl.pallas_call(
        functools.partial(forward_kernel, first, count, local_heads),
        in_specs=whole(2, pltpu.SMEM) + whole(len(pieces)),
        out_specs=whole(2),
        out_shape=[
            jax.ShapeDtypeStruct((count * HD, length), jnp.bfloat16),
            jax.ShapeDtypeStruct((count, length, length), jnp.float32),
        ],
        compiler_params=pltpu.CompilerParams(vmem_limit_bytes=VMEM_LIMIT),
        cost_estimate=SMALL_COST,
        name="attend_forward",
    )(pos, mask, *pieces)


def attend_backward(pieces, probs, grad, grad_recv, count):
    tokens = pieces[0].shape[1]
    return pl.pallas_call(
        functools.partial(backward_kernel, count, len(pieces)),
        in_specs=whole(3 + len(pieces)),
        out_specs=whole(len(pieces)),
        out_shape=[jax.ShapeDtypeStruct((2, tokens, count * HD), jnp.bfloat16)] * len(pieces),
        compiler_params=pltpu.CompilerParams(vmem_limit_bytes=VMEM_LIMIT),
        cost_estimate=SMALL_COST,
        name="attend_backward",
    )(*pieces, probs, grad, grad_recv)


def collect_kernel(local_heads, pieces, pos_ref, *refs):
    sources, out_refs, sems = refs[:3], refs[3:-1], refs[-1]
    copies = []
    for out_ref, (distance, first, count) in zip(out_refs, pieces):
        start = pl.multiple_of(((pos_ref[0] ^ distance) * local_heads + first) * HD, HD)
        for slot, source in enumerate(sources):
            copies.append(
                pltpu.make_async_copy(
                    source.at[:, pl.ds(start, count * HD)],
                    out_ref.at[slot],
                    sems.at[len(copies)],
                )
            )
    for copy in copies:
        copy.start()
    for copy in copies:
        copy.wait()


def pick_kernel(local_heads, pieces, pos_ref, *refs):
    sources, out_refs = refs[:3], refs[3:]
    for out_ref, (distance, first, count) in zip(out_refs, pieces):
        start = pl.multiple_of(((pos_ref[0] ^ distance) * local_heads + first) * HD, HD)
        for slot, source in enumerate(sources):
            out_ref[slot] = source[:, pl.ds(start, count * HD)]


def pick_columns(pos, sources, local_heads, pieces):
    tokens = sources[0].shape[0]
    return pl.pallas_call(
        functools.partial(pick_kernel, local_heads, pieces),
        in_specs=whole(1, pltpu.SMEM) + whole(len(sources)),
        out_specs=whole(len(pieces)),
        out_shape=[
            jax.ShapeDtypeStruct((len(sources), tokens, count * HD), sources[0].dtype)
            for _, _, count in pieces
        ],
        compiler_params=pltpu.CompilerParams(vmem_limit_bytes=VMEM_LIMIT),
        cost_estimate=SMALL_COST,
        name="pick_columns",
    )(pos, *sources)


def collect_columns(pos, sources, local_heads, pieces):
    tokens = sources[0].shape[0]
    shapes = [(len(sources), tokens, count * HD) for _, _, count in pieces]
    return pl.pallas_call(
        functools.partial(collect_kernel, local_heads, pieces),
        in_specs=whole(1, pltpu.SMEM) + whole(len(sources), pltpu.HBM),
        out_specs=whole(len(pieces)),
        out_shape=[jax.ShapeDtypeStruct(shape, sources[0].dtype) for shape in shapes],
        scratch_shapes=[pltpu.SemaphoreType.DMA((len(sources) * len(pieces),))],
        compiler_params=pltpu.CompilerParams(vmem_limit_bytes=COLLECT_VMEM),
        cost_estimate=SMALL_COST,
        name="collect_columns",
    )(pos, *sources)


def turn_kernel(row_ref, grad_ref, near_ref, far_ref, held_ref):
    blocks, cols, _ = held_ref.shape
    layers = blocks // GROUP
    for block in range(blocks):
        held_ref[block] = grad_ref[:, block * cols : (block + 1) * cols].T
    for dc in range(2):
        for slot, layer in enumerate(bit_reversed(layers)):
            rows = slice(slot * cols, (slot + 1) * cols)
            near_ref[dc, rows] = held_ref[row_ref[0] ^ (GROUP * layer + dc)]
            far_ref[dc, rows] = held_ref[row_ref[0] ^ (GROUP * layer + 2 + dc)]


def turn_columns(row, grad, dp_size):
    tokens, cols = grad.shape[0], grad.shape[1] // dp_size
    layers = dp_size // GROUP
    if cols % 16:
        turned = grad.T.reshape(dp_size, cols, tokens)
        order = [GROUP * layer + kind for kind in range(GROUP) for layer in bit_reversed(layers)]
        turned = jnp.take(turned, row ^ jnp.array(order, jnp.int32), axis=0, mode="clip")
        turned = turned.reshape(2, 2, layers * cols, tokens)
        return turned[0], turned[1]
    return pl.pallas_call(
        turn_kernel,
        in_specs=whole(1, pltpu.SMEM) + whole(1),
        out_specs=whole(2),
        out_shape=[jax.ShapeDtypeStruct((2, layers * cols, tokens), grad.dtype)] * 2,
        scratch_shapes=[pltpu.VMEM((dp_size, cols, tokens), grad.dtype)],
        compiler_params=pltpu.CompilerParams(vmem_limit_bytes=VMEM_LIMIT),
        cost_estimate=SMALL_COST,
        name="turn_columns",
    )(row.astype(jnp.int32).reshape(1), grad)


def join_kernel(*refs):
    piece_refs, wide_ref, turned_ref = refs[:-2], refs[-2], refs[-1]
    tokens = piece_refs[0].shape[2]
    column = 0
    for sequence in range(2):
        for piece_ref in piece_refs:
            piece = piece_ref[sequence]
            wide_ref[:, column : column + tokens] = piece
            turned_ref[column : column + tokens, :] = piece.T
            column += tokens


def join_pieces(pieces):
    _, depth, tokens = pieces[0].shape
    width = 2 * tokens * len(pieces)
    return pl.pallas_call(
        join_kernel,
        in_specs=whole(len(pieces)),
        out_specs=whole(2),
        out_shape=[
            jax.ShapeDtypeStruct((depth, width), jnp.bfloat16),
            jax.ShapeDtypeStruct((width, depth), jnp.bfloat16),
        ],
        compiler_params=pltpu.CompilerParams(vmem_limit_bytes=VMEM_LIMIT),
        cost_estimate=SMALL_COST,
        name="join_pieces",
    )(*pieces)


def partial_kernel(first, count, grad_ref, grad_core_ref, *refs):
    weight_refs, (kept_ref, sent_ref) = refs[:-2], refs[-2:]
    length = kept_ref.shape[0]
    grad = jnp.concatenate([grad_ref[...], grad_core_ref[...]], axis=1)
    width = 2 * HD if count % 2 == 0 else HD
    for start in range(0, count * HD, width):
        rows = slice(first * HD + start, first * HD + start + width)
        weight = jnp.concatenate([weight_ref[:, rows] for weight_ref in weight_refs], axis=0)
        columns = slice(start, start + width)
        total = dot(grad, weight, 1, 0)
        kept_ref[:, columns] = total[:length]
        sent_ref[:, columns] = total[length:].astype(jnp.bfloat16)


def partial_heads(weights, grad, grad_core, first, count):
    length = grad.shape[0] // 2
    return pl.pallas_call(
        functools.partial(partial_kernel, first, count),
        in_specs=whole(2 + len(weights)),
        out_specs=whole(2),
        out_shape=[
            jax.ShapeDtypeStruct((length, count * HD), jnp.float32),
            jax.ShapeDtypeStruct((length, count * HD), jnp.bfloat16),
        ],
        compiler_params=pltpu.CompilerParams(vmem_limit_bytes=VMEM_LIMIT),
        cost_estimate=SMALL_COST,
        name="partial_heads",
    )(grad, grad_core, *weights)


def columns_kernel(start, stop, wide_ref, *refs):
    (outs_ref, outs_x_ref), arrived, out_ref = refs[:2], refs[2:-1], refs[-1]
    rows = outs_ref.shape[0]
    width = 2 * HD if rows % (2 * HD) == 0 else HD
    for first in range(0, rows, width):
        columns = slice(first, first + width)
        outs = jnp.concatenate([outs_ref[columns], outs_x_ref[columns]], axis=1)
        total = dot(wide_ref[start:stop], outs, 1, 1)
        for arrived_ref in arrived:
            total = total + arrived_ref[start:stop, columns].astype(jnp.float32)
        out_ref[:, columns] = total.astype(out_ref.dtype)


def columns_sum(wide, outs, outs_x, arrived, start, stop, kind):
    rows = outs.shape[0]
    if start % 16 or stop % 16:
        total = dot(wide[start:stop], jnp.concatenate([outs, outs_x], axis=1), 1, 1)
        for piece in arrived:
            total = total + piece[start:stop].astype(jnp.float32)
        return total.astype(kind)
    return pl.pallas_call(
        functools.partial(columns_kernel, start, stop),
        in_specs=whole(3 + len(arrived)),
        out_specs=whole(1)[0],
        out_shape=jax.ShapeDtypeStruct((stop - start, rows), kind),
        compiler_params=pltpu.CompilerParams(vmem_limit_bytes=VMEM_LIMIT),
        cost_estimate=SMALL_COST,
        name="columns_sum",
    )(wide, outs, outs_x, *arrived)


def assemble_kernel(local_heads, firsts, pos_ref, *refs):
    part_refs, (query_ref, key_ref, sems) = refs[:-3], refs[-3:]
    sections = len(part_refs) // len(firsts)
    copies = []
    for index, part_ref in enumerate(part_refs):
        distance, part = index % sections, index // sections
        start = pl.multiple_of(((pos_ref[0] ^ distance) * local_heads + firsts[part]) * HD, HD)
        columns = pl.ds(start, part_ref.shape[2])
        for slot, out_ref in enumerate((query_ref, key_ref)):
            copies.append(
                pltpu.make_async_copy(
                    part_ref.at[slot], out_ref.at[:, columns], sems.at[len(copies)]
                )
            )
    for copy in copies:
        copy.start()
    for copy in copies:
        copy.wait()


def assemble(pos, parts, local_heads, firsts):
    tokens = parts[0].shape[1]
    return pl.pallas_call(
        functools.partial(assemble_kernel, local_heads, firsts),
        in_specs=whole(1, pltpu.SMEM) + whole(len(parts)),
        out_specs=whole(2, pltpu.HBM),
        out_shape=[jax.ShapeDtypeStruct((tokens, HEADS * HD), jnp.bfloat16)] * 2,
        scratch_shapes=[pltpu.SemaphoreType.DMA((2 * len(parts),))],
        compiler_params=pltpu.CompilerParams(vmem_limit_bytes=VMEM_LIMIT),
        cost_estimate=SMALL_COST,
        name="assemble",
    )(pos, *parts)


def add_kernel(*refs):
    out_ref = refs[-1]
    column = 0
    for base_ref, last_ref in zip(refs[:-1:2], refs[1:-1:2]):
        width = base_ref.shape[1]
        out_ref[:, column : column + width] = base_ref[...] + last_ref[...].astype(jnp.float32)
        column += width


def add_parts(pairs):
    rows = pairs[0][0].shape[0]
    width = sum(base.shape[1] for base, _ in pairs)
    return pl.pallas_call(
        add_kernel,
        in_specs=whole(2 * len(pairs)),
        out_specs=whole(1)[0],
        out_shape=jax.ShapeDtypeStruct((rows, width), jnp.float32),
        compiler_params=pltpu.CompilerParams(vmem_limit_bytes=VMEM_LIMIT),
        cost_estimate=SMALL_COST,
        name="add_parts",
    )(*[each for pair in pairs for each in pair])


def bit_reversed(count):
    order = [0]
    while len(order) < count:
        order = [2 * value for value in order] + [2 * value + 1 for value in order]
    return order


def swap_with(array_in, axis_name, distance):
    size = lax.axis_size(axis_name)
    return lax.ppermute(array_in, axis_name, [(i, i ^ distance) for i in range(size)])


def after(array_in, *earlier):
    return lax.optimization_barrier((array_in,) + earlier)[0]


def mask_bits(key_blocks, key_count):
    slots = jnp.arange(key_blocks.shape[2])
    live = slots[None, None, :] < key_count[:, :, None]
    return jnp.sum(jnp.where(live, 1 << key_blocks, 0), axis=2, dtype=jnp.int32)


def split_parts(local_heads):
    if local_heads % 6:
        return (local_heads,)
    return PARTS


def per_device(queries, key_states, value_states, grad_out, out_weight, key_blocks, key_count):
    seq_size = lax.axis_size("seq")
    dp_size = lax.axis_size("dp")
    layers = dp_size // GROUP
    place = lax.axis_index("seq")
    row = lax.axis_index("dp")
    tokens = queries.shape[0]
    local_heads = HEADS // seq_size
    cols = out_weight.shape[1]
    own = (queries, key_states, value_states)
    pos = place.astype(jnp.int32).reshape(1)
    counts = split_parts(local_heads)
    firsts = [sum(counts[:part]) for part in range(len(counts))]
    layer_order = bit_reversed(layers)
    class_cols = layers * cols

    mask = mask_bits(key_blocks, key_count)
    others = range(1, seq_size)
    collected = collect_columns(
        pos, own, local_heads, [(k, firsts[0], counts[0]) for k in others]
    )
    received = [[swap_with(collected[k - 1], "seq", k) for k in others]]

    turned, turned_far = turn_columns(row, after(grad_out, *collected), dp_size)
    grad_x = swap_with(turned_far, "dp", 2)

    shards = {0: after(out_weight, turned).T}
    bit = layers // 2
    while bit:
        for known in sorted(shards):
            shards[known ^ bit] = swap_with(shards[known], "dp", bit * GROUP)
        bit //= 2
    near = [shards[layer] for layer in shards if layer and not layer & (layer - 1)]
    shards = [shards[layer] for layer in layer_order]
    weights = shards + [swap_with(shard, "dp", 1) for shard in shards]
    if cols % 16:
        weights = [jnp.concatenate(weights, axis=0)]

    rest = [(0, firsts[part], counts[part]) for part in range(len(counts))]
    rest += [(k, firsts[part], counts[part]) for part in range(1, len(counts)) for k in others]
    rest = pick_columns(after(pos, turned, mask), own, local_heads, rest)
    own_heads, rest = rest[: len(counts)], rest[len(counts) :]
    for part in range(1, len(counts)):
        sent = rest[(part - 1) * len(others) : part * len(others)]
        received.append([swap_with(after(sent[k - 1], grad_x, *received[part - 1]), "seq", k) for k in others])

    def gather_tokens(dc, *earlier):
        held = after(jnp.stack([turned[dc], grad_x[dc]]), *earlier)
        return [held] + [swap_with(held, "seq", k) for k in others]

    core_pieces = gather_tokens(1, *received[0])
    pieces = gather_tokens(0, *received[-1])

    outs_all, probs_all, outs_x = [], [], []
    for part, count in enumerate(counts):
        outs, probs = attend_forward(
            pos,
            mask,
            [own_heads[part]] + list(received[part]),
            firsts[part],
            count,
            local_heads,
        )
        outs_all.append(outs)
        probs_all.append(probs)
        outs_x.append(swap_with(after(outs, *near) if part else outs, "dp", 2))

    core_wide, core_turned = join_pieces(
        [core_pieces[0]] + [after(piece, outs_all[-1]) for piece in core_pieces[1:]]
    )
    arrived = []
    for part in range(len(counts)):
        if part:
            outs_x[part] = after(outs_x[part], *pieces[1:], *shards)
        sent = columns_sum(
            core_wide, outs_all[part], outs_x[part], [], 0, class_cols, jnp.bfloat16
        )
        arrived.append([swap_with(sent, "dp", 1)])

    grad_wide, grad_turned = join_pieces(
        [pieces[0]] + [after(piece, *[each[0] for each in arrived]) for piece in pieces[1:]]
    )

    def columns_of(part, start, stop, kind):
        return columns_sum(
            grad_wide, outs_all[part], outs_x[part], arrived[part], start, stop, kind
        )

    kept, got, steps = [], [], []
    for part, count in enumerate(counts):
        steps.append([columns_of(part, class_cols // 2, class_cols, jnp.bfloat16)])
        arrived[part].append(swap_with(steps[part][0], "dp", GROUP))
        total, sent = partial_heads(
            weights, after(grad_turned, steps[part][0]), core_turned, firsts[part], count
        )
        kept.append(total)
        got.append(swap_with(sent, "dp", 2))

    weight_parts = []
    for part in range(len(counts)):
        size, bit = class_cols // 2, 1
        while 2 * bit < layers:
            size //= 2
            bit *= 2
            steps[part].append(columns_of(part, size, 2 * size, jnp.bfloat16))
            arrived[part].append(swap_with(steps[part][-1], "dp", bit * GROUP))
        last = arrived[part].pop()
        weight_parts.append((columns_of(part, 0, size, jnp.float32), last))

    back_parts = []
    for part, count in enumerate(counts):
        earlier = [steps[part][-1], steps[-1][0]]
        if part:
            earlier.append(weight_parts[part - 1][1])
        backs = attend_backward(
            [own_heads[part]] + list(received[part]),
            probs_all[part],
            after(kept[part], *earlier),
            got[part],
            count,
        )
        back_parts.append(backs[0])
        back_parts += [swap_with(backs[k], "seq", k) for k in others]
    back_parts[-1] = after(back_parts[-1], steps[-1][-1])
    grad_queries, grad_keys = assemble(pos, back_parts, local_heads, firsts)
    return (grad_queries, grad_keys, add_parts(weight_parts).T)


def solution(mesh):
    return jax.shard_map(
        per_device,
        mesh=mesh,
        in_specs=(
            P(("dp", "seq"), None),
            P(("dp", "seq"), None),
            P(("dp", "seq"), None),
            P(("dp", "seq"), None),
            P("seq", "dp"),
            P(),
            P(),
        ),
        out_specs=(P(("dp", "seq"), None), P(("dp", "seq"), None), P("seq", "dp")),
        check_vma=False,
    )
```

time: 319 us -> 113 us (0.35)
  local copies, waits for them, and re-layouts: 135 us -> 4.49 us
  matrix products: 60.9 us -> 0 us
  waiting for transfers between devices: 79.7 us -> 53.6 us
  Pallas kernels: 0 us -> 25.4 us
  between operations: 14 us -> 0.9 us
  starting transfers between devices: 18.5 us -> 27.7 us
  other arithmetic: 4.67 us -> 0.09 us
    ppermute x0 -> x24, waiting for transfers between devices: none -> 53.6 us  [swap_with(): lax.ppermute(array_in, axis_name, [(i, i ^ distance) for i in range(size)])]
    dot_general x134 -> x0, matrix products: 48.7 us -> none  [the longest x1 9.35 us: reduce_grads(): jnp.einsum('hld,lc->hdc', head_outputs, whole_grad, preferred_element_typ...]
    all_to_all x5 -> x0, waiting for transfers between devices: 45.3 us -> none  [the longest x1 15 us: per_device(): lax.all_to_all(queries, 'seq', split_axis=1, concat_axis=0, tiled=True)]
    reduce_scatter x1 -> x0, waiting for transfers between devices: 33 us -> none  [reduce_grads(): return lax.psum_scatter(local_sum, 'dp', scatter_dimension=1, tiled=True)]
    gather x48 -> x0, local copies, waits for them, and re-layouts: 27.7 us -> none  [the longest x24 13.9 us: arrange(): mid_keys = key_blocks_here[chosen].reshape(middle, slot_count * BLK, HD)]
    ppermute x0 -> x24, starting transfers between devices: none -> 27.7 us  [swap_with(): lax.ppermute(array_in, axis_name, [(i, i ^ distance) for i in range(size)])]
    pallas_call x0 -> x21, Pallas kernels: none -> 25.4 us  [the longest x2 6.09 us: attend_forward(): pl.pallas_call(functools.partial(forward_kernel, first, count, local_head...]
    all_to_all x7 -> x0, local copies, waits for them, and re-layouts: 22.1 us -> none  [the longest x1 6.67 us: per_device(): lax.all_to_all(value_states, 'seq', split_axis=1, concat_axis=0, tiled=True)]
  transfers between devices with their start and end apart: 8 -> 24, of which waited for: 5 -> 12; matrix products, arithmetic and copies ran while one was open for 63% -> 1% of each run, Pallas kernels for 0% -> 20%
where the time goes in v2:
time: 113 us; the launch traced here: 112 us
  waiting for transfers between devices  53.6 us (47%)
  starting transfers between devices  27.7 us (25%)
  Pallas kernels  25.4 us (22%)
  local copies, waits for them, and re-layouts  4.49 us (4%)
    ppermute x24, waiting for transfers between devices, swap_with(): lax.ppermute(array_in, axis_name, [(i, i ^ distance) for i in range(size)])  53.6 us
    ppermute x24, starting transfers between devices, swap_with(): lax.ppermute(array_in, axis_name, [(i, i ^ distance) for i in range(size)])  27.7 us
    pallas_call x2, Pallas kernels, attend_forward(): pl.pallas_call(functools.partial(forward_kernel, first, count, local_head...  6.09 us
    pallas_call x2, Pallas kernels, partial_heads(): pl.pallas_call(functools.partial(partial_kernel, first, count), in_specs=...  4.72 us
    pallas_call x8, Pallas kernels, columns_sum(): pl.pallas_call(functools.partial(columns_kernel, start, stop), in_specs=w...  3.95 us
    pallas_call x2, Pallas kernels, attend_backward(): pl.pallas_call(functools.partial(backward_kernel, count, len(pieces)), in...  3.85 us
    unnamed x14, local copies, waits for them, and re-layouts  3.37 us
  transfers between devices with their start and end apart: 24, of which 12 were waited for; matrix products, arithmetic and copies ran while one was open for 1% of the time, Pallas kernels for 20%

profile of v2, /device:TPU:0, one launch (start us, length us, event | category | flops | bytes accessed | tf_op | source)
XLA Modules:
  0.0 112.2 jit_solution(17316662630774795813)
XLA Ops:
  0.7 2.0 %collect_columns.1 = bf16[3,128,768]{2,1,0:T(8,128)(2,1)} custom-call(s32[1]{0:T(128)} %bitcast.pos_ref, bf16[128,3072]{1,0:T(8,128)(2,1)} %refs_0_.3, bf16[128,3072]{1,0:T(8,128)(2,1)} %refs_1_.3, bf16[128,3072]{1,0:T(8,128)(2,1)} %refs_2_.3), custom_call_target="tpu_custom_call" | custom-call | tf_op jit(solution)/shard_map/collect_columns/pallas_call | solution.py:213
  2.7 3.0 %collective-permute-start = (bf16[3,128,768]{2,1,0:T(8,128)(2,1)}, bf16[3,128,768]{2,1,0:T(8,128)(2,1)S(1)}, u32[]{:S(2)}, u32[]{:S(2)}) collective-permute-start(bf16[3,128,768]{2,1,0:T(8,128)(2,1)} %collect_columns.1), channel_id=1, source_target_pairs={{0,1},{1,0},{2,3},{3,2},{4,5},{5,4},{6,7},{7,6},{8,9},{9,8},{10,11... | collective-permute-start | bytes 1769480 | tf_op jit(solution)/shard_map/ppermute | solution.py:414
  5.7 1.1 copy-done.4
  7.9 1.6 %collective-permute-start.1 = (bf16[2,640,128]{2,1,0:T(8,128)(2,1)S(1)}, bf16[2,640,128]{2,1,0:T(8,128)(2,1)}, u32[]{:S(2)}, u32[]{:S(2)}) collective-permute-start(bf16[2,640,128]{2,1,0:T(8,128)(2,1)S(1)} %get-tuple-element.46), channel_id=1, source_target_pairs={{0,4},{2,6},{4,0},{6,2},{8,12},{10,14},{12,8},{14,10},{16,20},{18,... | collective-permute-start | bytes 983048 | tf_op jit(solution)/shard_map/ppermute | solution.py:414
  9.5 2.6 %collective-permute-start.7 = (bf16[160,1536]{1,0:T(8,128)(2,1)}, bf16[160,1536]{1,0:T(8,128)(2,1)}, u32[]{:S(2)}, u32[]{:S(2)}) collective-permute-start(bf16[160,1536]{1,0:T(8,128)(2,1)} %bitcast.4), channel_id=1, source_target_pairs={{0,16},{2,18},{4,20},{6,22},{8,24},{10,26},{12,28},{14,30},{16,0},... | collective-permute-start | bytes 1474568 | tf_op jit(solution)/shard_map/ppermute | solution.py:414
  12.1 1.6 %collective-permute-start.8 = (bf16[160,1536]{1,0:T(8,128)(2,1)}, bf16[160,1536]{1,0:T(8,128)(2,1)}, u32[]{:S(2)}, u32[]{:S(2)}) collective-permute-start(bf16[160,1536]{1,0:T(8,128)(2,1)} %bitcast.5), channel_id=1, source_target_pairs={{0,8},{2,10},{4,12},{6,14},{8,0},{10,2},{12,4},{14,6},{16,24},{18,... | collective-permute-start | bytes 1474568 | tf_op jit(solution)/shard_map/ppermute | solution.py:414
  13.7 1.1 %copy-done.1 = bf16[128,3072]{1,0:T(8,128)(2,1)S(1)} copy-done((bf16[128,3072]{1,0:T(8,128)(2,1)S(1)}, bf16[128,3072]{1,0:T(8,128)(2,1)}, u32[]{:S(2)}) %copy-start.1) | copy-done | bytes 786456
  14.8 1.1 %copy-done.2 = bf16[128,3072]{1,0:T(8,128)(2,1)S(1)} copy-done((bf16[128,3072]{1,0:T(8,128)(2,1)S(1)}, bf16[128,3072]{1,0:T(8,128)(2,1)}, u32[]{:S(2)}) %copy-start.2) | copy-done | bytes 786456
  17.2 2.0 %collective-permute-done.refs_1_ = bf16[3,128,768]{2,1,0:T(8,128)(2,1)S(1)} collective-permute-done((bf16[3,128,768]{2,1,0:T(8,128)(2,1)}, bf16[3,128,768]{2,1,0:T(8,128)(2,1)S(1)}, u32[]{:S(2)}, u32[]{:S(2)}) %collective-permute-start) | collective-permute-done | bytes 589856 | tf_op jit(solution)/shard_map/ppermute | solution.py:414
  19.3 1.7 %collective-permute-start.2 = (bf16[3,128,768]{2,1,0:T(8,128)(2,1)}, bf16[3,128,768]{2,1,0:T(8,128)(2,1)S(1)}, u32[]{:S(2)}, u32[]{:S(2)}) collective-permute-start(bf16[3,128,768]{2,1,0:T(8,128)(2,1)} %get-tuple-element.48), channel_id=1, source_target_pairs={{0,1},{1,0},{2,3},{3,2},{4,5},{5,4},{6,7},{7,6},{8,9},{9,8},{10,11... | collective-permute-start | bytes 1769480 | tf_op jit(solution)/shard_map/ppermute | solution.py:414
  22.2 11.6 %collective-permute-done.7.refs_1_ = bf16[160,1536]{1,0:T(8,128)(2,1)} collective-permute-done((bf16[160,1536]{1,0:T(8,128)(2,1)}, bf16[160,1536]{1,0:T(8,128)(2,1)}, u32[]{:S(2)}, u32[]{:S(2)}) %collective-permute-start.7) | collective-permute-done | bytes 491552 | tf_op jit(solution)/shard_map/ppermute | solution.py:414
  34.3 3.0 %attend_forward.2 = (bf16[768,256]{1,0:T(8,128)(2,1)S(1)}, f32[6,256,256]{2,1,0:T(8,128)S(1)}) custom-call(s32[1]{0:T(128)} %bitcast.pos_ref, s32[24,4]{1,0:T(8,128)S(1)} %copy.10.mask_ref, bf16[3,128,768]{2,1,0:T(8,128)(2,1)S(1)} %get-tuple-element.44.refs_0_, bf16[3,128,768]{2,1,0:T(8,128)(2,1)S(1)} %collective-permute-done.refs_1_), custom_call_target="tpu_custom_call" | custom-call | tf_op jit(solution)/shard_map/attend_forward/pallas_call | solution.py:140
  38.5 3.0 %attend_forward.3 = (bf16[768,256]{1,0:T(8,128)(2,1)S(1)}, f32[6,256,256]{2,1,0:T(8,128)S(1)}) custom-call(s32[1]{0:T(128)} %bitcast.pos_ref, s32[24,4]{1,0:T(8,128)S(1)} %copy.10.mask_ref, bf16[3,128,768]{2,1,0:T(8,128)(2,1)S(1)} %get-tuple-element.51.refs_0_, bf16[3,128,768]{2,1,0:T(8,128)(2,1)S(1)} %collective-permute-done.2.refs_1_), custom_call_target="tpu_custom_call" | custom-call | tf_op jit(solution)/shard_map/attend_forward/pallas_call | solution.py:140
  41.6 1.6 %collective-permute-start.9 = (bf16[768,256]{1,0:T(8,128)(2,1)S(1)}, bf16[768,256]{1,0:T(8,128)(2,1)S(1)}, u32[]{:S(2)}, u32[]{:S(2)}) collective-permute-start(bf16[768,256]{1,0:T(8,128)(2,1)S(1)} %get-tuple-element.57.refs_0_), channel_id=1, source_target_pairs={{0,4},{2,6},{4,0},{6,2},{8,12},{10,14},{12,8},{14,10},{16,20},{18,... | collective-permute-start | bytes 1179656 | tf_op jit(solution)/shard_map/ppermute | solution.py:414
  43.2 1.6 %collective-permute-start.3 = (bf16[2,640,128]{2,1,0:T(8,128)(2,1)S(1)}, bf16[2,640,128]{2,1,0:T(8,128)(2,1)S(1)}, u32[]{:S(2)}, u32[]{:S(2)}) collective-permute-start(bf16[2,640,128]{2,1,0:T(8,128)(2,1)S(1)} %pad_maximum_fusion.refs_0_), channel_id=1, source_target_pairs={{0,1},{1,0},{2,3},{3,2},{4,5},{5,4},{6,7},{7,6},{8,9},{9,8},{10,11... | collective-permute-start | bytes 983048 | tf_op jit(solution)/shard_map/ppermute | solution.py:414
  44.8 3.9 %collective-permute-done.4.refs_1_ = bf16[2,640,128]{2,1,0:T(8,128)(2,1)S(1)} collective-permute-done((bf16[2,640,128]{2,1,0:T(8,128)(2,1)S(1)}, bf16[2,640,128]{2,1,0:T(8,128)(2,1)S(1)}, u32[]{:S(2)}, u32[]{:S(2)}) %collective-permute-start.4) | collective-permute-done | bytes 327712 | tf_op jit(solution)/shard_map/ppermute | solution.py:414
  50.2 3.9 %collective-permute-done.3.refs_1_ = bf16[2,640,128]{2,1,0:T(8,128)(2,1)S(1)} collective-permute-done((bf16[2,640,128]{2,1,0:T(8,128)(2,1)S(1)}, bf16[2,640,128]{2,1,0:T(8,128)(2,1)S(1)}, u32[]{:S(2)}, u32[]{:S(2)}) %collective-permute-start.3) | collective-permute-done | bytes 327712 | tf_op jit(solution)/shard_map/ppermute | solution.py:414
  54.1 2.5 %collective-permute-done.9.refs_1_ = bf16[768,256]{1,0:T(8,128)(2,1)S(1)} collective-permute-done((bf16[768,256]{1,0:T(8,128)(2,1)S(1)}, bf16[768,256]{1,0:T(8,128)(2,1)S(1)}, u32[]{:S(2)}, u32[]{:S(2)}) %collective-permute-start.9) | collective-permute-done | bytes 393248 | tf_op jit(solution)/shard_map/ppermute | solution.py:414
  58.5 1.5 %collective-permute-done.11.refs_2_ = bf16[640,768]{1,0:T(8,128)(2,1)S(1)} collective-permute-done((bf16[640,768]{1,0:T(8,128)(2,1)S(1)}, bf16[640,768]{1,0:T(8,128)(2,1)S(1)}, u32[]{:S(2)}, u32[]{:S(2)}) %collective-permute-start.11) | collective-permute-done | bytes 983072 | tf_op jit(solution)/shard_map/ppermute | solution.py:414
  61.5 1.8 %collective-permute-start.19 = (bf16[320,768]{1,0:T(8,128)(2,1)S(1)}, bf16[320,768]{1,0:T(8,128)(2,1)S(1)}, u32[]{:S(2)}, u32[]{:S(2)}) collective-permute-start(bf16[320,768]{1,0:T(8,128)(2,1)S(1)} %columns_sum.12), channel_id=1, source_target_pairs={{0,8},{2,10},{4,12},{6,14},{8,0},{10,2},{12,4},{14,6},{16,24},{18,... | collective-permute-start | bytes 1474568 | tf_op jit(solution)/shard_map/ppermute | solution.py:414
  63.3 2.4 %partial_heads.3 = (f32[256,768]{1,0:T(8,128)S(1)}, bf16[256,768]{1,0:T(8,128)(2,1)S(1)}) custom-call(bf16[512,640]{1,0:T(8,128)(2,1)S(1)} %get-tuple-element.70.grad_ref, bf16[512,640]{1,0:T(8,128)(2,1)S(1)} %get-tuple-element.63.grad_core_ref, bf16[160,1536]{1,0:T(8,128)(2,1)S(1)} %bitcast.7, bf16[160,1536]{1,0:T(8,128)(2,1)} %collective-permute-done.7.refs_1_, ...), custom_call_target="tpu_custom_call" | custom-call | tf_op jit(solution)/shard_map/partial_heads/pallas_call | solution.py:303
  66.3 2.4 %partial_heads.2 = (f32[256,768]{1,0:T(8,128)S(1)}, bf16[256,768]{1,0:T(8,128)(2,1)S(1)}) custom-call(bf16[512,640]{1,0:T(8,128)(2,1)S(1)} %get-tuple-element.70.grad_ref, bf16[512,640]{1,0:T(8,128)(2,1)S(1)} %get-tuple-element.63.grad_core_ref, bf16[160,1536]{1,0:T(8,128)(2,1)S(1)} %bitcast.8, bf16[160,1536]{1,0:T(8,128)(2,1)} %collective-permute-done.7.refs_1_, ...), custom_call_target="tpu_custom_call" | custom-call | tf_op jit(solution)/shard_map/partial_heads/pallas_call | solution.py:303
  68.6 1.6 %collective-permute-start.17 = (bf16[256,768]{1,0:T(8,128)(2,1)S(1)}, bf16[256,768]{1,0:T(8,128)(2,1)S(1)}, u32[]{:S(2)}, u32[]{:S(2)}) collective-permute-start(bf16[256,768]{1,0:T(8,128)(2,1)S(1)} %get-tuple-element.66), channel_id=1, source_target_pairs={{0,4},{2,6},{4,0},{6,2},{8,12},{10,14},{12,8},{14,10},{16,20},{18,... | collective-permute-start | bytes 1179656 | tf_op jit(solution)/shard_map/ppermute | solution.py:414
  70.2 4.6 %collective-permute-done.16.refs_3_ = bf16[320,768]{1,0:T(8,128)(2,1)S(1)} collective-permute-done((bf16[320,768]{1,0:T(8,128)(2,1)S(1)}, bf16[320,768]{1,0:T(8,128)(2,1)S(1)}, u32[]{:S(2)}, u32[]{:S(2)}) %collective-permute-start.16) | collective-permute-done | bytes 491552 | tf_op jit(solution)/shard_map/ppermute | solution.py:414
  75.2 3.4 %collective-permute-start.20 = (bf16[160,768]{1,0:T(8,128)(2,1)S(1)}, bf16[160,768]{1,0:T(8,128)(2,1)S(1)}, u32[]{:S(2)}, u32[]{:S(2)}) collective-permute-start(bf16[160,768]{1,0:T(8,128)(2,1)S(1)} %columns_sum.11), channel_id=1, source_target_pairs={{0,16},{2,18},{4,20},{6,22},{8,24},{10,26},{12,28},{14,30},{16,0},... | collective-permute-start | bytes 737288 | tf_op jit(solution)/shard_map/ppermute | solution.py:414
  78.7 11.1 %collective-permute-done.19.refs_3_ = bf16[320,768]{1,0:T(8,128)(2,1)S(1)} collective-permute-done((bf16[320,768]{1,0:T(8,128)(2,1)S(1)}, bf16[320,768]{1,0:T(8,128)(2,1)S(1)}, u32[]{:S(2)}, u32[]{:S(2)}) %collective-permute-start.19) | collective-permute-done | bytes 491552 | tf_op jit(solution)/shard_map/ppermute | solution.py:414
  90.2 1.9 %attend_backward.3 = (bf16[2,128,768]{2,1,0:T(8,128)(2,1)S(1)}, bf16[2,128,768]{2,1,0:T(8,128)(2,1)S(1)}) custom-call(bf16[3,128,768]{2,1,0:T(8,128)(2,1)S(1)} %get-tuple-element.51.refs_0_, bf16[3,128,768]{2,1,0:T(8,128)(2,1)S(1)} %collective-permute-done.2.refs_1_, f32[6,256,256]{2,1,0:T(8,128)S(1)} %get-tuple-element.69.refs_2_, ...), custom_call_target="tpu_custom_call" | custom-call | tf_op jit(solution)/shard_map/attend_backward/pallas_call | solution.py:156
  92.7 1.9 %attend_backward.2 = (bf16[2,128,768]{2,1,0:T(8,128)(2,1)S(1)}, bf16[2,128,768]{2,1,0:T(8,128)(2,1)S(1)}) custom-call(bf16[3,128,768]{2,1,0:T(8,128)(2,1)S(1)} %get-tuple-element.44.refs_0_, bf16[3,128,768]{2,1,0:T(8,128)(2,1)S(1)} %collective-permute-done.refs_1_, f32[6,256,256]{2,1,0:T(8,128)S(1)} %get-tuple-element.45.refs_2_, ...), custom_call_target="tpu_custom_call" | custom-call | tf_op jit(solution)/shard_map/attend_backward/pallas_call | solution.py:156
  94.7 1.6 %collective-permute-start.18 = (bf16[2,128,768]{2,1,0:T(8,128)(2,1)S(1)}, bf16[2,128,768]{2,1,0:T(8,128)(2,1)S(1)}, u32[]{:S(2)}, u32[]{:S(2)}) collective-permute-start(bf16[2,128,768]{2,1,0:T(8,128)(2,1)S(1)} %get-tuple-element.68), channel_id=1, source_target_pairs={{0,1},{1,0},{2,3},{3,2},{4,5},{5,4},{6,7},{7,6},{8,9},{9,8},{10,11... | collective-permute-start | bytes 1179656 | tf_op jit(solution)/shard_map/ppermute | solution.py:414
  96.3 1.2 %collective-permute-start.23 = (bf16[160,768]{1,0:T(8,128)(2,1)S(1)}, bf16[160,768]{1,0:T(8,128)(2,1)S(1)}, u32[]{:S(2)}, u32[]{:S(2)}) collective-permute-start(bf16[160,768]{1,0:T(8,128)(2,1)S(1)} %columns_sum.13), channel_id=1, source_target_pairs={{0,16},{2,18},{4,20},{6,22},{8,24},{10,26},{12,28},{14,30},{16,0},... | collective-permute-start | bytes 737288 | tf_op jit(solution)/shard_map/ppermute | solution.py:414
  98.3 10.8 %collective-permute-done.23.refs_3_ = bf16[160,768]{1,0:T(8,128)(2,1)S(1)} collective-permute-done((bf16[160,768]{1,0:T(8,128)(2,1)S(1)}, bf16[160,768]{1,0:T(8,128)(2,1)S(1)}, u32[]{:S(2)}, u32[]{:S(2)}) %collective-permute-start.23) | collective-permute-done | bytes 245792 | tf_op jit(solution)/shard_map/ppermute | solution.py:414
  111.0 1.2 %assemble.1 = (bf16[128,3072]{1,0:T(8,128)(2,1)}, bf16[128,3072]{1,0:T(8,128)(2,1)}) custom-call(s32[1]{0:T(128)} %bitcast.pos_ref, bf16[2,128,768]{2,1,0:T(8,128)(2,1)S(1)} %get-tuple-element.67.refs_0_, bf16[2,128,768]{2,1,0:T(8,128)(2,1)S(1)} %collective-permute-done.18.refs_1_, bf16[2,128,768]{2,1,0:T(8,128)(2,1)S(1)} %get-tuple-element.74.refs_2_, ...), custom_call_target="tpu_custom_call" | custom-call | tf_op jit(solution)/shard_map/assemble/pallas_call | solution.py:370
  (57 shorter events, 15.1 us)
Async XLA Ops:
  0.6 13.0 %copy-start.5 = (s32[24,4,4]{0,2,1:T(4,128)S(1)}, s32[24,4,4]{0,2,1:T(4,128)}, u32[]{:S(2)}) copy-start(s32[24,4,4]{0,2,1:T(4,128)} %param.12) | copy-start | bytes 4612
  0.6 13.0 %copy-start.6 = (s32[24,4]{0,1:T(4,128)S(1)}, s32[24,4]{0,1:T(4,128)}, u32[]{:S(2)}) copy-start(s32[24,4]{0,1:T(4,128)} %param.13) | copy-start | bytes 1156
  0.7 13.0 %copy-start = (bf16[128,3072]{1,0:T(8,128)(2,1)S(1)}, bf16[128,3072]{1,0:T(8,128)(2,1)}, u32[]{:S(2)}) copy-start(bf16[128,3072]{1,0:T(8,128)(2,1)} %refs_0_.3) | copy-start | bytes 2359300
  2.7 16.6 %collective-permute-start = (bf16[3,128,768]{2,1,0:T(8,128)(2,1)}, bf16[3,128,768]{2,1,0:T(8,128)(2,1)S(1)}, u32[]{:S(2)}, u32[]{:S(2)}) collective-permute-start(bf16[3,128,768]{2,1,0:T(8,128)(2,1)} %collect_columns.1), channel_id=1, source_target_pairs={{0,1},{1,0},{2,3},{3,2},{4,5},{5,4},{6,7},{7,6},{8,9},{9,8},{10,11... | collective-permute-start | bytes 1769480 | tf_op jit(solution)/shard_map/ppermute | solution.py:414
  5.7 1.1 copy-start.4
  7.9 9.3 %collective-permute-start.1 = (bf16[2,640,128]{2,1,0:T(8,128)(2,1)S(1)}, bf16[2,640,128]{2,1,0:T(8,128)(2,1)}, u32[]{:S(2)}, u32[]{:S(2)}) collective-permute-start(bf16[2,640,128]{2,1,0:T(8,128)(2,1)S(1)} %get-tuple-element.46), channel_id=1, source_target_pairs={{0,4},{2,6},{4,0},{6,2},{8,12},{10,14},{12,8},{14,10},{16,20},{18,... | collective-permute-start | bytes 983048 | tf_op jit(solution)/shard_map/ppermute | solution.py:414
  9.5 24.3 %collective-permute-start.7 = (bf16[160,1536]{1,0:T(8,128)(2,1)}, bf16[160,1536]{1,0:T(8,128)(2,1)}, u32[]{:S(2)}, u32[]{:S(2)}) collective-permute-start(bf16[160,1536]{1,0:T(8,128)(2,1)} %bitcast.4), channel_id=1, source_target_pairs={{0,16},{2,18},{4,20},{6,22},{8,24},{10,26},{12,28},{14,30},{16,0},... | collective-permute-start | bytes 1474568 | tf_op jit(solution)/shard_map/ppermute | solution.py:414
  12.1 29.6 %collective-permute-start.8 = (bf16[160,1536]{1,0:T(8,128)(2,1)}, bf16[160,1536]{1,0:T(8,128)(2,1)}, u32[]{:S(2)}, u32[]{:S(2)}) collective-permute-start(bf16[160,1536]{1,0:T(8,128)(2,1)} %bitcast.5), channel_id=1, source_target_pairs={{0,8},{2,10},{4,12},{6,14},{8,0},{10,2},{12,4},{14,6},{16,24},{18,... | collective-permute-start | bytes 1474568 | tf_op jit(solution)/shard_map/ppermute | solution.py:414
  13.7 1.1 %copy-start.1 = (bf16[128,3072]{1,0:T(8,128)(2,1)S(1)}, bf16[128,3072]{1,0:T(8,128)(2,1)}, u32[]{:S(2)}) copy-start(bf16[128,3072]{1,0:T(8,128)(2,1)} %refs_1_.3) | copy-start | bytes 2359300
  14.8 1.1 %copy-start.2 = (bf16[128,3072]{1,0:T(8,128)(2,1)S(1)}, bf16[128,3072]{1,0:T(8,128)(2,1)}, u32[]{:S(2)}) copy-start(bf16[128,3072]{1,0:T(8,128)(2,1)} %refs_2_.3) | copy-start | bytes 2359300
  19.3 19.3 %collective-permute-start.2 = (bf16[3,128,768]{2,1,0:T(8,128)(2,1)}, bf16[3,128,768]{2,1,0:T(8,128)(2,1)S(1)}, u32[]{:S(2)}, u32[]{:S(2)}) collective-permute-start(bf16[3,128,768]{2,1,0:T(8,128)(2,1)} %get-tuple-element.48), channel_id=1, source_target_pairs={{0,1},{1,0},{2,3},{3,2},{4,5},{5,4},{6,7},{7,6},{8,9},{9,8},{10,11... | collective-permute-start | bytes 1769480 | tf_op jit(solution)/shard_map/ppermute | solution.py:414
  33.7 16.5 %collective-permute-start.10 = (bf16[160,1536]{1,0:T(8,128)(2,1)}, bf16[160,1536]{1,0:T(8,128)(2,1)S(1)}, u32[]{:S(2)}, u32[]{:S(2)}) collective-permute-start(bf16[160,1536]{1,0:T(8,128)(2,1)} %collective-permute-done.7.refs_1_), channel_id=1, source_target_pairs={{0,8},{2,10},{4,12},{6,14},{8,0},{10,2},{12,4},{14,6},{16,24},{18,... | collective-permute-start | bytes 1474568 | tf_op jit(solution)/shard_map/ppermute | solution.py:414
  37.3 12.1 %collective-permute-start.5 = (bf16[768,256]{1,0:T(8,128)(2,1)S(1)}, bf16[768,256]{1,0:T(8,128)(2,1)S(1)}, u32[]{:S(2)}, u32[]{:S(2)}) collective-permute-start(bf16[768,256]{1,0:T(8,128)(2,1)S(1)} %get-tuple-element.55.refs_0_), channel_id=1, source_target_pairs={{0,4},{2,6},{4,0},{6,2},{8,12},{10,14},{12,8},{14,10},{16,20},{18,... | collective-permute-start | bytes 1179656 | tf_op jit(solution)/shard_map/ppermute | solution.py:414
  38.0 10.7 %collective-permute-start.4 = (bf16[2,640,128]{2,1,0:T(8,128)(2,1)S(1)}, bf16[2,640,128]{2,1,0:T(8,128)(2,1)S(1)}, u32[]{:S(2)}, u32[]{:S(2)}) collective-permute-start(bf16[2,640,128]{2,1,0:T(8,128)(2,1)S(1)} %pad_maximum_fusion.1.refs_0_), channel_id=1, source_target_pairs={{0,1},{1,0},{2,3},{3,2},{4,5},{5,4},{6,7},{7,6},{8,9},{9,8},{10,11... | collective-permute-start | bytes 983048 | tf_op jit(solution)/shard_map/ppermute | solution.py:414
  41.6 15.0 %collective-permute-start.9 = (bf16[768,256]{1,0:T(8,128)(2,1)S(1)}, bf16[768,256]{1,0:T(8,128)(2,1)S(1)}, u32[]{:S(2)}, u32[]{:S(2)}) collective-permute-start(bf16[768,256]{1,0:T(8,128)(2,1)S(1)} %get-tuple-element.57.refs_0_), channel_id=1, source_target_pairs={{0,4},{2,6},{4,0},{6,2},{8,12},{10,14},{12,8},{14,10},{16,20},{18,... | collective-permute-start | bytes 1179656 | tf_op jit(solution)/shard_map/ppermute | solution.py:414
  43.2 10.9 %collective-permute-start.3 = (bf16[2,640,128]{2,1,0:T(8,128)(2,1)S(1)}, bf16[2,640,128]{2,1,0:T(8,128)(2,1)S(1)}, u32[]{:S(2)}, u32[]{:S(2)}) collective-permute-start(bf16[2,640,128]{2,1,0:T(8,128)(2,1)S(1)} %pad_maximum_fusion.refs_0_), channel_id=1, source_target_pairs={{0,1},{1,0},{2,3},{3,2},{4,5},{5,4},{6,7},{7,6},{8,9},{9,8},{10,11... | collective-permute-start | bytes 983048 | tf_op jit(solution)/shard_map/ppermute | solution.py:414
  50.1 7.2 %copy-start.3 = (bf16[1536,160]{0,1:T(8,128)(2,1)S(1)}, bf16[1536,160]{0,1:T(8,128)(2,1)}, u32[]{:S(2)}) copy-start(bf16[1536,160]{0,1:T(8,128)(2,1)} %param.11) | copy-start | bytes 1474564
  50.2 8.2 %collective-permute-start.6 = (bf16[640,768]{1,0:T(8,128)(2,1)S(1)}, bf16[640,768]{1,0:T(8,128)(2,1)S(1)}, u32[]{:S(2)}, u32[]{:S(2)}) collective-permute-start(bf16[640,768]{1,0:T(8,128)(2,1)S(1)} %columns_sum.8), channel_id=1, source_target_pairs={{0,2},{2,0},{4,6},{6,4},{8,10},{10,8},{12,14},{14,12},{16,18},{18,... | collective-permute-start | bytes 2949128 | tf_op jit(solution)/shard_map/ppermute | solution.py:414
  57.3 2.6 %collective-permute-start.11 = (bf16[640,768]{1,0:T(8,128)(2,1)S(1)}, bf16[640,768]{1,0:T(8,128)(2,1)S(1)}, u32[]{:S(2)}, u32[]{:S(2)}) collective-permute-start(bf16[640,768]{1,0:T(8,128)(2,1)S(1)} %columns_sum.9), channel_id=1, source_target_pairs={{0,2},{2,0},{4,6},{6,4},{8,10},{10,8},{12,14},{14,12},{16,18},{18,... | collective-permute-start | bytes 2949128 | tf_op jit(solution)/shard_map/ppermute | solution.py:414
  57.4 4.1 %collective-permute-start.12 = (bf16[160,1536]{1,0:T(8,128)(2,1)S(1)}, bf16[160,1536]{1,0:T(8,128)(2,1)S(1)}, u32[]{:S(2)}, u32[]{:S(2)}) collective-permute-start(bf16[160,1536]{1,0:T(8,128)(2,1)S(1)} %bitcast.6), channel_id=1, source_target_pairs={{0,2},{2,0},{4,6},{6,4},{8,10},{10,8},{12,14},{14,12},{16,18},{18,... | collective-permute-start | bytes 1474568 | tf_op jit(solution)/shard_map/ppermute | solution.py:414
  57.9 5.4 %collective-permute-start.13 = (bf16[160,1536]{1,0:T(8,128)(2,1)}, bf16[160,1536]{1,0:T(8,128)(2,1)S(1)}, u32[]{:S(2)}, u32[]{:S(2)}) collective-permute-start(bf16[160,1536]{1,0:T(8,128)(2,1)} %collective-permute-done.7.refs_1_), channel_id=1, source_target_pairs={{0,2},{2,0},{4,6},{6,4},{8,10},{10,8},{12,14},{14,12},{16,18},{18,... | collective-permute-start | bytes 1474568 | tf_op jit(solution)/shard_map/ppermute | solution.py:414
  58.0 5.3 %collective-permute-start.14 = (bf16[160,1536]{1,0:T(8,128)(2,1)}, bf16[160,1536]{1,0:T(8,128)(2,1)S(1)}, u32[]{:S(2)}, u32[]{:S(2)}) collective-permute-start(bf16[160,1536]{1,0:T(8,128)(2,1)} %collective-permute-done.8.refs_2_), channel_id=1, source_target_pairs={{0,2},{2,0},{4,6},{6,4},{8,10},{10,8},{12,14},{14,12},{16,18},{18,... | collective-permute-start | bytes 1474568 | tf_op jit(solution)/shard_map/ppermute | solution.py:414
  58.4 4.9 %collective-permute-start.15 = (bf16[160,1536]{1,0:T(8,128)(2,1)S(1)}, bf16[160,1536]{1,0:T(8,128)(2,1)S(1)}, u32[]{:S(2)}, u32[]{:S(2)}) collective-permute-start(bf16[160,1536]{1,0:T(8,128)(2,1)S(1)} %collective-permute-done.10.refs_3_), channel_id=1, source_target_pairs={{0,2},{2,0},{4,6},{6,4},{8,10},{10,8},{12,14},{14,12},{16,18},{18,... | collective-permute-start | bytes 1474568 | tf_op jit(solution)/shard_map/ppermute | solution.py:414
  60.7 14.1 %collective-permute-start.16 = (bf16[320,768]{1,0:T(8,128)(2,1)S(1)}, bf16[320,768]{1,0:T(8,128)(2,1)S(1)}, u32[]{:S(2)}, u32[]{:S(2)}) collective-permute-start(bf16[320,768]{1,0:T(8,128)(2,1)S(1)} %columns_sum.10), channel_id=1, source_target_pairs={{0,8},{2,10},{4,12},{6,14},{8,0},{10,2},{12,4},{14,6},{16,24},{18,... | collective-permute-start | bytes 1474568 | tf_op jit(solution)/shard_map/ppermute | solution.py:414
  61.5 28.3 %collective-permute-start.19 = (bf16[320,768]{1,0:T(8,128)(2,1)S(1)}, bf16[320,768]{1,0:T(8,128)(2,1)S(1)}, u32[]{:S(2)}, u32[]{:S(2)}) collective-permute-start(bf16[320,768]{1,0:T(8,128)(2,1)S(1)} %columns_sum.12), channel_id=1, source_target_pairs={{0,8},{2,10},{4,12},{6,14},{8,0},{10,2},{12,4},{14,6},{16,24},{18,... | collective-permute-start | bytes 1474568 | tf_op jit(solution)/shard_map/ppermute | solution.py:414
  65.7 24.6 %collective-permute-start.21 = (bf16[256,768]{1,0:T(8,128)(2,1)S(1)}, bf16[256,768]{1,0:T(8,128)(2,1)S(1)}, u32[]{:S(2)}, u32[]{:S(2)}) collective-permute-start(bf16[256,768]{1,0:T(8,128)(2,1)S(1)} %get-tuple-element.73), channel_id=1, source_target_pairs={{0,4},{2,6},{4,0},{6,2},{8,12},{10,14},{12,8},{14,10},{16,20},{18,... | collective-permute-start | bytes 1179656 | tf_op jit(solution)/shard_map/ppermute | solution.py:414
  68.6 24.1 %collective-permute-start.17 = (bf16[256,768]{1,0:T(8,128)(2,1)S(1)}, bf16[256,768]{1,0:T(8,128)(2,1)S(1)}, u32[]{:S(2)}, u32[]{:S(2)}) collective-permute-start(bf16[256,768]{1,0:T(8,128)(2,1)S(1)} %get-tuple-element.66), channel_id=1, source_target_pairs={{0,4},{2,6},{4,0},{6,2},{8,12},{10,14},{12,8},{14,10},{16,20},{18,... | collective-permute-start | bytes 1179656 | tf_op jit(solution)/shard_map/ppermute | solution.py:414
  75.2 15.0 %collective-permute-start.20 = (bf16[160,768]{1,0:T(8,128)(2,1)S(1)}, bf16[160,768]{1,0:T(8,128)(2,1)S(1)}, u32[]{:S(2)}, u32[]{:S(2)}) collective-permute-start(bf16[160,768]{1,0:T(8,128)(2,1)S(1)} %columns_sum.11), channel_id=1, source_target_pairs={{0,16},{2,18},{4,20},{6,22},{8,24},{10,26},{12,28},{14,30},{16,0},... | collective-permute-start | bytes 737288 | tf_op jit(solution)/shard_map/ppermute | solution.py:414
  92.2 17.9 %collective-permute-start.22 = (bf16[2,128,768]{2,1,0:T(8,128)(2,1)S(1)}, bf16[2,128,768]{2,1,0:T(8,128)(2,1)S(1)}, u32[]{:S(2)}, u32[]{:S(2)}) collective-permute-start(bf16[2,128,768]{2,1,0:T(8,128)(2,1)S(1)} %get-tuple-element.75), channel_id=1, source_target_pairs={{0,1},{1,0},{2,3},{3,2},{4,5},{5,4},{6,7},{7,6},{8,9},{9,8},{10,11... | collective-permute-start | bytes 1179656 | tf_op jit(solution)/shard_map/ppermute | solution.py:414
  94.7 16.3 %collective-permute-start.18 = (bf16[2,128,768]{2,1,0:T(8,128)(2,1)S(1)}, bf16[2,128,768]{2,1,0:T(8,128)(2,1)S(1)}, u32[]{:S(2)}, u32[]{:S(2)}) collective-permute-start(bf16[2,128,768]{2,1,0:T(8,128)(2,1)S(1)} %get-tuple-element.68), channel_id=1, source_target_pairs={{0,1},{1,0},{2,3},{3,2},{4,5},{5,4},{6,7},{7,6},{8,9},{9,8},{10,11... | collective-permute-start | bytes 1179656 | tf_op jit(solution)/shard_map/ppermute | solution.py:414
  96.3 12.8 %collective-permute-start.23 = (bf16[160,768]{1,0:T(8,128)(2,1)S(1)}, bf16[160,768]{1,0:T(8,128)(2,1)S(1)}, u32[]{:S(2)}, u32[]{:S(2)}) collective-permute-start(bf16[160,768]{1,0:T(8,128)(2,1)S(1)} %columns_sum.13), channel_id=1, source_target_pairs={{0,16},{2,18},{4,20},{6,22},{8,24},{10,26},{12,28},{14,30},{16,0},... | collective-permute-start | bytes 737288 | tf_op jit(solution)/shard_map/ppermute | solution.py:414

commit v3 on v2

--- a/solution.py
+++ b/solution.py
@@ -59,7 +59,7 @@
 
 
 def each_head(count, body):
-    step = 4 if count % 4 == 0 else 3 if count % 3 == 0 else 2 if count % 2 == 0 else 1
+    step = count if count <= 8 else 1
 
     def run(index, carry):
         for offset in range(step):
@@ -74,6 +74,10 @@
         jnp.concatenate([piece_ref[slot, :, columns] for piece_ref in piece_refs], axis=0)
         for slot in range(3)
     ]
+
+
+def column_blocks(width):
+    return [slice(low, min(low + 2 * HD, width)) for low in range(0, width, 2 * HD)]
 
 
 def lanes(head):
@@ -284,15 +288,19 @@
     )(*pieces)
 
 
-def partial_kernel(first, count, grad_ref, grad_core_ref, *refs):
+def partial_kernel(first, grad_ref, grad_core_ref, *refs):
     weight_refs, (kept_ref, sent_ref) = refs[:-2], refs[-2:]
-    length = kept_ref.shape[0]
+    length, width = kept_ref.shape
     grad = jnp.concatenate([grad_ref[...], grad_core_ref[...]], axis=1)
-    width = 2 * HD if count % 2 == 0 else HD
-    for start in range(0, count * HD, width):
-        rows = slice(first * HD + start, first * HD + start + width)
-        weight = jnp.concatenate([weight_ref[:, rows] for weight_ref in weight_refs], axis=0)
-        columns = slice(start, start + width)
+    for columns in column_blocks(width):
+        rows = slice(first * HD + columns.start, first * HD + columns.stop)
+        weight = jnp.concatenate(
+            [
+                weight_ref[:, columns if weight_ref.shape[1] == width else rows]
+                for weight_ref in weight_refs
+            ],
+            axis=0,
+        )
         total = dot(grad, weight, 1, 0)
         kept_ref[:, columns] = total[:length]
         sent_ref[:, columns] = total[length:].astype(jnp.bfloat16)
@@ -301,7 +309,7 @@
 def partial_heads(weights, grad, grad_core, first, count):
     length = grad.shape[0] // 2
     return pl.pallas_call(
-        functools.partial(partial_kernel, first, count),
+        functools.partial(partial_kernel, first),
         in_specs=whole(2 + len(weights)),
         out_specs=whole(2),
         out_shape=[
@@ -314,35 +322,42 @@
     )(grad, grad_core, *weights)
 
 
-def columns_kernel(start, stop, wide_ref, *refs):
-    (outs_ref, outs_x_ref), arrived, out_ref = refs[:2], refs[2:-1], refs[-1]
-    rows = outs_ref.shape[0]
-    width = 2 * HD if rows % (2 * HD) == 0 else HD
-    for first in range(0, rows, width):
-        columns = slice(first, first + width)
+def columns_kernel(start, stop, starts, wide_ref, outs_ref, outs_x_ref, *refs):
+    arrived_refs, out_ref = refs[:-1], refs[-1]
+    bounds = {start, stop}
+    for arrived_ref, first in zip(arrived_refs, starts):
+        bounds |= {edge for edge in (first, first + arrived_ref.shape[0]) if start < edge < stop}
+    bounds = sorted(bounds)
+    for columns in column_blocks(outs_ref.shape[0]):
         outs = jnp.concatenate([outs_ref[columns], outs_x_ref[columns]], axis=1)
-        total = dot(wide_ref[start:stop], outs, 1, 1)
-        for arrived_ref in arrived:
-            total = total + arrived_ref[start:stop, columns].astype(jnp.float32)
-        out_ref[:, columns] = total.astype(out_ref.dtype)
+        for low, high in zip(bounds[:-1], bounds[1:]):
+            total = dot(wide_ref[low:high], outs, 1, 1)
+            for arrived_ref, first in zip(arrived_refs, starts):
+                if first <= low and high <= first + arrived_ref.shape[0]:
+                    rows = slice(low - first, high - first)
+                    total = total + arrived_ref[rows, columns].astype(jnp.float32)
+            out_ref[low - start : high - start, columns] = total.astype(out_ref.dtype)
 
 
 def columns_sum(wide, outs, outs_x, arrived, start, stop, kind):
     rows = outs.shape[0]
+    arrived = [(p, first) for p, first in arrived if first < stop and start < first + p.shape[0]]
     if start % 16 or stop % 16:
         total = dot(wide[start:stop], jnp.concatenate([outs, outs_x], axis=1), 1, 1)
-        for piece in arrived:
-            total = total + piece[start:stop].astype(jnp.float32)
+        for piece, first in arrived:
+            low, high = max(start, first), min(stop, first + piece.shape[0])
+            part = piece[low - first : high - first].astype(jnp.float32)
+            total = total + jnp.pad(part, ((low - start, stop - high), (0, 0)))
         return total.astype(kind)
     return pl.pallas_call(
-        functools.partial(columns_kernel, start, stop),
+        functools.partial(columns_kernel, start, stop, [first for _, first in arrived]),
         in_specs=whole(3 + len(arrived)),
         out_specs=whole(1)[0],
         out_shape=jax.ShapeDtypeStruct((stop - start, rows), kind),
         compiler_params=pltpu.CompilerParams(vmem_limit_bytes=VMEM_LIMIT),
         cost_estimate=SMALL_COST,
         name="columns_sum",
-    )(wide, outs, outs_x, *arrived)
+    )(wide, outs, outs_x, *[piece for piece, _ in arrived])
 
 
 def assemble_kernel(local_heads, firsts, pos_ref, *refs):
@@ -457,16 +472,9 @@
     grad_x = swap_with(turned_far, "dp", 2)
 
     shards = {0: after(out_weight, turned).T}
-    bit = layers // 2
-    while bit:
-        for known in sorted(shards):
-            shards[known ^ bit] = swap_with(shards[known], "dp", bit * GROUP)
-        bit //= 2
-    near = [shards[layer] for layer in shards if layer and not layer & (layer - 1)]
-    shards = [shards[layer] for layer in layer_order]
-    weights = shards + [swap_with(shard, "dp", 1) for shard in shards]
-    if cols % 16:
-        weights = [jnp.concatenate(weights, axis=0)]
+    bits = [1 << power for power in reversed(range(layers.bit_length() - 1))]
+    for bit in bits:
+        shards[bit] = swap_with(shards[0], "dp", bit * GROUP)
 
     rest = [(0, firsts[part], counts[part]) for part in range(len(counts))]
     rest += [(k, firsts[part], counts[part]) for part in range(1, len(counts)) for k in others]
@@ -474,86 +482,132 @@
     own_heads, rest = rest[: len(counts)], rest[len(counts) :]
     for part in range(1, len(counts)):
         sent = rest[(part - 1) * len(others) : part * len(others)]
-        received.append([swap_with(after(sent[k - 1], grad_x, *received[part - 1]), "seq", k) for k in others])
-
-    def gather_tokens(dc, *earlier):
-        held = after(jnp.stack([turned[dc], grad_x[dc]]), *earlier)
-        return [held] + [swap_with(held, "seq", k) for k in others]
-
-    core_pieces = gather_tokens(1, *received[0])
-    pieces = gather_tokens(0, *received[-1])
-
+        received.append(
+            [swap_with(after(sent[k - 1], grad_x, *received[part - 1]), "seq", k) for k in others]
+        )
+
+    def swap_core(part, layer, *earlier):
+        rows = slice(firsts[part] * HD, (firsts[part] + counts[part]) * HD)
+        shard = after(shards[layer], *earlier) if earlier else shards[layer]
+        core_shards[part][layer] = swap_with(shard[:, rows], "dp", 1)
+
+    core_shards = [{} for _ in counts]
+    for part in range(len(counts)):
+        swap_core(part, 0)
+    own_core = [each[0] for each in core_shards]
     outs_all, probs_all, outs_x = [], [], []
     for part, count in enumerate(counts):
         outs, probs = attend_forward(
             pos,
             mask,
-            [own_heads[part]] + list(received[part]),
+            [after(own_heads[part], *own_core)] + list(received[part]),
             firsts[part],
             count,
             local_heads,
         )
         outs_all.append(outs)
         probs_all.append(probs)
-        outs_x.append(swap_with(after(outs, *near) if part else outs, "dp", 2))
-
-    core_wide, core_turned = join_pieces(
-        [core_pieces[0]] + [after(piece, outs_all[-1]) for piece in core_pieces[1:]]
-    )
-    arrived = []
+        outs_x.append(swap_with(outs, "dp", 2))
+    for layer in bits:
+        swap_core(0, layer, outs_all[0])
+    near = [core_shards[0][layer] for layer in bits]
+    for bit in bits:
+        for known in sorted(shards):
+            if known & (bit - 1) == 0 and known ^ bit not in shards:
+                shards[known ^ bit] = swap_with(
+                    after(shards[known], outs_all[0]), "dp", bit * GROUP
+                )
     for part in range(len(counts)):
-        if part:
-            outs_x[part] = after(outs_x[part], *pieces[1:], *shards)
+        for layer in layer_order:
+            if layer not in core_shards[part]:
+                swap_core(part, layer)
+    shards = [shards[layer] for layer in layer_order]
+
+    def weights_of(part):
+        rows = slice(firsts[part] * HD, (firsts[part] + counts[part]) * HD)
+        core = [core_shards[part][layer] for layer in layer_order]
+        if cols % 16:
+            return [jnp.concatenate([shard[:, rows] for shard in shards] + core, axis=0)]
+        return shards + core
+
+    def gather_tokens(dc, *earlier):
+        held = after(jnp.stack([turned[dc], grad_x[dc]]), *earlier)
+        return [held] + [swap_with(held, "seq", k) for k in others]
+
+    core_pieces = gather_tokens(1, *received[-1], *near)
+    pieces = gather_tokens(0, *received[-1])
+
+    core_pieces[1:] = [after(piece, outs_all[-1]) for piece in core_pieces[1:]]
+    core_wide, core_turned = join_pieces(core_pieces)
+    arrived = [[] for _ in counts]
+    quarter = class_cols // 4
+
+    def send_core(part, start, stop, *earlier):
         sent = columns_sum(
-            core_wide, outs_all[part], outs_x[part], [], 0, class_cols, jnp.bfloat16
+            after(core_wide, *earlier) if earlier else core_wide,
+            outs_all[part],
+            outs_x[part],
+            [],
+            start * quarter,
+            stop * quarter,
+            jnp.bfloat16,
         )
-        arrived.append([swap_with(sent, "dp", 1)])
-
-    grad_wide, grad_turned = join_pieces(
-        [pieces[0]] + [after(piece, *[each[0] for each in arrived]) for piece in pieces[1:]]
-    )
-
-    def columns_of(part, start, stop, kind):
-        return columns_sum(
-            grad_wide, outs_all[part], outs_x[part], arrived[part], start, stop, kind
-        )
-
-    kept, got, steps = [], [], []
+        arrived[part].append((swap_with(sent, "dp", 1), start * quarter))
+
+    send_core(0, 3, 4)
+    send_core(0, 2, 3)
+    for part in range(1, len(counts)):
+        send_core(part, 2, 4)
+
+    pieces[1:] = [after(piece, *shards) for piece in pieces[1:]]
+    grad_wide, grad_turned = join_pieces(pieces)
+
+    def columns_of(part, start, stop, kind, *earlier):
+        outs = after(outs_all[part], *earlier) if earlier else outs_all[part]
+        return columns_sum(grad_wide, outs, outs_x[part], arrived[part], start, stop, kind)
+
+    kept, got, last = [], [], []
     for part, count in enumerate(counts):
-        steps.append([columns_of(part, class_cols // 2, class_cols, jnp.bfloat16)])
-        arrived[part].append(swap_with(steps[part][0], "dp", GROUP))
+        sent = columns_of(part, quarter * 2, quarter * 4, jnp.bfloat16, *last)
+        arrived[part].append((swap_with(sent, "dp", GROUP), 0))
         total, sent = partial_heads(
-            weights, after(grad_turned, steps[part][0]), core_turned, firsts[part], count
+            weights_of(part), after(grad_turned, sent), core_turned, firsts[part], count
         )
         kept.append(total)
         got.append(swap_with(sent, "dp", 2))
-
-    weight_parts = []
-    for part in range(len(counts)):
-        size, bit = class_cols // 2, 1
-        while 2 * bit < layers:
-            size //= 2
-            bit *= 2
-            steps[part].append(columns_of(part, size, 2 * size, jnp.bfloat16))
-            arrived[part].append(swap_with(steps[part][-1], "dp", bit * GROUP))
-        last = arrived[part].pop()
-        weight_parts.append((columns_of(part, 0, size, jnp.float32), last))
-
-    back_parts = []
+        last = [total]
+        send_core(part, 0, 2, total)
+
+    weight_parts, back_parts = [], []
     for part, count in enumerate(counts):
-        earlier = [steps[part][-1], steps[-1][0]]
-        if part:
-            earlier.append(weight_parts[part - 1][1])
+        size = class_cols // 2
+
+        def next_sums(last):
+            size = class_cols // 2
+            for bit in [1 << power for power in range(1, layers.bit_length() - 1)]:
+                size //= 2
+                sent = columns_of(part, size, 2 * size, jnp.bfloat16, *last)
+                arrived[part].append((swap_with(sent, "dp", bit * GROUP), 0))
+                last = [sent]
+            return last
+
+        if part == 0:
+            last = next_sums(last)
         backs = attend_backward(
             [own_heads[part]] + list(received[part]),
             probs_all[part],
-            after(kept[part], *earlier),
+            after(kept[part], *last),
             got[part],
             count,
         )
+        last = [backs[0]]
         back_parts.append(backs[0])
         back_parts += [swap_with(backs[k], "seq", k) for k in others]
-    back_parts[-1] = after(back_parts[-1], steps[-1][-1])
+        if part:
+            last = next_sums(last + [arrived[0][-1][0]])
+    for part in range(len(counts)):
+        final, _ = arrived[part].pop()
+        weight_parts.append((columns_of(part, 0, cols, jnp.float32, *last), final))
     grad_queries, grad_keys = assemble(pos, back_parts, local_heads, firsts)
     return (grad_queries, grad_keys, add_parts(weight_parts).T)
 

time: 113 us -> 104 us (0.920)
  waiting for transfers between devices: 53.6 us -> 39.2 us
  local copies, waits for them, and re-layouts: 4.49 us -> 8.18 us
  starting transfers between devices: 27.7 us -> 29.5 us
    ppermute x24 -> x31, waiting for transfers between devices: 53.6 us -> 39.2 us  [swap_with(): lax.ppermute(array_in, axis_name, [(i, i ^ distance) for i in range(size)])]
    unnamed x14 -> x28, local copies, waits for them, and re-layouts: 3.37 us -> 7.22 us
    ppermute x24 -> x31, starting transfers between devices: 27.7 us -> 29.5 us  [swap_with(): lax.ppermute(array_in, axis_name, [(i, i ^ distance) for i in range(size)])]
    pallas_call x10 -> x13, Pallas kernels: 8.67 us -> 7.29 us  [the longest x11 4.92 us: columns_sum(): pl.pallas_call(functools.partial(columns_kernel, start, stop, [first for...]
    pallas_call x2, Pallas kernels: 3.85 us -> 5.12 us  [attend_backward(): pl.pallas_call(functools.partial(backward_kernel, count, len(pieces)), in...]
  transfers between devices with their start and end apart: 24 -> 31, of which waited for: 12 -> 10; matrix products, arithmetic and copies ran while one was open for 1% -> 1% of each run, Pallas kernels for 20% -> 21%
where the time goes in v3:
time: 104 us; the launch traced here: 103 us
  waiting for transfers between devices  39.2 us (38%)
  starting transfers between devices  29.5 us (28%)
  Pallas kernels  25.3 us (24%)
  local copies, waits for them, and re-layouts  8.18 us (8%)
  between operations  1.15 us (1%)
    ppermute x31, waiting for transfers between devices, swap_with(): lax.ppermute(array_in, axis_name, [(i, i ^ distance) for i in range(size)])  39.2 us
    ppermute x31, starting transfers between devices, swap_with(): lax.ppermute(array_in, axis_name, [(i, i ^ distance) for i in range(size)])  29.5 us
    unnamed x28, local copies, waits for them, and re-layouts  7.22 us
    pallas_call x2, Pallas kernels, attend_forward(): pl.pallas_call(functools.partial(forward_kernel, first, count, local_head...  6.12 us
    pallas_call x2, Pallas kernels, attend_backward(): pl.pallas_call(functools.partial(backward_kernel, count, len(pieces)), in...  5.12 us
    pallas_call x11, Pallas kernels, columns_sum(): pl.pallas_call(functools.partial(columns_kernel, start, stop, [first for...  4.92 us
    pallas_call x2, Pallas kernels, partial_heads(): pl.pallas_call(functools.partial(partial_kernel, first), in_specs=whole(2...  2.37 us
  transfers between devices with their start and end apart: 31, of which 10 were waited for; matrix products, arithmetic and copies ran while one was open for 1% of the time, Pallas kernels for 21%

profile of v3, /device:TPU:0, one launch (start us, length us, event | category | flops | bytes accessed | tf_op | source)
XLA Modules:
  0.0 103.4 jit_solution(8075481083642075837)
XLA Ops:
  0.7 2.0 %collect_columns.1 = bf16[3,128,768]{2,1,0:T(8,128)(2,1)} custom-call(s32[1]{0:T(128)} %bitcast.pos_ref, bf16[128,3072]{1,0:T(8,128)(2,1)} %refs_0_.3, bf16[128,3072]{1,0:T(8,128)(2,1)} %refs_1_.3, bf16[128,3072]{1,0:T(8,128)(2,1)} %refs_2_.3), custom_call_target="tpu_custom_call" | custom-call | tf_op jit(solution)/shard_map/collect_columns/pallas_call | solution.py:217
  2.7 3.0 %collective-permute-start = (bf16[3,128,768]{2,1,0:T(8,128)(2,1)}, bf16[3,128,768]{2,1,0:T(8,128)(2,1)S(1)}, u32[]{:S(2)}, u32[]{:S(2)}) collective-permute-start(bf16[3,128,768]{2,1,0:T(8,128)(2,1)} %collect_columns.1), channel_id=1, source_target_pairs={{0,1},{1,0},{2,3},{3,2},{4,5},{5,4},{6,7},{7,6},{8,9},{9,8},{10,11... | collective-permute-start | bytes 1769480 | tf_op jit(solution)/shard_map/ppermute | solution.py:429
  5.7 1.1 %copy-done.9 = bf16[128,2560]{1,0:T(8,128)(2,1)S(1)} copy-done((bf16[128,2560]{1,0:T(8,128)(2,1)S(1)}, bf16[128,2560]{1,0:T(8,128)(2,1)}, u32[]{:S(2)}) %copy-start.9) | copy-done | bytes 655384
  6.8 1.1 %turn_columns.1 = (bf16[2,640,128]{2,1,0:T(8,128)(2,1)S(1)}, bf16[2,640,128]{2,1,0:T(8,128)(2,1)S(1)}) custom-call(s32[1]{0:T(128)} %bitcast.1.row_ref, bf16[128,2560]{1,0:T(8,128)(2,1)S(1)} %copy-done.9), custom_call_target="tpu_custom_call" | custom-call | tf_op jit(solution)/shard_map/turn_columns/pallas_call | solution.py:250
  7.9 1.6 %collective-permute-start.3 = (bf16[2,640,128]{2,1,0:T(8,128)(2,1)S(1)}, bf16[2,640,128]{2,1,0:T(8,128)(2,1)S(1)}, u32[]{:S(2)}, u32[]{:S(2)}) collective-permute-start(bf16[2,640,128]{2,1,0:T(8,128)(2,1)S(1)} %get-tuple-element.56), channel_id=1, source_target_pairs={{0,4},{2,6},{4,0},{6,2},{8,12},{10,14},{12,8},{14,10},{16,20},{18,... | collective-permute-start | bytes 983048 | tf_op jit(solution)/shard_map/ppermute | solution.py:429
  9.4 2.6 %collective-permute-start.6 = (bf16[160,1536]{1,0:T(8,128)(2,1)S(1)}, bf16[160,1536]{1,0:T(8,128)(2,1)S(1)}, u32[]{:S(2)}, u32[]{:S(2)}) collective-permute-start(bf16[160,1536]{1,0:T(8,128)(2,1)S(1)} %bitcast.4), channel_id=1, source_target_pairs={{0,16},{2,18},{4,20},{6,22},{8,24},{10,26},{12,28},{14,30},{16,0},... | collective-permute-start | bytes 1474568 | tf_op jit(solution)/shard_map/ppermute | solution.py:429
  12.0 1.6 %collective-permute-start.7 = (bf16[160,1536]{1,0:T(8,128)(2,1)S(1)}, bf16[160,1536]{1,0:T(8,128)(2,1)S(1)}, u32[]{:S(2)}, u32[]{:S(2)}) collective-permute-start(bf16[160,1536]{1,0:T(8,128)(2,1)S(1)} %bitcast.5), channel_id=1, source_target_pairs={{0,8},{2,10},{4,12},{6,14},{8,0},{10,2},{12,4},{14,6},{16,24},{18,... | collective-permute-start | bytes 1474568 | tf_op jit(solution)/shard_map/ppermute | solution.py:429
  13.6 1.1 %copy-done.1 = bf16[128,3072]{1,0:T(8,128)(2,1)S(1)} copy-done((bf16[128,3072]{1,0:T(8,128)(2,1)S(1)}, bf16[128,3072]{1,0:T(8,128)(2,1)}, u32[]{:S(2)}) %copy-start.1) | copy-done | bytes 786456
  14.8 1.1 %copy-done.2 = bf16[128,3072]{1,0:T(8,128)(2,1)S(1)} copy-done((bf16[128,3072]{1,0:T(8,128)(2,1)S(1)}, bf16[128,3072]{1,0:T(8,128)(2,1)}, u32[]{:S(2)}) %copy-start.2) | copy-done | bytes 786456
  15.9 1.1 %copy-done.3 = bf16[128,3072]{1,0:T(8,128)(2,1)S(1)} copy-done((bf16[128,3072]{1,0:T(8,128)(2,1)S(1)}, bf16[128,3072]{1,0:T(8,128)(2,1)}, u32[]{:S(2)}) %copy-start.3) | copy-done | bytes 786456
  19.6 1.4 %collective-permute-start.4 = (bf16[3,128,768]{2,1,0:T(8,128)(2,1)}, bf16[3,128,768]{2,1,0:T(8,128)(2,1)}, u32[]{:S(2)}, u32[]{:S(2)}) collective-permute-start(bf16[3,128,768]{2,1,0:T(8,128)(2,1)} %get-tuple-element.58), channel_id=1, source_target_pairs={{0,1},{1,0},{2,3},{3,2},{4,5},{5,4},{6,7},{7,6},{8,9},{9,8},{10,11... | collective-permute-start | bytes 1769480 | tf_op jit(solution)/shard_map/ppermute | solution.py:429
  22.4 1.4 %collective-permute-done.1.refs_4_ = bf16[160,768]{1,0:T(8,128)(2,1)S(1)} collective-permute-done((bf16[160,768]{1,0:T(8,128)(2,1)}, bf16[160,768]{1,0:T(8,128)(2,1)S(1)}, u32[]{:S(2)}, u32[]{:S(2)}) %collective-permute-start.1) | collective-permute-done | bytes 245792 | tf_op jit(solution)/shard_map/ppermute | solution.py:429
  24.8 2.9 %attend_forward.2 = (bf16[768,256]{1,0:T(8,128)(2,1)S(1)}, f32[6,256,256]{2,1,0:T(8,128)S(1)}) custom-call(s32[1]{0:T(128)} %bitcast.pos_ref, s32[24,4]{1,0:T(8,128)S(1)} %copy.10.mask_ref, bf16[3,128,768]{2,1,0:T(8,128)(2,1)S(1)} %copy-done.7, bf16[3,128,768]{2,1,0:T(8,128)(2,1)S(1)} %collective-permute-done.refs_1_), custom_call_target="tpu_custom_call" | custom-call | tf_op jit(solution)/shard_map/attend_forward/pallas_call | solution.py:144
  27.7 5.7 %collective-permute-done.6.refs_1_ = bf16[160,1536]{1,0:T(8,128)(2,1)S(1)} collective-permute-done((bf16[160,1536]{1,0:T(8,128)(2,1)S(1)}, bf16[160,1536]{1,0:T(8,128)(2,1)S(1)}, u32[]{:S(2)}, u32[]{:S(2)}) %collective-permute-start.6) | collective-permute-done | bytes 491552 | tf_op jit(solution)/shard_map/ppermute | solution.py:429
  35.3 3.2 %attend_forward.3 = (bf16[768,256]{1,0:T(8,128)(2,1)S(1)}, f32[6,256,256]{2,1,0:T(8,128)S(1)}) custom-call(s32[1]{0:T(128)} %bitcast.pos_ref, s32[24,4]{1,0:T(8,128)S(1)} %copy.10.mask_ref, bf16[3,128,768]{2,1,0:T(8,128)(2,1)S(1)} %copy-done.5, bf16[3,128,768]{2,1,0:T(8,128)(2,1)} %collective-permute-done.4.refs_1_), custom_call_target="tpu_custom_call" | custom-call | tf_op jit(solution)/shard_map/attend_forward/pallas_call | solution.py:144
  38.5 1.6 %collective-permute-start.16 = (bf16[768,256]{1,0:T(8,128)(2,1)S(1)}, bf16[768,256]{1,0:T(8,128)(2,1)S(1)}, u32[]{:S(2)}, u32[]{:S(2)}) collective-permute-start(bf16[768,256]{1,0:T(8,128)(2,1)S(1)} %get-tuple-element.94.outs_ref), channel_id=1, source_target_pairs={{0,4},{2,6},{4,0},{6,2},{8,12},{10,14},{12,8},{14,10},{16,20},{18,... | collective-permute-start | bytes 1179656 | tf_op jit(solution)/shard_map/ppermute | solution.py:429
  40.7 1.6 %collective-permute-start.5 = (bf16[2,640,128]{2,1,0:T(8,128)(2,1)S(1)}, bf16[2,640,128]{2,1,0:T(8,128)(2,1)S(1)}, u32[]{:S(2)}, u32[]{:S(2)}) collective-permute-start(bf16[2,640,128]{2,1,0:T(8,128)(2,1)S(1)} %pad_maximum_fusion.refs_0_), channel_id=1, source_target_pairs={{0,1},{1,0},{2,3},{3,2},{4,5},{5,4},{6,7},{7,6},{8,9},{9,8},{10,11... | collective-permute-start | bytes 983048 | tf_op jit(solution)/shard_map/ppermute | solution.py:429
  42.3 8.5 %collective-permute-done.12.refs_1_ = bf16[2,640,128]{2,1,0:T(8,128)(2,1)S(1)} collective-permute-done((bf16[2,640,128]{2,1,0:T(8,128)(2,1)S(1)}, bf16[2,640,128]{2,1,0:T(8,128)(2,1)S(1)}, u32[]{:S(2)}, u32[]{:S(2)}) %collective-permute-start.12) | collective-permute-done | bytes 327712 | tf_op jit(solution)/shard_map/ppermute | solution.py:429
  52.6 1.6 %collective-permute-done.16.outs_x_ref = bf16[768,256]{1,0:T(8,128)(2,1)S(1)} collective-permute-done((bf16[768,256]{1,0:T(8,128)(2,1)S(1)}, bf16[768,256]{1,0:T(8,128)(2,1)S(1)}, u32[]{:S(2)}, u32[]{:S(2)}) %collective-permute-start.16) | collective-permute-done | bytes 393248 | tf_op jit(solution)/shard_map/ppermute | solution.py:429
  57.3 1.5 %collective-permute-start.21 = (bf16[320,768]{1,0:T(8,128)(2,1)S(1)}, bf16[320,768]{1,0:T(8,128)(2,1)S(1)}, u32[]{:S(2)}, u32[]{:S(2)}) collective-permute-start(bf16[320,768]{1,0:T(8,128)(2,1)S(1)} %columns_sum.13), channel_id=1, source_target_pairs={{0,8},{2,10},{4,12},{6,14},{8,0},{10,2},{12,4},{14,6},{16,24},{18,... | collective-permute-start | bytes 1474568 | tf_op jit(solution)/shard_map/ppermute | solution.py:429
  59.4 1.2 %partial_heads.2 = (f32[256,768]{1,0:T(8,128)S(1)}, bf16[256,768]{1,0:T(8,128)(2,1)S(1)}) custom-call(bf16[512,640]{1,0:T(8,128)(2,1)S(1)} %get-tuple-element.76.grad_ref, bf16[512,640]{1,0:T(8,128)(2,1)S(1)} %get-tuple-element.73.grad_core_ref, bf16[160,1536]{1,0:T(8,128)(2,1)S(1)} %bitcast.7, bf16[160,1536]{1,0:T(8,128)(2,1)S(1)} %collective-permute-done.6.refs_1_, ...), custom_call_target="tpu_custom_call" | custom-call | tf_op jit(solution)/shard_map/partial_heads/pallas_call | solution.py:311
  62.4 1.2 %partial_heads.3 = (f32[256,768]{1,0:T(8,128)S(1)}, bf16[256,768]{1,0:T(8,128)(2,1)S(1)}) custom-call(bf16[512,640]{1,0:T(8,128)(2,1)S(1)} %get-tuple-element.76.grad_ref, bf16[512,640]{1,0:T(8,128)(2,1)S(1)} %get-tuple-element.73.grad_core_ref, bf16[160,1536]{1,0:T(8,128)(2,1)S(1)} %bitcast.8, bf16[160,1536]{1,0:T(8,128)(2,1)S(1)} %collective-permute-done.6.refs_1_, ...), custom_call_target="tpu_custom_call" | custom-call | tf_op jit(solution)/shard_map/partial_heads/pallas_call | solution.py:311
  63.5 1.6 %collective-permute-start.25 = (bf16[256,768]{1,0:T(8,128)(2,1)S(1)}, bf16[256,768]{1,0:T(8,128)(2,1)S(1)}, u32[]{:S(2)}, u32[]{:S(2)}) collective-permute-start(bf16[256,768]{1,0:T(8,128)(2,1)S(1)} %get-tuple-element.86), channel_id=1, source_target_pairs={{0,4},{2,6},{4,0},{6,2},{8,12},{10,14},{12,8},{14,10},{16,20},{18,... | collective-permute-start | bytes 1179656 | tf_op jit(solution)/shard_map/ppermute | solution.py:429
  66.1 5.2 %collective-permute-done.21.refs_0_ = bf16[320,768]{1,0:T(8,128)(2,1)S(1)} collective-permute-done((bf16[320,768]{1,0:T(8,128)(2,1)S(1)}, bf16[320,768]{1,0:T(8,128)(2,1)S(1)}, u32[]{:S(2)}, u32[]{:S(2)}) %collective-permute-start.21) | collective-permute-done | bytes 491552 | tf_op jit(solution)/shard_map/ppermute | solution.py:429
  71.8 3.4 %collective-permute-start.27 = (bf16[160,768]{1,0:T(8,128)(2,1)S(1)}, bf16[160,768]{1,0:T(8,128)(2,1)S(1)}, u32[]{:S(2)}, u32[]{:S(2)}) collective-permute-start(bf16[160,768]{1,0:T(8,128)(2,1)S(1)} %columns_sum.17), channel_id=1, source_target_pairs={{0,16},{2,18},{4,20},{6,22},{8,24},{10,26},{12,28},{14,30},{16,0},... | collective-permute-start | bytes 737288 | tf_op jit(solution)/shard_map/ppermute | solution.py:429
  75.2 2.1 %attend_backward.2 = (bf16[2,128,768]{2,1,0:T(8,128)(2,1)S(1)}, bf16[2,128,768]{2,1,0:T(8,128)(2,1)S(1)}) custom-call(bf16[3,128,768]{2,1,0:T(8,128)(2,1)S(1)} %copy-done.8, bf16[3,128,768]{2,1,0:T(8,128)(2,1)S(1)} %collective-permute-done.refs_1_, f32[6,256,256]{2,1,0:T(8,128)S(1)} %get-tuple-element.55.refs_2_, f32[256,768]{1,0:T(8,128)S(1)} %get-tuple-element.80.refs_3_, ...), custom_call_target="tpu_custom_call" | custom-call | tf_op jit(solution)/shard_map/attend_backward/pallas_call | solution.py:160
  77.9 3.1 %collective-permute-done.25.refs_4_ = bf16[256,768]{1,0:T(8,128)(2,1)S(1)} collective-permute-done((bf16[256,768]{1,0:T(8,128)(2,1)S(1)}, bf16[256,768]{1,0:T(8,128)(2,1)S(1)}, u32[]{:S(2)}, u32[]{:S(2)}) %collective-permute-start.25) | collective-permute-done | bytes 393248 | tf_op jit(solution)/shard_map/ppermute | solution.py:429
  81.1 3.0 %attend_backward.3 = (bf16[2,128,768]{2,1,0:T(8,128)(2,1)S(1)}, bf16[2,128,768]{2,1,0:T(8,128)(2,1)S(1)}) custom-call(bf16[3,128,768]{2,1,0:T(8,128)(2,1)S(1)} %copy-done.5, bf16[3,128,768]{2,1,0:T(8,128)(2,1)} %collective-permute-done.4.refs_1_, f32[6,256,256]{2,1,0:T(8,128)S(1)} %get-tuple-element.84.refs_2_, f32[256,768]{1,0:T(8,128)S(1)} %get-tuple-element.85.refs_3_, ...), custom_call_target="tpu_custom_call" | custom-call | tf_op jit(solution)/shard_map/attend_backward/pallas_call | solution.py:160
  84.6 1.1 %collective-permute-done.27.refs_1_ = bf16[160,768]{1,0:T(8,128)(2,1)S(1)} collective-permute-done((bf16[160,768]{1,0:T(8,128)(2,1)S(1)}, bf16[160,768]{1,0:T(8,128)(2,1)S(1)}, u32[]{:S(2)}, u32[]{:S(2)}) %collective-permute-start.27) | collective-permute-done | bytes 245792 | tf_op jit(solution)/shard_map/ppermute | solution.py:429
  87.2 2.4 %collective-permute-start.30 = (bf16[160,768]{1,0:T(8,128)(2,1)S(1)}, bf16[160,768]{1,0:T(8,128)(2,1)S(1)}, u32[]{:S(2)}, u32[]{:S(2)}) collective-permute-start(bf16[160,768]{1,0:T(8,128)(2,1)S(1)} %columns_sum.19), channel_id=1, source_target_pairs={{0,16},{2,18},{4,20},{6,22},{8,24},{10,26},{12,28},{14,30},{16,0},... | collective-permute-start | bytes 737288 | tf_op jit(solution)/shard_map/ppermute | solution.py:429
  90.4 10.6 %collective-permute-done.30.refs_3_ = bf16[160,768]{1,0:T(8,128)(2,1)S(1)} collective-permute-done((bf16[160,768]{1,0:T(8,128)(2,1)S(1)}, bf16[160,768]{1,0:T(8,128)(2,1)S(1)}, u32[]{:S(2)}, u32[]{:S(2)}) %collective-permute-start.30) | collective-permute-done | bytes 245792 | tf_op jit(solution)/shard_map/ppermute | solution.py:429
  102.0 1.2 %assemble.1 = (bf16[128,3072]{1,0:T(8,128)(2,1)}, bf16[128,3072]{1,0:T(8,128)(2,1)}) custom-call(s32[1]{0:T(128)} %bitcast.pos_ref, bf16[2,128,768]{2,1,0:T(8,128)(2,1)S(1)} %get-tuple-element.82.refs_0_, bf16[2,128,768]{2,1,0:T(8,128)(2,1)S(1)} %collective-permute-done.24.refs_1_, bf16[2,128,768]{2,1,0:T(8,128)(2,1)S(1)} %get-tuple-element.87.refs_2_, ...), custom_call_target="tpu_custom_call" | custom-call | tf_op jit(solution)/shard_map/assemble/pallas_call | solution.py:385
  (94 shorter events, 20.5 us)
Async XLA Ops:
  0.6 13.0 %copy-start.12 = (s32[24,4,4]{0,2,1:T(4,128)S(1)}, s32[24,4,4]{0,2,1:T(4,128)}, u32[]{:S(2)}) copy-start(s32[24,4,4]{0,2,1:T(4,128)} %param.12) | copy-start | bytes 4612
  2.7 16.9 %collective-permute-start = (bf16[3,128,768]{2,1,0:T(8,128)(2,1)}, bf16[3,128,768]{2,1,0:T(8,128)(2,1)S(1)}, u32[]{:S(2)}, u32[]{:S(2)}) collective-permute-start(bf16[3,128,768]{2,1,0:T(8,128)(2,1)} %collect_columns.1), channel_id=1, source_target_pairs={{0,1},{1,0},{2,3},{3,2},{4,5},{5,4},{6,7},{7,6},{8,9},{9,8},{10,11... | collective-permute-start | bytes 1769480 | tf_op jit(solution)/shard_map/ppermute | solution.py:429
  7.9 11.7 %collective-permute-start.3 = (bf16[2,640,128]{2,1,0:T(8,128)(2,1)S(1)}, bf16[2,640,128]{2,1,0:T(8,128)(2,1)S(1)}, u32[]{:S(2)}, u32[]{:S(2)}) collective-permute-start(bf16[2,640,128]{2,1,0:T(8,128)(2,1)S(1)} %get-tuple-element.56), channel_id=1, source_target_pairs={{0,4},{2,6},{4,0},{6,2},{8,12},{10,14},{12,8},{14,10},{16,20},{18,... | collective-permute-start | bytes 983048 | tf_op jit(solution)/shard_map/ppermute | solution.py:429
  9.4 23.9 %collective-permute-start.6 = (bf16[160,1536]{1,0:T(8,128)(2,1)S(1)}, bf16[160,1536]{1,0:T(8,128)(2,1)S(1)}, u32[]{:S(2)}, u32[]{:S(2)}) collective-permute-start(bf16[160,1536]{1,0:T(8,128)(2,1)S(1)} %bitcast.4), channel_id=1, source_target_pairs={{0,16},{2,18},{4,20},{6,22},{8,24},{10,26},{12,28},{14,30},{16,0},... | collective-permute-start | bytes 1474568 | tf_op jit(solution)/shard_map/ppermute | solution.py:429
  12.0 22.0 %collective-permute-start.7 = (bf16[160,1536]{1,0:T(8,128)(2,1)S(1)}, bf16[160,1536]{1,0:T(8,128)(2,1)S(1)}, u32[]{:S(2)}, u32[]{:S(2)}) collective-permute-start(bf16[160,1536]{1,0:T(8,128)(2,1)S(1)} %bitcast.5), channel_id=1, source_target_pairs={{0,8},{2,10},{4,12},{6,14},{8,0},{10,2},{12,4},{14,6},{16,24},{18,... | collective-permute-start | bytes 1474568 | tf_op jit(solution)/shard_map/ppermute | solution.py:429
  19.6 15.6 %collective-permute-start.4 = (bf16[3,128,768]{2,1,0:T(8,128)(2,1)}, bf16[3,128,768]{2,1,0:T(8,128)(2,1)}, u32[]{:S(2)}, u32[]{:S(2)}) collective-permute-start(bf16[3,128,768]{2,1,0:T(8,128)(2,1)} %get-tuple-element.58), channel_id=1, source_target_pairs={{0,1},{1,0},{2,3},{3,2},{4,5},{5,4},{6,7},{7,6},{8,9},{9,8},{10,11... | collective-permute-start | bytes 1769480 | tf_op jit(solution)/shard_map/ppermute | solution.py:429
  21.7 2.0 %collective-permute-start.1 = (bf16[160,768]{1,0:T(8,128)(2,1)}, bf16[160,768]{1,0:T(8,128)(2,1)S(1)}, u32[]{:S(2)}, u32[]{:S(2)}) collective-permute-start(bf16[160,768]{1,0:T(8,128)(2,1)} %get-tuple-element.98), channel_id=1, source_target_pairs={{0,2},{2,0},{4,6},{6,4},{8,10},{10,8},{12,14},{14,12},{16,18},{18,... | collective-permute-start | bytes 737288 | tf_op jit(solution)/shard_map/ppermute | solution.py:429
  21.7 2.0 %collective-permute-start.2 = (bf16[160,768]{1,0:T(8,128)(2,1)S(1)}, bf16[160,768]{1,0:T(8,128)(2,1)S(1)}, u32[]{:S(2)}, u32[]{:S(2)}) collective-permute-start(bf16[160,768]{1,0:T(8,128)(2,1)S(1)} %get-tuple-element.97), channel_id=1, source_target_pairs={{0,2},{2,0},{4,6},{6,4},{8,10},{10,8},{12,14},{14,12},{16,18},{18,... | collective-permute-start | bytes 737288 | tf_op jit(solution)/shard_map/ppermute | solution.py:429
  33.4 21.4 %collective-permute-start.8 = (bf16[160,1536]{1,0:T(8,128)(2,1)S(1)}, bf16[160,1536]{1,0:T(8,128)(2,1)S(1)}, u32[]{:S(2)}, u32[]{:S(2)}) collective-permute-start(bf16[160,1536]{1,0:T(8,128)(2,1)S(1)} %collective-permute-done.6.refs_1_), channel_id=1, source_target_pairs={{0,8},{2,10},{4,12},{6,14},{8,0},{10,2},{12,4},{14,6},{16,24},{18,... | collective-permute-start | bytes 1474568 | tf_op jit(solution)/shard_map/ppermute | solution.py:429
  34.0 6.1 %collective-permute-start.10 = (bf16[160,768]{1,0:T(8,128)(2,1)S(1)}, bf16[160,768]{1,0:T(8,128)(2,1)S(1)}, u32[]{:S(2)}, u32[]{:S(2)}) collective-permute-start(bf16[160,768]{1,0:T(8,128)(2,1)S(1)} %slice.42), channel_id=1, source_target_pairs={{0,2},{2,0},{4,6},{6,4},{8,10},{10,8},{12,14},{14,12},{16,18},{18,... | collective-permute-start | bytes 737288 | tf_op jit(solution)/shard_map/ppermute | solution.py:429
  34.1 6.0 %collective-permute-start.11 = (bf16[160,768]{1,0:T(8,128)(2,1)S(1)}, bf16[160,768]{1,0:T(8,128)(2,1)S(1)}, u32[]{:S(2)}, u32[]{:S(2)}) collective-permute-start(bf16[160,768]{1,0:T(8,128)(2,1)S(1)} %slice.43), channel_id=1, source_target_pairs={{0,2},{2,0},{4,6},{6,4},{8,10},{10,8},{12,14},{14,12},{16,18},{18,... | collective-permute-start | bytes 737288 | tf_op jit(solution)/shard_map/ppermute | solution.py:429
  34.7 16.4 %collective-permute-start.9 = (bf16[768,256]{1,0:T(8,128)(2,1)S(1)}, bf16[768,256]{1,0:T(8,128)(2,1)S(1)}, u32[]{:S(2)}, u32[]{:S(2)}) collective-permute-start(bf16[768,256]{1,0:T(8,128)(2,1)S(1)} %get-tuple-element.93.outs_ref), channel_id=1, source_target_pairs={{0,4},{2,6},{4,0},{6,2},{8,12},{10,14},{12,8},{14,10},{16,20},{18,... | collective-permute-start | bytes 1179656 | tf_op jit(solution)/shard_map/ppermute | solution.py:429
  38.5 15.7 %collective-permute-start.16 = (bf16[768,256]{1,0:T(8,128)(2,1)S(1)}, bf16[768,256]{1,0:T(8,128)(2,1)S(1)}, u32[]{:S(2)}, u32[]{:S(2)}) collective-permute-start(bf16[768,256]{1,0:T(8,128)(2,1)S(1)} %get-tuple-element.94.outs_ref), channel_id=1, source_target_pairs={{0,4},{2,6},{4,0},{6,2},{8,12},{10,14},{12,8},{14,10},{16,20},{18,... | collective-permute-start | bytes 1179656 | tf_op jit(solution)/shard_map/ppermute | solution.py:429
  40.1 10.7 %collective-permute-start.12 = (bf16[2,640,128]{2,1,0:T(8,128)(2,1)S(1)}, bf16[2,640,128]{2,1,0:T(8,128)(2,1)S(1)}, u32[]{:S(2)}, u32[]{:S(2)}) collective-permute-start(bf16[2,640,128]{2,1,0:T(8,128)(2,1)S(1)} %pad_maximum_fusion.1.refs_0_), channel_id=1, source_target_pairs={{0,1},{1,0},{2,3},{3,2},{4,5},{5,4},{6,7},{7,6},{8,9},{9,8},{10,11... | collective-permute-start | bytes 983048 | tf_op jit(solution)/shard_map/ppermute | solution.py:429
  40.7 15.6 %collective-permute-start.5 = (bf16[2,640,128]{2,1,0:T(8,128)(2,1)S(1)}, bf16[2,640,128]{2,1,0:T(8,128)(2,1)S(1)}, u32[]{:S(2)}, u32[]{:S(2)}) collective-permute-start(bf16[2,640,128]{2,1,0:T(8,128)(2,1)S(1)} %pad_maximum_fusion.refs_0_), channel_id=1, source_target_pairs={{0,1},{1,0},{2,3},{3,2},{4,5},{5,4},{6,7},{7,6},{8,9},{9,8},{10,11... | collective-permute-start | bytes 983048 | tf_op jit(solution)/shard_map/ppermute | solution.py:429
  51.5 5.0 %collective-permute-start.13 = (bf16[160,768]{1,0:T(8,128)(2,1)S(1)}, bf16[160,768]{1,0:T(8,128)(2,1)S(1)}, u32[]{:S(2)}, u32[]{:S(2)}) collective-permute-start(bf16[160,768]{1,0:T(8,128)(2,1)S(1)} %columns_sum.11), channel_id=1, source_target_pairs={{0,2},{2,0},{4,6},{6,4},{8,10},{10,8},{12,14},{14,12},{16,18},{18,... | collective-permute-start | bytes 737288 | tf_op jit(solution)/shard_map/ppermute | solution.py:429
  52.0 4.6 %collective-permute-start.14 = (bf16[160,768]{1,0:T(8,128)(2,1)S(1)}, bf16[160,768]{1,0:T(8,128)(2,1)S(1)}, u32[]{:S(2)}, u32[]{:S(2)}) collective-permute-start(bf16[160,768]{1,0:T(8,128)(2,1)S(1)} %columns_sum.12), channel_id=1, source_target_pairs={{0,2},{2,0},{4,6},{6,4},{8,10},{10,8},{12,14},{14,12},{16,18},{18,... | collective-permute-start | bytes 737288 | tf_op jit(solution)/shard_map/ppermute | solution.py:429
  54.7 6.7 %collective-permute-start.17 = (bf16[320,768]{1,0:T(8,128)(2,1)S(1)}, bf16[320,768]{1,0:T(8,128)(2,1)S(1)}, u32[]{:S(2)}, u32[]{:S(2)}) collective-permute-start(bf16[320,768]{1,0:T(8,128)(2,1)S(1)} %columns_sum.14), channel_id=1, source_target_pairs={{0,2},{2,0},{4,6},{6,4},{8,10},{10,8},{12,14},{14,12},{16,18},{18,... | collective-permute-start | bytes 1474568 | tf_op jit(solution)/shard_map/ppermute | solution.py:429
  54.8 4.3 %collective-permute-start.15 = (bf16[160,768]{1,0:T(8,128)(2,1)S(1)}, bf16[160,768]{1,0:T(8,128)(2,1)S(1)}, u32[]{:S(2)}, u32[]{:S(2)}) collective-permute-start(bf16[160,768]{1,0:T(8,128)(2,1)S(1)} %get-tuple-element.96), channel_id=1, source_target_pairs={{0,2},{2,0},{4,6},{6,4},{8,10},{10,8},{12,14},{14,12},{16,18},{18,... | collective-permute-start | bytes 737288 | tf_op jit(solution)/shard_map/ppermute | solution.py:429
  56.3 4.7 %collective-permute-start.18 = (bf16[160,768]{1,0:T(8,128)(2,1)S(1)}, bf16[160,768]{1,0:T(8,128)(2,1)S(1)}, u32[]{:S(2)}, u32[]{:S(2)}) collective-permute-start(bf16[160,768]{1,0:T(8,128)(2,1)S(1)} %slice.53), channel_id=1, source_target_pairs={{0,2},{2,0},{4,6},{6,4},{8,10},{10,8},{12,14},{14,12},{16,18},{18,... | collective-permute-start | bytes 737288 | tf_op jit(solution)/shard_map/ppermute | solution.py:429
  57.3 14.1 %collective-permute-start.21 = (bf16[320,768]{1,0:T(8,128)(2,1)S(1)}, bf16[320,768]{1,0:T(8,128)(2,1)S(1)}, u32[]{:S(2)}, u32[]{:S(2)}) collective-permute-start(bf16[320,768]{1,0:T(8,128)(2,1)S(1)} %columns_sum.13), channel_id=1, source_target_pairs={{0,8},{2,10},{4,12},{6,14},{8,0},{10,2},{12,4},{14,6},{16,24},{18,... | collective-permute-start | bytes 1474568 | tf_op jit(solution)/shard_map/ppermute | solution.py:429
  58.8 3.5 %collective-permute-start.19 = (bf16[160,768]{1,0:T(8,128)(2,1)S(1)}, bf16[160,768]{1,0:T(8,128)(2,1)S(1)}, u32[]{:S(2)}, u32[]{:S(2)}) collective-permute-start(bf16[160,768]{1,0:T(8,128)(2,1)S(1)} %slice.54), channel_id=1, source_target_pairs={{0,2},{2,0},{4,6},{6,4},{8,10},{10,8},{12,14},{14,12},{16,18},{18,... | collective-permute-start | bytes 737288 | tf_op jit(solution)/shard_map/ppermute | solution.py:429
  59.1 3.3 %collective-permute-start.20 = (bf16[160,768]{1,0:T(8,128)(2,1)S(1)}, bf16[160,768]{1,0:T(8,128)(2,1)S(1)}, u32[]{:S(2)}, u32[]{:S(2)}) collective-permute-start(bf16[160,768]{1,0:T(8,128)(2,1)S(1)} %get-tuple-element.95), channel_id=1, source_target_pairs={{0,2},{2,0},{4,6},{6,4},{8,10},{10,8},{12,14},{14,12},{16,18},{18,... | collective-permute-start | bytes 737288 | tf_op jit(solution)/shard_map/ppermute | solution.py:429
  61.0 10.3 %collective-permute-start.22 = (bf16[320,768]{1,0:T(8,128)(2,1)S(1)}, bf16[320,768]{1,0:T(8,128)(2,1)S(1)}, u32[]{:S(2)}, u32[]{:S(2)}) collective-permute-start(bf16[320,768]{1,0:T(8,128)(2,1)S(1)} %columns_sum.16), channel_id=1, source_target_pairs={{0,2},{2,0},{4,6},{6,4},{8,10},{10,8},{12,14},{14,12},{16,18},{18,... | collective-permute-start | bytes 1474568 | tf_op jit(solution)/shard_map/ppermute | solution.py:429
  61.3 13.9 %collective-permute-start.23 = (bf16[256,768]{1,0:T(8,128)(2,1)S(1)}, bf16[256,768]{1,0:T(8,128)(2,1)S(1)}, u32[]{:S(2)}, u32[]{:S(2)}) collective-permute-start(bf16[256,768]{1,0:T(8,128)(2,1)S(1)} %get-tuple-element.81), channel_id=1, source_target_pairs={{0,4},{2,6},{4,0},{6,2},{8,12},{10,14},{12,8},{14,10},{16,20},{18,... | collective-permute-start | bytes 1179656 | tf_op jit(solution)/shard_map/ppermute | solution.py:429
  63.5 17.5 %collective-permute-start.25 = (bf16[256,768]{1,0:T(8,128)(2,1)S(1)}, bf16[256,768]{1,0:T(8,128)(2,1)S(1)}, u32[]{:S(2)}, u32[]{:S(2)}) collective-permute-start(bf16[256,768]{1,0:T(8,128)(2,1)S(1)} %get-tuple-element.86), channel_id=1, source_target_pairs={{0,4},{2,6},{4,0},{6,2},{8,12},{10,14},{12,8},{14,10},{16,20},{18,... | collective-permute-start | bytes 1179656 | tf_op jit(solution)/shard_map/ppermute | solution.py:429
  65.1 21.6 %collective-permute-start.28 = (bf16[320,768]{1,0:T(8,128)(2,1)S(1)}, bf16[320,768]{1,0:T(8,128)(2,1)S(1)}, u32[]{:S(2)}, u32[]{:S(2)}) collective-permute-start(bf16[320,768]{1,0:T(8,128)(2,1)S(1)} %columns_sum.15), channel_id=1, source_target_pairs={{0,8},{2,10},{4,12},{6,14},{8,0},{10,2},{12,4},{14,6},{16,24},{18,... | collective-permute-start | bytes 1474568 | tf_op jit(solution)/shard_map/ppermute | solution.py:429
  71.3 15.4 %collective-permute-start.29 = (bf16[320,768]{1,0:T(8,128)(2,1)S(1)}, bf16[320,768]{1,0:T(8,128)(2,1)S(1)}, u32[]{:S(2)}, u32[]{:S(2)}) collective-permute-start(bf16[320,768]{1,0:T(8,128)(2,1)S(1)} %columns_sum.18), channel_id=1, source_target_pairs={{0,2},{2,0},{4,6},{6,4},{8,10},{10,8},{12,14},{14,12},{16,18},{18,... | collective-permute-start | bytes 1474568 | tf_op jit(solution)/shard_map/ppermute | solution.py:429
  71.8 14.0 %collective-permute-start.27 = (bf16[160,768]{1,0:T(8,128)(2,1)S(1)}, bf16[160,768]{1,0:T(8,128)(2,1)S(1)}, u32[]{:S(2)}, u32[]{:S(2)}) collective-permute-start(bf16[160,768]{1,0:T(8,128)(2,1)S(1)} %columns_sum.17), channel_id=1, source_target_pairs={{0,16},{2,18},{4,20},{6,22},{8,24},{10,26},{12,28},{14,30},{16,0},... | collective-permute-start | bytes 737288 | tf_op jit(solution)/shard_map/ppermute | solution.py:429
  77.3 24.7 %collective-permute-start.24 = (bf16[2,128,768]{2,1,0:T(8,128)(2,1)S(1)}, bf16[2,128,768]{2,1,0:T(8,128)(2,1)S(1)}, u32[]{:S(2)}, u32[]{:S(2)}) collective-permute-start(bf16[2,128,768]{2,1,0:T(8,128)(2,1)S(1)} %get-tuple-element.83), channel_id=1, source_target_pairs={{0,1},{1,0},{2,3},{3,2},{4,5},{5,4},{6,7},{7,6},{8,9},{9,8},{10,11... | collective-permute-start | bytes 1179656 | tf_op jit(solution)/shard_map/ppermute | solution.py:429
  84.1 17.9 %collective-permute-start.26 = (bf16[2,128,768]{2,1,0:T(8,128)(2,1)S(1)}, bf16[2,128,768]{2,1,0:T(8,128)(2,1)S(1)}, u32[]{:S(2)}, u32[]{:S(2)}) collective-permute-start(bf16[2,128,768]{2,1,0:T(8,128)(2,1)S(1)} %get-tuple-element.88), channel_id=1, source_target_pairs={{0,1},{1,0},{2,3},{3,2},{4,5},{5,4},{6,7},{7,6},{8,9},{9,8},{10,11... | collective-permute-start | bytes 1179656 | tf_op jit(solution)/shard_map/ppermute | solution.py:429
  87.2 13.8 %collective-permute-start.30 = (bf16[160,768]{1,0:T(8,128)(2,1)S(1)}, bf16[160,768]{1,0:T(8,128)(2,1)S(1)}, u32[]{:S(2)}, u32[]{:S(2)}) collective-permute-start(bf16[160,768]{1,0:T(8,128)(2,1)S(1)} %columns_sum.19), channel_id=1, source_target_pairs={{0,16},{2,18},{4,20},{6,22},{8,24},{10,26},{12,28},{14,30},{16,0},... | collective-permute-start | bytes 737288 | tf_op jit(solution)/shard_map/ppermute | solution.py:429
  (13 other events, 65.4 us)

commit v4 on v3

--- a/solution.py
+++ b/solution.py
@@ -16,8 +16,10 @@
 VMEM_LIMIT = 16 * 1024 * 1024
 COLLECT_VMEM = 63 * 1024 * 1024
 GROUP = 4
+FIRST_COST = pl.CostEstimate(flops=3500000000, bytes_accessed=0, transcendentals=0)
+LAST_COST = pl.CostEstimate(flops=1200000000, bytes_accessed=0, transcendentals=0)
 SMALL_COST = pl.CostEstimate(flops=0, bytes_accessed=0, transcendentals=0)
-PARTS = (6, 6)
+PARTS = (8, 4)
 
 
 def dot(left, right, left_dim, right_dim):
@@ -155,7 +157,7 @@
     )(pos, mask, *pieces)
 
 
-def attend_backward(pieces, probs, grad, grad_recv, count):
+def attend_backward(pieces, probs, grad, grad_recv, count, cost):
     tokens = pieces[0].shape[1]
     return pl.pallas_call(
         functools.partial(backward_kernel, count, len(pieces)),
@@ -163,7 +165,7 @@
         out_specs=whole(len(pieces)),
         out_shape=[jax.ShapeDtypeStruct((2, tokens, count * HD), jnp.bfloat16)] * len(pieces),
         compiler_params=pltpu.CompilerParams(vmem_limit_bytes=VMEM_LIMIT),
-        cost_estimate=SMALL_COST,
+        cost_estimate=cost,
         name="attend_backward",
     )(*pieces, probs, grad, grad_recv)
 
@@ -233,9 +235,10 @@
         held_ref[block] = grad_ref[:, block * cols : (block + 1) * cols].T
     for dc in range(2):
         for slot, layer in enumerate(bit_reversed(layers)):
-            rows = slice(slot * cols, (slot + 1) * cols)
-            near_ref[dc, rows] = held_ref[row_ref[0] ^ (GROUP * layer + dc)]
-            far_ref[dc, rows] = held_ref[row_ref[0] ^ (GROUP * layer + 2 + dc)]
+            first = (dc * layers + slot) * cols
+            rows = slice(first, first + cols)
+            near_ref[rows] = held_ref[row_ref[0] ^ (GROUP * layer + dc)]
+            far_ref[rows] = held_ref[row_ref[0] ^ (GROUP * layer + 2 + dc)]
 
 
 def turn_columns(row, grad, dp_size):
@@ -245,13 +248,13 @@
         turned = grad.T.reshape(dp_size, cols, tokens)
         order = [GROUP * layer + kind for kind in range(GROUP) for layer in bit_reversed(layers)]
         turned = jnp.take(turned, row ^ jnp.array(order, jnp.int32), axis=0, mode="clip")
-        turned = turned.reshape(2, 2, layers * cols, tokens)
+        turned = turned.reshape(2, 2 * layers * cols, tokens)
         return turned[0], turned[1]
     return pl.pallas_call(
         turn_kernel,
         in_specs=whole(1, pltpu.SMEM) + whole(1),
         out_specs=whole(2),
-        out_shape=[jax.ShapeDtypeStruct((2, layers * cols, tokens), grad.dtype)] * 2,
+        out_shape=[jax.ShapeDtypeStruct((2 * layers * cols, tokens), grad.dtype)] * 2,
         scratch_shapes=[pltpu.VMEM((dp_size, cols, tokens), grad.dtype)],
         compiler_params=pltpu.CompilerParams(vmem_limit_bytes=VMEM_LIMIT),
         cost_estimate=SMALL_COST,
@@ -288,10 +291,9 @@
     )(*pieces)
 
 
-def partial_kernel(first, grad_ref, grad_core_ref, *refs):
+def partial_kernel(first, grad_ref, *refs):
     weight_refs, (kept_ref, sent_ref) = refs[:-2], refs[-2:]
     length, width = kept_ref.shape
-    grad = jnp.concatenate([grad_ref[...], grad_core_ref[...]], axis=1)
     for columns in column_blocks(width):
         rows = slice(first * HD + columns.start, first * HD + columns.stop)
         weight = jnp.concatenate(
@@ -301,16 +303,16 @@
             ],
             axis=0,
         )
-        total = dot(grad, weight, 1, 0)
+        total = dot(grad_ref[...], weight, 1, 0)
         kept_ref[:, columns] = total[:length]
         sent_ref[:, columns] = total[length:].astype(jnp.bfloat16)
 
 
-def partial_heads(weights, grad, grad_core, first, count):
+def partial_heads(weights, grad, first, count):
     length = grad.shape[0] // 2
     return pl.pallas_call(
         functools.partial(partial_kernel, first),
-        in_specs=whole(2 + len(weights)),
+        in_specs=whole(1 + len(weights)),
         out_specs=whole(2),
         out_shape=[
             jax.ShapeDtypeStruct((length, count * HD), jnp.float32),
@@ -319,7 +321,7 @@
         compiler_params=pltpu.CompilerParams(vmem_limit_bytes=VMEM_LIMIT),
         cost_estimate=SMALL_COST,
         name="partial_heads",
-    )(grad, grad_core, *weights)
+    )(grad, *weights)
 
 
 def columns_kernel(start, stop, starts, wide_ref, outs_ref, outs_x_ref, *refs):
@@ -339,7 +341,7 @@
             out_ref[low - start : high - start, columns] = total.astype(out_ref.dtype)
 
 
-def columns_sum(wide, outs, outs_x, arrived, start, stop, kind):
+def columns_sum(wide, outs, outs_x, arrived, start, stop, kind, cost=SMALL_COST):
     rows = outs.shape[0]
     arrived = [(p, first) for p, first in arrived if first < stop and start < first + p.shape[0]]
     if start % 16 or stop % 16:
@@ -355,7 +357,7 @@
         out_specs=whole(1)[0],
         out_shape=jax.ShapeDtypeStruct((stop - start, rows), kind),
         compiler_params=pltpu.CompilerParams(vmem_limit_bytes=VMEM_LIMIT),
-        cost_estimate=SMALL_COST,
+        cost_estimate=cost,
         name="columns_sum",
     )(wide, outs, outs_x, *[piece for piece, _ in arrived])
 
@@ -480,10 +482,12 @@
     rest += [(k, firsts[part], counts[part]) for part in range(1, len(counts)) for k in others]
     rest = pick_columns(after(pos, turned, mask), own, local_heads, rest)
     own_heads, rest = rest[: len(counts)], rest[len(counts) :]
+    held = after(jnp.stack([turned, grad_x]), *received[0], *own_heads)
+    pieces = [held] + [swap_with(held, "seq", k) for k in others]
     for part in range(1, len(counts)):
         sent = rest[(part - 1) * len(others) : part * len(others)]
         received.append(
-            [swap_with(after(sent[k - 1], grad_x, *received[part - 1]), "seq", k) for k in others]
+            [swap_with(after(sent[k - 1], *pieces[1:]), "seq", k) for k in others]
         )
 
     def swap_core(part, layer, *earlier):
@@ -496,18 +500,21 @@
         swap_core(part, 0)
     own_core = [each[0] for each in core_shards]
     outs_all, probs_all, outs_x = [], [], []
-    for part, count in enumerate(counts):
+
+    def forward(part, *earlier):
         outs, probs = attend_forward(
             pos,
             mask,
-            [after(own_heads[part], *own_core)] + list(received[part]),
+            [after(own_heads[part], own_core[part], *earlier)] + list(received[part]),
             firsts[part],
-            count,
+            counts[part],
             local_heads,
         )
         outs_all.append(outs)
         probs_all.append(probs)
         outs_x.append(swap_with(outs, "dp", 2))
+
+    forward(0)
     for layer in bits:
         swap_core(0, layer, outs_all[0])
     near = [core_shards[0][layer] for layer in bits]
@@ -530,85 +537,82 @@
             return [jnp.concatenate([shard[:, rows] for shard in shards] + core, axis=0)]
         return shards + core
 
-    def gather_tokens(dc, *earlier):
-        held = after(jnp.stack([turned[dc], grad_x[dc]]), *earlier)
-        return [held] + [swap_with(held, "seq", k) for k in others]
-
-    core_pieces = gather_tokens(1, *received[-1], *near)
-    pieces = gather_tokens(0, *received[-1])
-
-    core_pieces[1:] = [after(piece, outs_all[-1]) for piece in core_pieces[1:]]
-    core_wide, core_turned = join_pieces(core_pieces)
+    pieces[1:] = [after(piece, *near) for piece in pieces[1:]]
+    grad_wide, grad_turned = join_pieces(pieces)
     arrived = [[] for _ in counts]
-    quarter = class_cols // 4
+    half = class_cols // 2
 
     def send_core(part, start, stop, *earlier):
         sent = columns_sum(
-            after(core_wide, *earlier) if earlier else core_wide,
+            after(grad_wide, *earlier) if earlier else grad_wide,
             outs_all[part],
             outs_x[part],
             [],
-            start * quarter,
-            stop * quarter,
+            class_cols + start,
+            class_cols + stop,
             jnp.bfloat16,
         )
-        arrived[part].append((swap_with(sent, "dp", 1), start * quarter))
-
-    send_core(0, 3, 4)
-    send_core(0, 2, 3)
-    for part in range(1, len(counts)):
-        send_core(part, 2, 4)
-
-    pieces[1:] = [after(piece, *shards) for piece in pieces[1:]]
-    grad_wide, grad_turned = join_pieces(pieces)
-
-    def columns_of(part, start, stop, kind, *earlier):
+        arrived[part].append((swap_with(sent, "dp", 1), start))
+
+    for start in range(half, class_cols, half // 2):
+        send_core(0, start, start + half // 2)
+
+    def columns_of(part, start, stop, kind, *earlier, cost=SMALL_COST):
         outs = after(outs_all[part], *earlier) if earlier else outs_all[part]
-        return columns_sum(grad_wide, outs, outs_x[part], arrived[part], start, stop, kind)
-
-    kept, got, last = [], [], []
+        return columns_sum(grad_wide, outs, outs_x[part], arrived[part], start, stop, kind, cost)
+
+    kept, got, layer_got, last = [], [], [], []
     for part, count in enumerate(counts):
-        sent = columns_of(part, quarter * 2, quarter * 4, jnp.bfloat16, *last)
-        arrived[part].append((swap_with(sent, "dp", GROUP), 0))
+        if part == 0:
+            arrived[0][0] = (after(arrived[0][0][0], *shards, *received[-1]), arrived[0][0][1])
+        upper = columns_of(part, half, class_cols, jnp.bfloat16, *last, *layer_got)
+        layer_got.append(swap_with(upper, "dp", GROUP))
+        arrived[part].append((layer_got[part], 0))
         total, sent = partial_heads(
-            weights_of(part), after(grad_turned, sent), core_turned, firsts[part], count
+            weights_of(part), after(grad_turned, upper), firsts[part], count
         )
         kept.append(total)
         got.append(swap_with(sent, "dp", 2))
         last = [total]
-        send_core(part, 0, 2, total)
+        send_core(part, 0, half, total)
+        if part + 1 < len(counts):
+            forward(part + 1, total)
+            send_core(part + 1, half, class_cols, total)
 
     weight_parts, back_parts = [], []
     for part, count in enumerate(counts):
-        size = class_cols // 2
-
         def next_sums(last):
-            size = class_cols // 2
+            size = half
             for bit in [1 << power for power in range(1, layers.bit_length() - 1)]:
                 size //= 2
-                sent = columns_of(part, size, 2 * size, jnp.bfloat16, *last)
+                sent = columns_of(part, size, 2 * size, jnp.bfloat16, *last, cost=LAST_COST)
                 arrived[part].append((swap_with(sent, "dp", bit * GROUP), 0))
                 last = [sent]
             return last
 
         if part == 0:
-            last = next_sums(last)
+            last = next_sums([])
+        else:
+            last = last + [layer_got[part]]
         backs = attend_backward(
             [own_heads[part]] + list(received[part]),
             probs_all[part],
             after(kept[part], *last),
             got[part],
             count,
+            SMALL_COST if part else FIRST_COST,
         )
         last = [backs[0]]
         back_parts.append(backs[0])
         back_parts += [swap_with(backs[k], "seq", k) for k in others]
         if part:
             last = next_sums(last + [arrived[0][-1][0]])
+    back_parts[-1] = after(back_parts[-1], *last)
+    grad_queries, grad_keys = assemble(pos, back_parts, local_heads, firsts)
     for part in range(len(counts)):
         final, _ = arrived[part].pop()
-        weight_parts.append((columns_of(part, 0, cols, jnp.float32, *last), final))
-    grad_queries, grad_keys = assemble(pos, back_parts, local_heads, firsts)
+        base = columns_of(part, 0, cols, jnp.float32, *last)
+        weight_parts.append((base, after(final, grad_queries)))
     return (grad_queries, grad_keys, add_parts(weight_parts).T)
 
 

time: 104 us -> 101 us (0.971)
  local copies, waits for them, and re-layouts: 8.18 us -> 5.5 us
    unnamed x28, local copies, waits for them, and re-layouts: 7.22 us -> 4.53 us
    ppermute x31 -> x30, starting transfers between devices: 29.5 us -> 28.5 us  [swap_with(): lax.ppermute(array_in, axis_name, [(i, i ^ distance) for i in range(size)])]
    ppermute x31 -> x30, waiting for transfers between devices: 39.2 us -> 39.8 us  [swap_with(): lax.ppermute(array_in, axis_name, [(i, i ^ distance) for i in range(size)])]
  transfers between devices with their start and end apart: 31 -> 30, of which waited for: 10 -> 12; matrix products, arithmetic and copies ran while one was open for 1% -> 1% of each run, Pallas kernels for 21% -> 23%
where the time goes in v4:
time: 101 us
  waiting for transfers between devices  39.8 us (39%)
  starting transfers between devices  28.5 us (28%)
  Pallas kernels  25.8 us (26%)
  local copies, waits for them, and re-layouts  5.5 us (5%)
  between operations  1.04 us (1%)
    ppermute x30, waiting for transfers between devices, swap_with(): lax.ppermute(array_in, axis_name, [(i, i ^ distance) for i in range(size)])  39.8 us
    ppermute x30, starting transfers between devices, swap_with(): lax.ppermute(array_in, axis_name, [(i, i ^ distance) for i in range(size)])  28.5 us
    pallas_call x2, Pallas kernels, attend_forward(): pl.pallas_call(functools.partial(forward_kernel, first, count, local_head...  6.34 us
    pallas_call x11, Pallas kernels, columns_sum(): pl.pallas_call(functools.partial(columns_kernel, start, stop, [first for...  5.07 us
    pallas_call x2, Pallas kernels, attend_backward(): pl.pallas_call(functools.partial(backward_kernel, count, len(pieces)), in...  5.03 us
    unnamed x28, local copies, waits for them, and re-layouts  4.53 us
    pallas_call x2, Pallas kernels, partial_heads(): pl.pallas_call(functools.partial(partial_kernel, first), in_specs=whole(1...  2.35 us
    pallas_call x1, Pallas kernels, collect_columns(): pl.pallas_call(functools.partial(collect_kernel, local_heads, pieces), in...  2.07 us
  transfers between devices with their start and end apart: 30, of which 12 were waited for; matrix products, arithmetic and copies ran while one was open for 1% of the time, Pallas kernels for 23%

profile of v4, /device:TPU:0, one launch (start us, length us, event | category | flops | bytes accessed | tf_op | source)
XLA Modules:
  0.0 100.7 jit_solution(16463157689929312256)
XLA Ops:
  0.7 2.1 %collect_columns.1 = bf16[3,128,1024]{2,1,0:T(8,128)(2,1)} custom-call(s32[1]{0:T(128)} %bitcast.pos_ref, bf16[128,3072]{1,0:T(8,128)(2,1)} %refs_0_.3, bf16[128,3072]{1,0:T(8,128)(2,1)} %refs_1_.3, bf16[128,3072]{1,0:T(8,128)(2,1)} %refs_2_.3), custom_call_target="tpu_custom_call" | custom-call | tf_op jit(solution)/shard_map/collect_columns/pallas_call | solution.py:219
  2.8 3.0 %collective-permute-start = (bf16[3,128,1024]{2,1,0:T(8,128)(2,1)}, bf16[3,128,1024]{2,1,0:T(8,128)(2,1)}, u32[]{:S(2)}, u32[]{:S(2)}) collective-permute-start(bf16[3,128,1024]{2,1,0:T(8,128)(2,1)} %collect_columns.1), channel_id=1, source_target_pairs={{0,1},{1,0},{2,3},{3,2},{4,5},{5,4},{6,7},{7,6},{8,9},{9,8},{10,11... | collective-permute-start | bytes 2359304 | tf_op jit(solution)/shard_map/ppermute | solution.py:431
  8.0 1.6 %collective-permute-start.2 = (bf16[1280,128]{1,0:T(8,128)(2,1)S(1)}, bf16[1280,128]{1,0:T(8,128)(2,1)S(1)}, u32[]{:S(2)}, u32[]{:S(2)}) collective-permute-start(bf16[1280,128]{1,0:T(8,128)(2,1)S(1)} %get-tuple-element.55), channel_id=1, source_target_pairs={{0,4},{2,6},{4,0},{6,2},{8,12},{10,14},{12,8},{14,10},{16,20},{18,... | collective-permute-start | bytes 983048 | tf_op jit(solution)/shard_map/ppermute | solution.py:431
  9.5 2.6 %collective-permute-start.4 = (bf16[160,1536]{1,0:T(8,128)(2,1)S(1)}, bf16[160,1536]{1,0:T(8,128)(2,1)S(1)}, u32[]{:S(2)}, u32[]{:S(2)}) collective-permute-start(bf16[160,1536]{1,0:T(8,128)(2,1)S(1)} %bitcast.6), channel_id=1, source_target_pairs={{0,16},{2,18},{4,20},{6,22},{8,24},{10,26},{12,28},{14,30},{16,0},... | collective-permute-start | bytes 1474568 | tf_op jit(solution)/shard_map/ppermute | solution.py:431
  12.1 1.6 %collective-permute-start.6 = (bf16[160,1536]{1,0:T(8,128)(2,1)S(1)}, bf16[160,1536]{1,0:T(8,128)(2,1)S(1)}, u32[]{:S(2)}, u32[]{:S(2)}) collective-permute-start(bf16[160,1536]{1,0:T(8,128)(2,1)S(1)} %bitcast.7), channel_id=1, source_target_pairs={{0,8},{2,10},{4,12},{6,14},{8,0},{10,2},{12,4},{14,6},{16,24},{18,... | collective-permute-start | bytes 1474568 | tf_op jit(solution)/shard_map/ppermute | solution.py:431
  14.5 1.1 %copy-done.2 = bf16[128,3072]{1,0:T(8,128)(2,1)S(1)} copy-done((bf16[128,3072]{1,0:T(8,128)(2,1)S(1)}, bf16[128,3072]{1,0:T(8,128)(2,1)}, u32[]{:S(2)}) %copy-start.2) | copy-done | bytes 786456
  15.6 1.1 %copy-done.3 = bf16[128,3072]{1,0:T(8,128)(2,1)S(1)} copy-done((bf16[128,3072]{1,0:T(8,128)(2,1)S(1)}, bf16[128,3072]{1,0:T(8,128)(2,1)}, u32[]{:S(2)}) %copy-start.3) | copy-done | bytes 786456
  17.3 6.4 %collective-permute-done.refs_1_ = bf16[3,128,1024]{2,1,0:T(8,128)(2,1)} collective-permute-done((bf16[3,128,1024]{2,1,0:T(8,128)(2,1)}, bf16[3,128,1024]{2,1,0:T(8,128)(2,1)}, u32[]{:S(2)}, u32[]{:S(2)}) %collective-permute-start) | collective-permute-done | bytes 786464 | tf_op jit(solution)/shard_map/ppermute | solution.py:431
  23.7 1.7 %collective-permute-start.3 = (bf16[2,1280,128]{2,1,0:T(8,128)(2,1)S(1)}, bf16[2,1280,128]{2,1,0:T(8,128)(2,1)}, u32[]{:S(2)}, u32[]{:S(2)}) collective-permute-start(bf16[2,1280,128]{2,1,0:T(8,128)(2,1)S(1)} %pad_maximum_fusion.refs_0_), channel_id=1, source_target_pairs={{0,1},{1,0},{2,3},{3,2},{4,5},{5,4},{6,7},{7,6},{8,9},{9,8},{10,11... | collective-permute-start | bytes 1966088 | tf_op jit(solution)/shard_map/ppermute | solution.py:431
  25.5 1.1 %copy-done.5 = bf16[3,128,1024]{2,1,0:T(8,128)(2,1)S(1)} copy-done((bf16[3,128,1024]{2,1,0:T(8,128)(2,1)S(1)}, bf16[3,128,1024]{2,1,0:T(8,128)(2,1)}, u32[]{:S(2)}) %copy-start.5) | copy-done | bytes 786456
  26.6 4.1 %attend_forward.2 = (bf16[1024,256]{1,0:T(8,128)(2,1)S(1)}, f32[8,256,256]{2,1,0:T(8,128)S(1)}) custom-call(s32[1]{0:T(128)} %bitcast.pos_ref, s32[24,4]{1,0:T(8,128)S(1)} %copy.10.mask_ref, bf16[3,128,1024]{2,1,0:T(8,128)(2,1)S(1)} %copy-done.5, bf16[3,128,1024]{2,1,0:T(8,128)(2,1)} %collective-permute-done.refs_1_), custom_call_target="tpu_custom_call" | custom-call | tf_op jit(solution)/shard_map/attend_forward/pallas_call | solution.py:146
  30.7 1.6 %collective-permute-start.8 = (bf16[1024,256]{1,0:T(8,128)(2,1)S(1)}, bf16[1024,256]{1,0:T(8,128)(2,1)S(1)}, u32[]{:S(2)}, u32[]{:S(2)}) collective-permute-start(bf16[1024,256]{1,0:T(8,128)(2,1)S(1)} %get-tuple-element.89.outs_ref), channel_id=1, source_target_pairs={{0,4},{2,6},{4,0},{6,2},{8,12},{10,14},{12,8},{14,10},{16,20},{18,... | collective-permute-start | bytes 1572872 | tf_op jit(solution)/shard_map/ppermute | solution.py:431
  32.3 1.1 %collective-permute-done.4.refs_1_ = bf16[160,1536]{1,0:T(8,128)(2,1)S(1)} collective-permute-done((bf16[160,1536]{1,0:T(8,128)(2,1)S(1)}, bf16[160,1536]{1,0:T(8,128)(2,1)S(1)}, u32[]{:S(2)}, u32[]{:S(2)}) %collective-permute-start.4) | collective-permute-done | bytes 491552 | tf_op jit(solution)/shard_map/ppermute | solution.py:431
  34.7 4.9 %collective-permute-done.3.refs_1_ = bf16[2,1280,128]{2,1,0:T(8,128)(2,1)} collective-permute-done((bf16[2,1280,128]{2,1,0:T(8,128)(2,1)S(1)}, bf16[2,1280,128]{2,1,0:T(8,128)(2,1)}, u32[]{:S(2)}, u32[]{:S(2)}) %collective-permute-start.3) | collective-permute-done | bytes 655392 | tf_op jit(solution)/shard_map/ppermute | solution.py:431
  39.7 1.4 %collective-permute-start.11 = (bf16[3,128,512]{2,1,0:T(8,128)(2,1)S(1)}, bf16[3,128,512]{2,1,0:T(8,128)(2,1)S(1)}, u32[]{:S(2)}, u32[]{:S(2)}) collective-permute-start(bf16[3,128,512]{2,1,0:T(8,128)(2,1)S(1)} %copy-done.11), channel_id=1, source_target_pairs={{0,1},{1,0},{2,3},{3,2},{4,5},{5,4},{6,7},{7,6},{8,9},{9,8},{10,11... | collective-permute-start | bytes 1179656 | tf_op jit(solution)/shard_map/ppermute | solution.py:431
  41.1 1.5 %join_pieces.1 = (bf16[1280,512]{1,0:T(8,128)(2,1)S(1)}, bf16[512,1280]{1,0:T(8,128)(2,1)S(1)}) custom-call(bf16[2,1280,128]{2,1,0:T(8,128)(2,1)S(1)} %pad_maximum_fusion.refs_0_, bf16[2,1280,128]{2,1,0:T(8,128)(2,1)} %collective-permute-done.3.refs_1_), custom_call_target="tpu_custom_call" | custom-call | tf_op jit(solution)/shard_map/join_pieces/pallas_call | solution.py:280
  46.2 2.9 %collective-permute-done.11.refs_1_ = bf16[3,128,512]{2,1,0:T(8,128)(2,1)S(1)} collective-permute-done((bf16[3,128,512]{2,1,0:T(8,128)(2,1)S(1)}, bf16[3,128,512]{2,1,0:T(8,128)(2,1)S(1)}, u32[]{:S(2)}, u32[]{:S(2)}) %collective-permute-start.11) | collective-permute-done | bytes 393248 | tf_op jit(solution)/shard_map/ppermute | solution.py:431
  49.9 1.2 %collective-permute-start.14 = (bf16[320,1024]{1,0:T(8,128)(2,1)S(1)}, bf16[320,1024]{1,0:T(8,128)(2,1)S(1)}, u32[]{:S(2)}, u32[]{:S(2)}) collective-permute-start(bf16[320,1024]{1,0:T(8,128)(2,1)S(1)} %columns_sum.13), channel_id=1, source_target_pairs={{0,8},{2,10},{4,12},{6,14},{8,0},{10,2},{12,4},{14,6},{16,24},{18,... | collective-permute-start | bytes 1966088 | tf_op jit(solution)/shard_map/ppermute | solution.py:431
  51.1 1.5 %partial_heads.2 = (f32[256,1024]{1,0:T(8,128)S(1)}, bf16[256,1024]{1,0:T(8,128)(2,1)S(1)}) custom-call(bf16[512,1280]{1,0:T(8,128)(2,1)S(1)} %get-tuple-element.78.grad_ref, bf16[160,1536]{1,0:T(8,128)(2,1)S(1)} %bitcast.10, bf16[160,1536]{1,0:T(8,128)(2,1)S(1)} %collective-permute-done.4.refs_1_, bf16[160,1536]{1,0:T(8,128)(2,1)S(1)} %collective-permute-done.6.refs_2_, ...), custom_call_target="tpu_custom_call" | custom-call | tf_op jit(solution)/shard_map/partial_heads/pallas_call | solution.py:313
  53.3 2.2 %attend_forward.3 = (bf16[512,256]{1,0:T(8,128)(2,1)S(1)}, f32[4,256,256]{2,1,0:T(8,128)S(1)}) custom-call(s32[1]{0:T(128)} %bitcast.pos_ref, s32[24,4]{1,0:T(8,128)S(1)} %copy.10.mask_ref, bf16[3,128,512]{2,1,0:T(8,128)(2,1)S(1)} %get-tuple-element.74.refs_0_, bf16[3,128,512]{2,1,0:T(8,128)(2,1)S(1)} %collective-permute-done.11.refs_1_), custom_call_target="tpu_custom_call" | custom-call | tf_op jit(solution)/shard_map/attend_forward/pallas_call | solution.py:146
  55.5 1.6 %collective-permute-start.19 = (bf16[512,256]{1,0:T(8,128)(2,1)S(1)}, bf16[512,256]{1,0:T(8,128)(2,1)S(1)}, u32[]{:S(2)}, u32[]{:S(2)}) collective-permute-start(bf16[512,256]{1,0:T(8,128)(2,1)S(1)} %get-tuple-element.91.outs_ref), channel_id=1, source_target_pairs={{0,4},{2,6},{4,0},{6,2},{8,12},{10,14},{12,8},{14,10},{16,20},{18,... | collective-permute-start | bytes 786440 | tf_op jit(solution)/shard_map/ppermute | solution.py:431
  57.6 7.1 %collective-permute-done.19.outs_x_ref = bf16[512,256]{1,0:T(8,128)(2,1)S(1)} collective-permute-done((bf16[512,256]{1,0:T(8,128)(2,1)S(1)}, bf16[512,256]{1,0:T(8,128)(2,1)S(1)}, u32[]{:S(2)}, u32[]{:S(2)}) %collective-permute-start.19) | collective-permute-done | bytes 262176 | tf_op jit(solution)/shard_map/ppermute | solution.py:431
  69.1 2.3 %collective-permute-start.27 = (bf16[160,1024]{1,0:T(8,128)(2,1)S(1)}, bf16[160,1024]{1,0:T(8,128)(2,1)S(1)}, u32[]{:S(2)}, u32[]{:S(2)}) collective-permute-start(bf16[160,1024]{1,0:T(8,128)(2,1)S(1)} %columns_sum.15), channel_id=1, source_target_pairs={{0,16},{2,18},{4,20},{6,22},{8,24},{10,26},{12,28},{14,30},{16,0},... | collective-permute-start | bytes 983048 | tf_op jit(solution)/shard_map/ppermute | solution.py:431
  72.2 1.5 %collective-permute-start.25 = (bf16[256,512]{1,0:T(8,128)(2,1)S(1)}, bf16[256,512]{1,0:T(8,128)(2,1)S(1)}, u32[]{:S(2)}, u32[]{:S(2)}) collective-permute-start(bf16[256,512]{1,0:T(8,128)(2,1)S(1)} %get-tuple-element.81), channel_id=1, source_target_pairs={{0,4},{2,6},{4,0},{6,2},{8,12},{10,14},{12,8},{14,10},{16,20},{18,... | collective-permute-start | bytes 786440 | tf_op jit(solution)/shard_map/ppermute | solution.py:431
  74.2 1.7 %collective-permute-done.16.refs_4_ = bf16[256,1024]{1,0:T(8,128)(2,1)S(1)} collective-permute-done((bf16[256,1024]{1,0:T(8,128)(2,1)S(1)}, bf16[256,1024]{1,0:T(8,128)(2,1)S(1)}, u32[]{:S(2)}, u32[]{:S(2)}) %collective-permute-start.16) | collective-permute-done | bytes 524320 | tf_op jit(solution)/shard_map/ppermute | solution.py:431
  75.9 3.7 %attend_backward.2 = (bf16[2,128,1024]{2,1,0:T(8,128)(2,1)S(1)}, bf16[2,128,1024]{2,1,0:T(8,128)(2,1)S(1)}) custom-call(bf16[3,128,1024]{2,1,0:T(8,128)(2,1)S(1)} %copy-done.6, bf16[3,128,1024]{2,1,0:T(8,128)(2,1)} %collective-permute-done.refs_1_, f32[8,256,256]{2,1,0:T(8,128)S(1)} %get-tuple-element.54.refs_2_, f32[256,1024]{1,0:T(8,128)S(1)} %get-tuple-element.70.refs_3_, ...), custom_call_target="tpu_custom_call" | custom-call | flops 3500000000 | tf_op jit(solution)/shard_map/attend_backward/pallas_call | solution.py:162
  79.6 1.6 %collective-permute-start.17 = (bf16[2,128,1024]{2,1,0:T(8,128)(2,1)S(1)}, bf16[2,128,1024]{2,1,0:T(8,128)(2,1)S(1)}, u32[]{:S(2)}, u32[]{:S(2)}) collective-permute-start(bf16[2,128,1024]{2,1,0:T(8,128)(2,1)S(1)} %get-tuple-element.73), channel_id=1, source_target_pairs={{0,1},{1,0},{2,3},{3,2},{4,5},{5,4},{6,7},{7,6},{8,9},{9,8},{10,11... | collective-permute-start | bytes 1572872 | tf_op jit(solution)/shard_map/ppermute | solution.py:431
  81.2 3.3 %collective-permute-done.24.refs_0_ = bf16[320,512]{1,0:T(8,128)(2,1)S(1)} collective-permute-done((bf16[320,512]{1,0:T(8,128)(2,1)S(1)}, bf16[320,512]{1,0:T(8,128)(2,1)S(1)}, u32[]{:S(2)}, u32[]{:S(2)}) %collective-permute-start.24) | collective-permute-done | bytes 327712 | tf_op jit(solution)/shard_map/ppermute | solution.py:431
  84.5 1.3 %attend_backward.3 = (bf16[2,128,512]{2,1,0:T(8,128)(2,1)S(1)}, bf16[2,128,512]{2,1,0:T(8,128)(2,1)S(1)}) custom-call(bf16[3,128,512]{2,1,0:T(8,128)(2,1)S(1)} %get-tuple-element.74.refs_0_, bf16[3,128,512]{2,1,0:T(8,128)(2,1)S(1)} %collective-permute-done.11.refs_1_, f32[4,256,256]{2,1,0:T(8,128)S(1)} %get-tuple-element.75.refs_2_, ...), custom_call_target="tpu_custom_call" | custom-call | tf_op jit(solution)/shard_map/attend_backward/pallas_call | solution.py:162
  85.8 1.6 %collective-permute-start.26 = (bf16[2,128,512]{2,1,0:T(8,128)(2,1)S(1)}, bf16[2,128,512]{2,1,0:T(8,128)(2,1)S(1)}, u32[]{:S(2)}, u32[]{:S(2)}) collective-permute-start(bf16[2,128,512]{2,1,0:T(8,128)(2,1)S(1)} %get-tuple-element.83), channel_id=1, source_target_pairs={{0,1},{1,0},{2,3},{3,2},{4,5},{5,4},{6,7},{7,6},{8,9},{9,8},{10,11... | collective-permute-start | bytes 786440 | tf_op jit(solution)/shard_map/ppermute | solution.py:431
  88.6 9.8 %collective-permute-done.26.refs_3_ = bf16[2,128,512]{2,1,0:T(8,128)(2,1)S(1)} collective-permute-done((bf16[2,128,512]{2,1,0:T(8,128)(2,1)S(1)}, bf16[2,128,512]{2,1,0:T(8,128)(2,1)S(1)}, u32[]{:S(2)}, u32[]{:S(2)}) %collective-permute-start.26) | collective-permute-done | bytes 262176 | tf_op jit(solution)/shard_map/ppermute | solution.py:431
  98.4 1.2 %assemble.1 = (bf16[128,3072]{1,0:T(8,128)(2,1)}, bf16[128,3072]{1,0:T(8,128)(2,1)}) custom-call(s32[1]{0:T(128)} %bitcast.pos_ref, bf16[2,128,1024]{2,1,0:T(8,128)(2,1)S(1)} %get-tuple-element.72.refs_0_, bf16[2,128,1024]{2,1,0:T(8,128)(2,1)S(1)} %collective-permute-done.17.refs_1_, bf16[2,128,512]{2,1,0:T(8,128)(2,1)S(1)} %get-tuple-element.82.refs_2_, ...), custom_call_target="tpu_custom_call" | custom-call | tf_op jit(solution)/shard_map/assemble/pallas_call | solution.py:387
  (90 shorter events, 18.1 us)
Async XLA Ops:
  0.6 13.8 %copy-start.12 = (s32[24,4,4]{0,2,1:T(4,128)S(1)}, s32[24,4,4]{0,2,1:T(4,128)}, u32[]{:S(2)}) copy-start(s32[24,4,4]{0,2,1:T(4,128)} %param.12) | copy-start | bytes 4612
  0.7 13.8 %copy-start.13 = (s32[24,4]{0,1:T(4,128)S(1)}, s32[24,4]{0,1:T(4,128)}, u32[]{:S(2)}) copy-start(s32[24,4]{0,1:T(4,128)} %param.13) | copy-start | bytes 1156
  2.8 20.9 %collective-permute-start = (bf16[3,128,1024]{2,1,0:T(8,128)(2,1)}, bf16[3,128,1024]{2,1,0:T(8,128)(2,1)}, u32[]{:S(2)}, u32[]{:S(2)}) collective-permute-start(bf16[3,128,1024]{2,1,0:T(8,128)(2,1)} %collect_columns.1), channel_id=1, source_target_pairs={{0,1},{1,0},{2,3},{3,2},{4,5},{5,4},{6,7},{7,6},{8,9},{9,8},{10,11... | collective-permute-start | bytes 2359304 | tf_op jit(solution)/shard_map/ppermute | solution.py:431
  8.0 9.2 %collective-permute-start.2 = (bf16[1280,128]{1,0:T(8,128)(2,1)S(1)}, bf16[1280,128]{1,0:T(8,128)(2,1)S(1)}, u32[]{:S(2)}, u32[]{:S(2)}) collective-permute-start(bf16[1280,128]{1,0:T(8,128)(2,1)S(1)} %get-tuple-element.55), channel_id=1, source_target_pairs={{0,4},{2,6},{4,0},{6,2},{8,12},{10,14},{12,8},{14,10},{16,20},{18,... | collective-permute-start | bytes 983048 | tf_op jit(solution)/shard_map/ppermute | solution.py:431
  9.5 23.9 %collective-permute-start.4 = (bf16[160,1536]{1,0:T(8,128)(2,1)S(1)}, bf16[160,1536]{1,0:T(8,128)(2,1)S(1)}, u32[]{:S(2)}, u32[]{:S(2)}) collective-permute-start(bf16[160,1536]{1,0:T(8,128)(2,1)S(1)} %bitcast.6), channel_id=1, source_target_pairs={{0,16},{2,18},{4,20},{6,22},{8,24},{10,26},{12,28},{14,30},{16,0},... | collective-permute-start | bytes 1474568 | tf_op jit(solution)/shard_map/ppermute | solution.py:431
  12.1 22.0 %collective-permute-start.6 = (bf16[160,1536]{1,0:T(8,128)(2,1)S(1)}, bf16[160,1536]{1,0:T(8,128)(2,1)S(1)}, u32[]{:S(2)}, u32[]{:S(2)}) collective-permute-start(bf16[160,1536]{1,0:T(8,128)(2,1)S(1)} %bitcast.7), channel_id=1, source_target_pairs={{0,8},{2,10},{4,12},{6,14},{8,0},{10,2},{12,4},{14,6},{16,24},{18,... | collective-permute-start | bytes 1474568 | tf_op jit(solution)/shard_map/ppermute | solution.py:431
  14.4 11.0 %collective-permute-start.1 = (bf16[160,1024]{1,0:T(8,128)(2,1)}, bf16[160,1024]{1,0:T(8,128)(2,1)S(1)}, u32[]{:S(2)}, u32[]{:S(2)}) collective-permute-start(bf16[160,1024]{1,0:T(8,128)(2,1)} %slice.32), channel_id=1, source_target_pairs={{0,2},{2,0},{4,6},{6,4},{8,10},{10,8},{12,14},{14,12},{16,18},{18,... | collective-permute-start | bytes 983048 | tf_op jit(solution)/shard_map/ppermute | solution.py:431
  23.7 16.0 %collective-permute-start.3 = (bf16[2,1280,128]{2,1,0:T(8,128)(2,1)S(1)}, bf16[2,1280,128]{2,1,0:T(8,128)(2,1)}, u32[]{:S(2)}, u32[]{:S(2)}) collective-permute-start(bf16[2,1280,128]{2,1,0:T(8,128)(2,1)S(1)} %pad_maximum_fusion.refs_0_), channel_id=1, source_target_pairs={{0,1},{1,0},{2,3},{3,2},{4,5},{5,4},{6,7},{7,6},{8,9},{9,8},{10,11... | collective-permute-start | bytes 1966088 | tf_op jit(solution)/shard_map/ppermute | solution.py:431
  30.7 12.6 %collective-permute-start.8 = (bf16[1024,256]{1,0:T(8,128)(2,1)S(1)}, bf16[1024,256]{1,0:T(8,128)(2,1)S(1)}, u32[]{:S(2)}, u32[]{:S(2)}) collective-permute-start(bf16[1024,256]{1,0:T(8,128)(2,1)S(1)} %get-tuple-element.89.outs_ref), channel_id=1, source_target_pairs={{0,4},{2,6},{4,0},{6,2},{8,12},{10,14},{12,8},{14,10},{16,20},{18,... | collective-permute-start | bytes 1572872 | tf_op jit(solution)/shard_map/ppermute | solution.py:431
  33.5 12.0 %collective-permute-start.10 = (bf16[160,1536]{1,0:T(8,128)(2,1)S(1)}, bf16[160,1536]{1,0:T(8,128)(2,1)S(1)}, u32[]{:S(2)}, u32[]{:S(2)}) collective-permute-start(bf16[160,1536]{1,0:T(8,128)(2,1)S(1)} %collective-permute-done.4.refs_1_), channel_id=1, source_target_pairs={{0,8},{2,10},{4,12},{6,14},{8,0},{10,2},{12,4},{14,6},{16,24},{18,... | collective-permute-start | bytes 1474568 | tf_op jit(solution)/shard_map/ppermute | solution.py:431
  34.1 7.1 %collective-permute-start.5 = (bf16[160,1024]{1,0:T(8,128)(2,1)S(1)}, bf16[160,1024]{1,0:T(8,128)(2,1)S(1)}, u32[]{:S(2)}, u32[]{:S(2)}) collective-permute-start(bf16[160,1024]{1,0:T(8,128)(2,1)S(1)} %slice.25), channel_id=1, source_target_pairs={{0,2},{2,0},{4,6},{6,4},{8,10},{10,8},{12,14},{14,12},{16,18},{18,... | collective-permute-start | bytes 983048 | tf_op jit(solution)/shard_map/ppermute | solution.py:431
  34.2 6.9 %collective-permute-start.7 = (bf16[160,1024]{1,0:T(8,128)(2,1)S(1)}, bf16[160,1024]{1,0:T(8,128)(2,1)S(1)}, u32[]{:S(2)}, u32[]{:S(2)}) collective-permute-start(bf16[160,1024]{1,0:T(8,128)(2,1)S(1)} %slice.26), channel_id=1, source_target_pairs={{0,2},{2,0},{4,6},{6,4},{8,10},{10,8},{12,14},{14,12},{16,18},{18,... | collective-permute-start | bytes 983048 | tf_op jit(solution)/shard_map/ppermute | solution.py:431
  39.7 9.4 %collective-permute-start.11 = (bf16[3,128,512]{2,1,0:T(8,128)(2,1)S(1)}, bf16[3,128,512]{2,1,0:T(8,128)(2,1)S(1)}, u32[]{:S(2)}, u32[]{:S(2)}) collective-permute-start(bf16[3,128,512]{2,1,0:T(8,128)(2,1)S(1)} %copy-done.11), channel_id=1, source_target_pairs={{0,1},{1,0},{2,3},{3,2},{4,5},{5,4},{6,7},{7,6},{8,9},{9,8},{10,11... | collective-permute-start | bytes 1179656 | tf_op jit(solution)/shard_map/ppermute | solution.py:431
  43.8 2.3 %collective-permute-start.9 = (bf16[160,1024]{1,0:T(8,128)(2,1)S(1)}, bf16[160,1024]{1,0:T(8,128)(2,1)S(1)}, u32[]{:S(2)}, u32[]{:S(2)}) collective-permute-start(bf16[160,1024]{1,0:T(8,128)(2,1)S(1)} %columns_sum.11), channel_id=1, source_target_pairs={{0,2},{2,0},{4,6},{6,4},{8,10},{10,8},{12,14},{14,12},{16,18},{18,... | collective-permute-start | bytes 983048 | tf_op jit(solution)/shard_map/ppermute | solution.py:431
  44.4 4.7 %collective-permute-start.12 = (bf16[160,1024]{1,0:T(8,128)(2,1)S(1)}, bf16[160,1024]{1,0:T(8,128)(2,1)S(1)}, u32[]{:S(2)}, u32[]{:S(2)}) collective-permute-start(bf16[160,1024]{1,0:T(8,128)(2,1)S(1)} %columns_sum.12), channel_id=1, source_target_pairs={{0,2},{2,0},{4,6},{6,4},{8,10},{10,8},{12,14},{14,12},{16,18},{18,... | collective-permute-start | bytes 983048 | tf_op jit(solution)/shard_map/ppermute | solution.py:431
  45.5 5.6 %collective-permute-start.13 = (bf16[160,1024]{1,0:T(8,128)(2,1)S(1)}, bf16[160,1024]{1,0:T(8,128)(2,1)S(1)}, u32[]{:S(2)}, u32[]{:S(2)}) collective-permute-start(bf16[160,1024]{1,0:T(8,128)(2,1)S(1)} %slice.33), channel_id=1, source_target_pairs={{0,2},{2,0},{4,6},{6,4},{8,10},{10,8},{12,14},{14,12},{16,18},{18,... | collective-permute-start | bytes 983048 | tf_op jit(solution)/shard_map/ppermute | solution.py:431
  45.6 7.7 %collective-permute-start.18 = (bf16[160,512]{1,0:T(8,128)(2,1)S(1)}, bf16[160,512]{1,0:T(8,128)(2,1)S(1)}, u32[]{:S(2)}, u32[]{:S(2)}) collective-permute-start(bf16[160,512]{1,0:T(8,128)(2,1)S(1)} %slice.34), channel_id=1, source_target_pairs={{0,2},{2,0},{4,6},{6,4},{8,10},{10,8},{12,14},{14,12},{16,18},{18,... | collective-permute-start | bytes 491528 | tf_op jit(solution)/shard_map/ppermute | solution.py:431
  49.9 17.0 %collective-permute-start.14 = (bf16[320,1024]{1,0:T(8,128)(2,1)S(1)}, bf16[320,1024]{1,0:T(8,128)(2,1)S(1)}, u32[]{:S(2)}, u32[]{:S(2)}) collective-permute-start(bf16[320,1024]{1,0:T(8,128)(2,1)S(1)} %columns_sum.13), channel_id=1, source_target_pairs={{0,8},{2,10},{4,12},{6,14},{8,0},{10,2},{12,4},{14,6},{16,24},{18,... | collective-permute-start | bytes 1966088 | tf_op jit(solution)/shard_map/ppermute | solution.py:431
  53.2 14.4 %collective-permute-start.15 = (bf16[320,1024]{1,0:T(8,128)(2,1)S(1)}, bf16[320,1024]{1,0:T(8,128)(2,1)S(1)}, u32[]{:S(2)}, u32[]{:S(2)}) collective-permute-start(bf16[320,1024]{1,0:T(8,128)(2,1)S(1)} %columns_sum.14), channel_id=1, source_target_pairs={{0,2},{2,0},{4,6},{6,4},{8,10},{10,8},{12,14},{14,12},{16,18},{18,... | collective-permute-start | bytes 1966088 | tf_op jit(solution)/shard_map/ppermute | solution.py:431
  55.5 9.2 %collective-permute-start.19 = (bf16[512,256]{1,0:T(8,128)(2,1)S(1)}, bf16[512,256]{1,0:T(8,128)(2,1)S(1)}, u32[]{:S(2)}, u32[]{:S(2)}) collective-permute-start(bf16[512,256]{1,0:T(8,128)(2,1)S(1)} %get-tuple-element.91.outs_ref), channel_id=1, source_target_pairs={{0,4},{2,6},{4,0},{6,2},{8,12},{10,14},{12,8},{14,10},{16,20},{18,... | collective-permute-start | bytes 786440 | tf_op jit(solution)/shard_map/ppermute | solution.py:431
  57.1 18.8 %collective-permute-start.16 = (bf16[256,1024]{1,0:T(8,128)(2,1)S(1)}, bf16[256,1024]{1,0:T(8,128)(2,1)S(1)}, u32[]{:S(2)}, u32[]{:S(2)}) collective-permute-start(bf16[256,1024]{1,0:T(8,128)(2,1)S(1)} %get-tuple-element.71), channel_id=1, source_target_pairs={{0,4},{2,6},{4,0},{6,2},{8,12},{10,14},{12,8},{14,10},{16,20},{18,... | collective-permute-start | bytes 1572872 | tf_op jit(solution)/shard_map/ppermute | solution.py:431
  65.0 1.7 %collective-permute-start.20 = (bf16[320,512]{1,0:T(8,128)(2,1)S(1)}, bf16[320,512]{1,0:T(8,128)(2,1)S(1)}, u32[]{:S(2)}, u32[]{:S(2)}) collective-permute-start(bf16[320,512]{1,0:T(8,128)(2,1)S(1)} %columns_sum.16), channel_id=1, source_target_pairs={{0,2},{2,0},{4,6},{6,4},{8,10},{10,8},{12,14},{14,12},{16,18},{18,... | collective-permute-start | bytes 983048 | tf_op jit(solution)/shard_map/ppermute | solution.py:431
  65.1 3.9 %collective-permute-start.21 = (bf16[160,512]{1,0:T(8,128)(2,1)S(1)}, bf16[160,512]{1,0:T(8,128)(2,1)S(1)}, u32[]{:S(2)}, u32[]{:S(2)}) collective-permute-start(bf16[160,512]{1,0:T(8,128)(2,1)S(1)} %slice.35), channel_id=1, source_target_pairs={{0,2},{2,0},{4,6},{6,4},{8,10},{10,8},{12,14},{14,12},{16,18},{18,... | collective-permute-start | bytes 491528 | tf_op jit(solution)/shard_map/ppermute | solution.py:431
  66.7 4.6 %collective-permute-start.22 = (bf16[160,512]{1,0:T(8,128)(2,1)S(1)}, bf16[160,512]{1,0:T(8,128)(2,1)S(1)}, u32[]{:S(2)}, u32[]{:S(2)}) collective-permute-start(bf16[160,512]{1,0:T(8,128)(2,1)S(1)} %slice.36), channel_id=1, source_target_pairs={{0,2},{2,0},{4,6},{6,4},{8,10},{10,8},{12,14},{14,12},{16,18},{18,... | collective-permute-start | bytes 491528 | tf_op jit(solution)/shard_map/ppermute | solution.py:431
  66.9 4.5 %collective-permute-start.23 = (bf16[160,512]{1,0:T(8,128)(2,1)S(1)}, bf16[160,512]{1,0:T(8,128)(2,1)S(1)}, u32[]{:S(2)}, u32[]{:S(2)}) collective-permute-start(bf16[160,512]{1,0:T(8,128)(2,1)S(1)} %slice.37), channel_id=1, source_target_pairs={{0,2},{2,0},{4,6},{6,4},{8,10},{10,8},{12,14},{14,12},{16,18},{18,... | collective-permute-start | bytes 491528 | tf_op jit(solution)/shard_map/ppermute | solution.py:431
  67.6 16.8 %collective-permute-start.24 = (bf16[320,512]{1,0:T(8,128)(2,1)S(1)}, bf16[320,512]{1,0:T(8,128)(2,1)S(1)}, u32[]{:S(2)}, u32[]{:S(2)}) collective-permute-start(bf16[320,512]{1,0:T(8,128)(2,1)S(1)} %columns_sum.17), channel_id=1, source_target_pairs={{0,8},{2,10},{4,12},{6,14},{8,0},{10,2},{12,4},{14,6},{16,24},{18,... | collective-permute-start | bytes 983048 | tf_op jit(solution)/shard_map/ppermute | solution.py:431
  69.1 18.3 %collective-permute-start.27 = (bf16[160,1024]{1,0:T(8,128)(2,1)S(1)}, bf16[160,1024]{1,0:T(8,128)(2,1)S(1)}, u32[]{:S(2)}, u32[]{:S(2)}) collective-permute-start(bf16[160,1024]{1,0:T(8,128)(2,1)S(1)} %columns_sum.15), channel_id=1, source_target_pairs={{0,16},{2,18},{4,20},{6,22},{8,24},{10,26},{12,28},{14,30},{16,0},... | collective-permute-start | bytes 983048 | tf_op jit(solution)/shard_map/ppermute | solution.py:431
  72.2 12.3 %collective-permute-start.25 = (bf16[256,512]{1,0:T(8,128)(2,1)S(1)}, bf16[256,512]{1,0:T(8,128)(2,1)S(1)}, u32[]{:S(2)}, u32[]{:S(2)}) collective-permute-start(bf16[256,512]{1,0:T(8,128)(2,1)S(1)} %get-tuple-element.81), channel_id=1, source_target_pairs={{0,4},{2,6},{4,0},{6,2},{8,12},{10,14},{12,8},{14,10},{16,20},{18,... | collective-permute-start | bytes 786440 | tf_op jit(solution)/shard_map/ppermute | solution.py:431
  74.1 13.3 %collective-permute-start.28 = (bf16[320,512]{1,0:T(8,128)(2,1)S(1)}, bf16[320,512]{1,0:T(8,128)(2,1)S(1)}, u32[]{:S(2)}, u32[]{:S(2)}) collective-permute-start(bf16[320,512]{1,0:T(8,128)(2,1)S(1)} %columns_sum.18), channel_id=1, source_target_pairs={{0,2},{2,0},{4,6},{6,4},{8,10},{10,8},{12,14},{14,12},{16,18},{18,... | collective-permute-start | bytes 983048 | tf_op jit(solution)/shard_map/ppermute | solution.py:431
  79.6 18.8 %collective-permute-start.17 = (bf16[2,128,1024]{2,1,0:T(8,128)(2,1)S(1)}, bf16[2,128,1024]{2,1,0:T(8,128)(2,1)S(1)}, u32[]{:S(2)}, u32[]{:S(2)}) collective-permute-start(bf16[2,128,1024]{2,1,0:T(8,128)(2,1)S(1)} %get-tuple-element.73), channel_id=1, source_target_pairs={{0,1},{1,0},{2,3},{3,2},{4,5},{5,4},{6,7},{7,6},{8,9},{9,8},{10,11... | collective-permute-start | bytes 1572872 | tf_op jit(solution)/shard_map/ppermute | solution.py:431
  85.8 12.6 %collective-permute-start.26 = (bf16[2,128,512]{2,1,0:T(8,128)(2,1)S(1)}, bf16[2,128,512]{2,1,0:T(8,128)(2,1)S(1)}, u32[]{:S(2)}, u32[]{:S(2)}) collective-permute-start(bf16[2,128,512]{2,1,0:T(8,128)(2,1)S(1)} %get-tuple-element.83), channel_id=1, source_target_pairs={{0,1},{1,0},{2,3},{3,2},{4,5},{5,4},{6,7},{7,6},{8,9},{9,8},{10,11... | collective-permute-start | bytes 786440 | tf_op jit(solution)/shard_map/ppermute | solution.py:431
  87.7 11.9 %collective-permute-start.29 = (bf16[160,512]{1,0:T(8,128)(2,1)S(1)}, bf16[160,512]{1,0:T(8,128)(2,1)S(1)}, u32[]{:S(2)}, u32[]{:S(2)}) collective-permute-start(bf16[160,512]{1,0:T(8,128)(2,1)S(1)} %columns_sum.19), channel_id=1, source_target_pairs={{0,16},{2,18},{4,20},{6,22},{8,24},{10,26},{12,28},{14,30},{16,0},... | collective-permute-start | bytes 491528 | tf_op jit(solution)/shard_map/ppermute | solution.py:431
  (12 other events, 66.7 us)

commit v5 on v4

--- a/solution.py
+++ b/solution.py
@@ -612,7 +612,7 @@
     for part in range(len(counts)):
         final, _ = arrived[part].pop()
         base = columns_of(part, 0, cols, jnp.float32, *last)
-        weight_parts.append((base, after(final, grad_queries)))
+        weight_parts.append((base, final))
     return (grad_queries, grad_keys, add_parts(weight_parts).T)
 
 

time: 101 us -> 100 us (0.990)
    ppermute x30, waiting for transfers between devices: 39.8 us -> 38.8 us  [swap_with(): lax.ppermute(array_in, axis_name, [(i, i ^ distance) for i in range(size)])]
  transfers between devices with their start and end apart: 30 -> 30, of which waited for: 12 -> 13; matrix products, arithmetic and copies ran while one was open for 1% -> 1% of each run, Pallas kernels for 23% -> 23%
where the time goes in v5:
time: 100 us; the launch traced here: 99.6 us
  waiting for transfers between devices  38.8 us (39%)
  starting transfers between devices  28.5 us (28%)
  Pallas kernels  25.8 us (26%)
  local copies, waits for them, and re-layouts  5.5 us (6%)
  between operations  1.02 us (1%)
    ppermute x30, waiting for transfers between devices, swap_with(): lax.ppermute(array_in, axis_name, [(i, i ^ distance) for i in range(size)])  38.8 us
    ppermute x30, starting transfers between devices, swap_with(): lax.ppermute(array_in, axis_name, [(i, i ^ distance) for i in range(size)])  28.5 us
    pallas_call x2, Pallas kernels, attend_forward(): pl.pallas_call(functools.partial(forward_kernel, first, count, local_head...  6.34 us
    pallas_call x11, Pallas kernels, columns_sum(): pl.pallas_call(functools.partial(columns_kernel, start, stop, [first for...  5.07 us
    pallas_call x2, Pallas kernels, attend_backward(): pl.pallas_call(functools.partial(backward_kernel, count, len(pieces)), in...  5.03 us
    unnamed x28, local copies, waits for them, and re-layouts  4.53 us
    pallas_call x2, Pallas kernels, partial_heads(): pl.pallas_call(functools.partial(partial_kernel, first), in_specs=whole(1...  2.35 us
    pallas_call x1, Pallas kernels, collect_columns(): pl.pallas_call(functools.partial(collect_kernel, local_heads, pieces), in...  2.07 us
  transfers between devices with their start and end apart: 30, of which 13 were waited for; matrix products, arithmetic and copies ran while one was open for 1% of the time, Pallas kernels for 23%

profile of v5, /device:TPU:0, one launch (start us, length us, event | category | flops | bytes accessed | tf_op | source)
XLA Modules:
  0.0 99.6 jit_solution(14615990712385479902)
XLA Ops:
  0.7 2.1 %collect_columns.1 = bf16[3,128,1024]{2,1,0:T(8,128)(2,1)} custom-call(s32[1]{0:T(128)} %bitcast.pos_ref, bf16[128,3072]{1,0:T(8,128)(2,1)} %refs_0_.3, bf16[128,3072]{1,0:T(8,128)(2,1)} %refs_1_.3, bf16[128,3072]{1,0:T(8,128)(2,1)} %refs_2_.3), custom_call_target="tpu_custom_call" | custom-call | tf_op jit(solution)/shard_map/collect_columns/pallas_call | solution.py:219
  2.8 3.0 %collective-permute-start = (bf16[3,128,1024]{2,1,0:T(8,128)(2,1)}, bf16[3,128,1024]{2,1,0:T(8,128)(2,1)}, u32[]{:S(2)}, u32[]{:S(2)}) collective-permute-start(bf16[3,128,1024]{2,1,0:T(8,128)(2,1)} %collect_columns.1), channel_id=1, source_target_pairs={{0,1},{1,0},{2,3},{3,2},{4,5},{5,4},{6,7},{7,6},{8,9},{9,8},{10,11... | collective-permute-start | bytes 2359304 | tf_op jit(solution)/shard_map/ppermute | solution.py:431
  8.0 1.6 %collective-permute-start.2 = (bf16[1280,128]{1,0:T(8,128)(2,1)S(1)}, bf16[1280,128]{1,0:T(8,128)(2,1)S(1)}, u32[]{:S(2)}, u32[]{:S(2)}) collective-permute-start(bf16[1280,128]{1,0:T(8,128)(2,1)S(1)} %get-tuple-element.53), channel_id=1, source_target_pairs={{0,4},{2,6},{4,0},{6,2},{8,12},{10,14},{12,8},{14,10},{16,20},{18,... | collective-permute-start | bytes 983048 | tf_op jit(solution)/shard_map/ppermute | solution.py:431
  9.5 2.6 %collective-permute-start.4 = (bf16[160,1536]{1,0:T(8,128)(2,1)S(1)}, bf16[160,1536]{1,0:T(8,128)(2,1)S(1)}, u32[]{:S(2)}, u32[]{:S(2)}) collective-permute-start(bf16[160,1536]{1,0:T(8,128)(2,1)S(1)} %bitcast.6), channel_id=1, source_target_pairs={{0,16},{2,18},{4,20},{6,22},{8,24},{10,26},{12,28},{14,30},{16,0},... | collective-permute-start | bytes 1474568 | tf_op jit(solution)/shard_map/ppermute | solution.py:431
  12.1 1.6 %collective-permute-start.6 = (bf16[160,1536]{1,0:T(8,128)(2,1)S(1)}, bf16[160,1536]{1,0:T(8,128)(2,1)S(1)}, u32[]{:S(2)}, u32[]{:S(2)}) collective-permute-start(bf16[160,1536]{1,0:T(8,128)(2,1)S(1)} %bitcast.7), channel_id=1, source_target_pairs={{0,8},{2,10},{4,12},{6,14},{8,0},{10,2},{12,4},{14,6},{16,24},{18,... | collective-permute-start | bytes 1474568 | tf_op jit(solution)/shard_map/ppermute | solution.py:431
  14.5 1.1 %copy-done.2 = bf16[128,3072]{1,0:T(8,128)(2,1)S(1)} copy-done((bf16[128,3072]{1,0:T(8,128)(2,1)S(1)}, bf16[128,3072]{1,0:T(8,128)(2,1)}, u32[]{:S(2)}) %copy-start.2) | copy-done | bytes 786456
  15.6 1.1 %copy-done.3 = bf16[128,3072]{1,0:T(8,128)(2,1)S(1)} copy-done((bf16[128,3072]{1,0:T(8,128)(2,1)S(1)}, bf16[128,3072]{1,0:T(8,128)(2,1)}, u32[]{:S(2)}) %copy-start.3) | copy-done | bytes 786456
  17.3 6.4 %collective-permute-done.refs_1_ = bf16[3,128,1024]{2,1,0:T(8,128)(2,1)} collective-permute-done((bf16[3,128,1024]{2,1,0:T(8,128)(2,1)}, bf16[3,128,1024]{2,1,0:T(8,128)(2,1)}, u32[]{:S(2)}, u32[]{:S(2)}) %collective-permute-start) | collective-permute-done | bytes 786464 | tf_op jit(solution)/shard_map/ppermute | solution.py:431
  23.7 1.7 %collective-permute-start.3 = (bf16[2,1280,128]{2,1,0:T(8,128)(2,1)S(1)}, bf16[2,1280,128]{2,1,0:T(8,128)(2,1)}, u32[]{:S(2)}, u32[]{:S(2)}) collective-permute-start(bf16[2,1280,128]{2,1,0:T(8,128)(2,1)S(1)} %pad_maximum_fusion.refs_0_), channel_id=1, source_target_pairs={{0,1},{1,0},{2,3},{3,2},{4,5},{5,4},{6,7},{7,6},{8,9},{9,8},{10,11... | collective-permute-start | bytes 1966088 | tf_op jit(solution)/shard_map/ppermute | solution.py:431
  25.5 1.1 %copy-done.5 = bf16[3,128,1024]{2,1,0:T(8,128)(2,1)S(1)} copy-done((bf16[3,128,1024]{2,1,0:T(8,128)(2,1)S(1)}, bf16[3,128,1024]{2,1,0:T(8,128)(2,1)}, u32[]{:S(2)}) %copy-start.5) | copy-done | bytes 786456
  26.6 4.1 %attend_forward.2 = (bf16[1024,256]{1,0:T(8,128)(2,1)S(1)}, f32[8,256,256]{2,1,0:T(8,128)S(1)}) custom-call(s32[1]{0:T(128)} %bitcast.pos_ref, s32[24,4]{1,0:T(8,128)S(1)} %copy.10.mask_ref, bf16[3,128,1024]{2,1,0:T(8,128)(2,1)S(1)} %copy-done.5, bf16[3,128,1024]{2,1,0:T(8,128)(2,1)} %collective-permute-done.refs_1_), custom_call_target="tpu_custom_call" | custom-call | tf_op jit(solution)/shard_map/attend_forward/pallas_call | solution.py:146
  30.7 1.6 %collective-permute-start.8 = (bf16[1024,256]{1,0:T(8,128)(2,1)S(1)}, bf16[1024,256]{1,0:T(8,128)(2,1)S(1)}, u32[]{:S(2)}, u32[]{:S(2)}) collective-permute-start(bf16[1024,256]{1,0:T(8,128)(2,1)S(1)} %get-tuple-element.87.outs_ref), channel_id=1, source_target_pairs={{0,4},{2,6},{4,0},{6,2},{8,12},{10,14},{12,8},{14,10},{16,20},{18,... | collective-permute-start | bytes 1572872 | tf_op jit(solution)/shard_map/ppermute | solution.py:431
  32.3 1.1 %collective-permute-done.4.refs_1_ = bf16[160,1536]{1,0:T(8,128)(2,1)S(1)} collective-permute-done((bf16[160,1536]{1,0:T(8,128)(2,1)S(1)}, bf16[160,1536]{1,0:T(8,128)(2,1)S(1)}, u32[]{:S(2)}, u32[]{:S(2)}) %collective-permute-start.4) | collective-permute-done | bytes 491552 | tf_op jit(solution)/shard_map/ppermute | solution.py:431
  34.7 4.9 %collective-permute-done.3.refs_1_ = bf16[2,1280,128]{2,1,0:T(8,128)(2,1)} collective-permute-done((bf16[2,1280,128]{2,1,0:T(8,128)(2,1)S(1)}, bf16[2,1280,128]{2,1,0:T(8,128)(2,1)}, u32[]{:S(2)}, u32[]{:S(2)}) %collective-permute-start.3) | collective-permute-done | bytes 655392 | tf_op jit(solution)/shard_map/ppermute | solution.py:431
  39.7 1.4 %collective-permute-start.11 = (bf16[3,128,512]{2,1,0:T(8,128)(2,1)S(1)}, bf16[3,128,512]{2,1,0:T(8,128)(2,1)S(1)}, u32[]{:S(2)}, u32[]{:S(2)}) collective-permute-start(bf16[3,128,512]{2,1,0:T(8,128)(2,1)S(1)} %copy-done.11), channel_id=1, source_target_pairs={{0,1},{1,0},{2,3},{3,2},{4,5},{5,4},{6,7},{7,6},{8,9},{9,8},{10,11... | collective-permute-start | bytes 1179656 | tf_op jit(solution)/shard_map/ppermute | solution.py:431
  41.1 1.5 %join_pieces.1 = (bf16[1280,512]{1,0:T(8,128)(2,1)S(1)}, bf16[512,1280]{1,0:T(8,128)(2,1)S(1)}) custom-call(bf16[2,1280,128]{2,1,0:T(8,128)(2,1)S(1)} %pad_maximum_fusion.refs_0_, bf16[2,1280,128]{2,1,0:T(8,128)(2,1)} %collective-permute-done.3.refs_1_), custom_call_target="tpu_custom_call" | custom-call | tf_op jit(solution)/shard_map/join_pieces/pallas_call | solution.py:280
  46.2 2.9 %collective-permute-done.11.refs_1_ = bf16[3,128,512]{2,1,0:T(8,128)(2,1)S(1)} collective-permute-done((bf16[3,128,512]{2,1,0:T(8,128)(2,1)S(1)}, bf16[3,128,512]{2,1,0:T(8,128)(2,1)S(1)}, u32[]{:S(2)}, u32[]{:S(2)}) %collective-permute-start.11) | collective-permute-done | bytes 393248 | tf_op jit(solution)/shard_map/ppermute | solution.py:431
  49.9 1.2 %collective-permute-start.14 = (bf16[320,1024]{1,0:T(8,128)(2,1)S(1)}, bf16[320,1024]{1,0:T(8,128)(2,1)S(1)}, u32[]{:S(2)}, u32[]{:S(2)}) collective-permute-start(bf16[320,1024]{1,0:T(8,128)(2,1)S(1)} %columns_sum.13), channel_id=1, source_target_pairs={{0,8},{2,10},{4,12},{6,14},{8,0},{10,2},{12,4},{14,6},{16,24},{18,... | collective-permute-start | bytes 1966088 | tf_op jit(solution)/shard_map/ppermute | solution.py:431
  51.1 1.5 %partial_heads.2 = (f32[256,1024]{1,0:T(8,128)S(1)}, bf16[256,1024]{1,0:T(8,128)(2,1)S(1)}) custom-call(bf16[512,1280]{1,0:T(8,128)(2,1)S(1)} %get-tuple-element.76.grad_ref, bf16[160,1536]{1,0:T(8,128)(2,1)S(1)} %bitcast.10, bf16[160,1536]{1,0:T(8,128)(2,1)S(1)} %collective-permute-done.4.refs_1_, bf16[160,1536]{1,0:T(8,128)(2,1)S(1)} %collective-permute-done.6.refs_2_, ...), custom_call_target="tpu_custom_call" | custom-call | tf_op jit(solution)/shard_map/partial_heads/pallas_call | solution.py:313
  53.3 2.2 %attend_forward.3 = (bf16[512,256]{1,0:T(8,128)(2,1)S(1)}, f32[4,256,256]{2,1,0:T(8,128)S(1)}) custom-call(s32[1]{0:T(128)} %bitcast.pos_ref, s32[24,4]{1,0:T(8,128)S(1)} %copy.10.mask_ref, bf16[3,128,512]{2,1,0:T(8,128)(2,1)S(1)} %get-tuple-element.72.refs_0_, bf16[3,128,512]{2,1,0:T(8,128)(2,1)S(1)} %collective-permute-done.11.refs_1_), custom_call_target="tpu_custom_call" | custom-call | tf_op jit(solution)/shard_map/attend_forward/pallas_call | solution.py:146
  55.5 1.6 %collective-permute-start.19 = (bf16[512,256]{1,0:T(8,128)(2,1)S(1)}, bf16[512,256]{1,0:T(8,128)(2,1)S(1)}, u32[]{:S(2)}, u32[]{:S(2)}) collective-permute-start(bf16[512,256]{1,0:T(8,128)(2,1)S(1)} %get-tuple-element.88.outs_ref), channel_id=1, source_target_pairs={{0,4},{2,6},{4,0},{6,2},{8,12},{10,14},{12,8},{14,10},{16,20},{18,... | collective-permute-start | bytes 786440 | tf_op jit(solution)/shard_map/ppermute | solution.py:431
  57.6 7.1 %collective-permute-done.19.outs_x_ref = bf16[512,256]{1,0:T(8,128)(2,1)S(1)} collective-permute-done((bf16[512,256]{1,0:T(8,128)(2,1)S(1)}, bf16[512,256]{1,0:T(8,128)(2,1)S(1)}, u32[]{:S(2)}, u32[]{:S(2)}) %collective-permute-start.19) | collective-permute-done | bytes 262176 | tf_op jit(solution)/shard_map/ppermute | solution.py:431
  69.1 2.3 %collective-permute-start.27 = (bf16[160,1024]{1,0:T(8,128)(2,1)S(1)}, bf16[160,1024]{1,0:T(8,128)(2,1)S(1)}, u32[]{:S(2)}, u32[]{:S(2)}) collective-permute-start(bf16[160,1024]{1,0:T(8,128)(2,1)S(1)} %columns_sum.15), channel_id=1, source_target_pairs={{0,16},{2,18},{4,20},{6,22},{8,24},{10,26},{12,28},{14,30},{16,0},... | collective-permute-start | bytes 983048 | tf_op jit(solution)/shard_map/ppermute | solution.py:431
  72.2 1.5 %collective-permute-start.25 = (bf16[256,512]{1,0:T(8,128)(2,1)S(1)}, bf16[256,512]{1,0:T(8,128)(2,1)S(1)}, u32[]{:S(2)}, u32[]{:S(2)}) collective-permute-start(bf16[256,512]{1,0:T(8,128)(2,1)S(1)} %get-tuple-element.79), channel_id=1, source_target_pairs={{0,4},{2,6},{4,0},{6,2},{8,12},{10,14},{12,8},{14,10},{16,20},{18,... | collective-permute-start | bytes 786440 | tf_op jit(solution)/shard_map/ppermute | solution.py:431
  74.2 1.7 %collective-permute-done.16.refs_4_ = bf16[256,1024]{1,0:T(8,128)(2,1)S(1)} collective-permute-done((bf16[256,1024]{1,0:T(8,128)(2,1)S(1)}, bf16[256,1024]{1,0:T(8,128)(2,1)S(1)}, u32[]{:S(2)}, u32[]{:S(2)}) %collective-permute-start.16) | collective-permute-done | bytes 524320 | tf_op jit(solution)/shard_map/ppermute | solution.py:431
  75.9 3.7 %attend_backward.2 = (bf16[2,128,1024]{2,1,0:T(8,128)(2,1)S(1)}, bf16[2,128,1024]{2,1,0:T(8,128)(2,1)S(1)}) custom-call(bf16[3,128,1024]{2,1,0:T(8,128)(2,1)S(1)} %copy-done.6, bf16[3,128,1024]{2,1,0:T(8,128)(2,1)} %collective-permute-done.refs_1_, f32[8,256,256]{2,1,0:T(8,128)S(1)} %get-tuple-element.52.refs_2_, f32[256,1024]{1,0:T(8,128)S(1)} %get-tuple-element.68.refs_3_, ...), custom_call_target="tpu_custom_call" | custom-call | flops 3500000000 | tf_op jit(solution)/shard_map/attend_backward/pallas_call | solution.py:162
  79.6 1.6 %collective-permute-start.17 = (bf16[2,128,1024]{2,1,0:T(8,128)(2,1)S(1)}, bf16[2,128,1024]{2,1,0:T(8,128)(2,1)S(1)}, u32[]{:S(2)}, u32[]{:S(2)}) collective-permute-start(bf16[2,128,1024]{2,1,0:T(8,128)(2,1)S(1)} %get-tuple-element.71), channel_id=1, source_target_pairs={{0,1},{1,0},{2,3},{3,2},{4,5},{5,4},{6,7},{7,6},{8,9},{9,8},{10,11... | collective-permute-start | bytes 1572872 | tf_op jit(solution)/shard_map/ppermute | solution.py:431
  81.2 3.3 %collective-permute-done.24.refs_0_ = bf16[320,512]{1,0:T(8,128)(2,1)S(1)} collective-permute-done((bf16[320,512]{1,0:T(8,128)(2,1)S(1)}, bf16[320,512]{1,0:T(8,128)(2,1)S(1)}, u32[]{:S(2)}, u32[]{:S(2)}) %collective-permute-start.24) | collective-permute-done | bytes 327712 | tf_op jit(solution)/shard_map/ppermute | solution.py:431
  84.5 1.3 %attend_backward.3 = (bf16[2,128,512]{2,1,0:T(8,128)(2,1)S(1)}, bf16[2,128,512]{2,1,0:T(8,128)(2,1)S(1)}) custom-call(bf16[3,128,512]{2,1,0:T(8,128)(2,1)S(1)} %get-tuple-element.72.refs_0_, bf16[3,128,512]{2,1,0:T(8,128)(2,1)S(1)} %collective-permute-done.11.refs_1_, f32[4,256,256]{2,1,0:T(8,128)S(1)} %get-tuple-element.73.refs_2_, ...), custom_call_target="tpu_custom_call" | custom-call | tf_op jit(solution)/shard_map/attend_backward/pallas_call | solution.py:162
  85.8 1.6 %collective-permute-start.26 = (bf16[2,128,512]{2,1,0:T(8,128)(2,1)S(1)}, bf16[2,128,512]{2,1,0:T(8,128)(2,1)S(1)}, u32[]{:S(2)}, u32[]{:S(2)}) collective-permute-start(bf16[2,128,512]{2,1,0:T(8,128)(2,1)S(1)} %get-tuple-element.81), channel_id=1, source_target_pairs={{0,1},{1,0},{2,3},{3,2},{4,5},{5,4},{6,7},{7,6},{8,9},{9,8},{10,11... | collective-permute-start | bytes 786440 | tf_op jit(solution)/shard_map/ppermute | solution.py:431
  88.6 8.5 %collective-permute-done.29.refs_3_ = bf16[160,512]{1,0:T(8,128)(2,1)S(1)} collective-permute-done((bf16[160,512]{1,0:T(8,128)(2,1)S(1)}, bf16[160,512]{1,0:T(8,128)(2,1)S(1)}, u32[]{:S(2)}, u32[]{:S(2)}) %collective-permute-start.29) | collective-permute-done | bytes 163872 | tf_op jit(solution)/shard_map/ppermute | solution.py:431
  98.4 1.2 %assemble.1 = (bf16[128,3072]{1,0:T(8,128)(2,1)}, bf16[128,3072]{1,0:T(8,128)(2,1)}) custom-call(s32[1]{0:T(128)} %bitcast.pos_ref, bf16[2,128,1024]{2,1,0:T(8,128)(2,1)S(1)} %get-tuple-element.70.refs_0_, bf16[2,128,1024]{2,1,0:T(8,128)(2,1)S(1)} %collective-permute-done.17.refs_1_, bf16[2,128,512]{2,1,0:T(8,128)(2,1)S(1)} %get-tuple-element.80.refs_2_, ...), custom_call_target="tpu_custom_call" | custom-call | tf_op jit(solution)/shard_map/assemble/pallas_call | solution.py:387
  (90 shorter events, 18.4 us)
Async XLA Ops:
  0.6 13.8 %copy-start.12 = (s32[24,4,4]{0,2,1:T(4,128)S(1)}, s32[24,4,4]{0,2,1:T(4,128)}, u32[]{:S(2)}) copy-start(s32[24,4,4]{0,2,1:T(4,128)} %param.12) | copy-start | bytes 4612
  0.7 13.8 %copy-start.13 = (s32[24,4]{0,1:T(4,128)S(1)}, s32[24,4]{0,1:T(4,128)}, u32[]{:S(2)}) copy-start(s32[24,4]{0,1:T(4,128)} %param.13) | copy-start | bytes 1156
  2.8 20.9 %collective-permute-start = (bf16[3,128,1024]{2,1,0:T(8,128)(2,1)}, bf16[3,128,1024]{2,1,0:T(8,128)(2,1)}, u32[]{:S(2)}, u32[]{:S(2)}) collective-permute-start(bf16[3,128,1024]{2,1,0:T(8,128)(2,1)} %collect_columns.1), channel_id=1, source_target_pairs={{0,1},{1,0},{2,3},{3,2},{4,5},{5,4},{6,7},{7,6},{8,9},{9,8},{10,11... | collective-permute-start | bytes 2359304 | tf_op jit(solution)/shard_map/ppermute | solution.py:431
  8.0 9.2 %collective-permute-start.2 = (bf16[1280,128]{1,0:T(8,128)(2,1)S(1)}, bf16[1280,128]{1,0:T(8,128)(2,1)S(1)}, u32[]{:S(2)}, u32[]{:S(2)}) collective-permute-start(bf16[1280,128]{1,0:T(8,128)(2,1)S(1)} %get-tuple-element.53), channel_id=1, source_target_pairs={{0,4},{2,6},{4,0},{6,2},{8,12},{10,14},{12,8},{14,10},{16,20},{18,... | collective-permute-start | bytes 983048 | tf_op jit(solution)/shard_map/ppermute | solution.py:431
  9.5 23.9 %collective-permute-start.4 = (bf16[160,1536]{1,0:T(8,128)(2,1)S(1)}, bf16[160,1536]{1,0:T(8,128)(2,1)S(1)}, u32[]{:S(2)}, u32[]{:S(2)}) collective-permute-start(bf16[160,1536]{1,0:T(8,128)(2,1)S(1)} %bitcast.6), channel_id=1, source_target_pairs={{0,16},{2,18},{4,20},{6,22},{8,24},{10,26},{12,28},{14,30},{16,0},... | collective-permute-start | bytes 1474568 | tf_op jit(solution)/shard_map/ppermute | solution.py:431
  12.1 22.0 %collective-permute-start.6 = (bf16[160,1536]{1,0:T(8,128)(2,1)S(1)}, bf16[160,1536]{1,0:T(8,128)(2,1)S(1)}, u32[]{:S(2)}, u32[]{:S(2)}) collective-permute-start(bf16[160,1536]{1,0:T(8,128)(2,1)S(1)} %bitcast.7), channel_id=1, source_target_pairs={{0,8},{2,10},{4,12},{6,14},{8,0},{10,2},{12,4},{14,6},{16,24},{18,... | collective-permute-start | bytes 1474568 | tf_op jit(solution)/shard_map/ppermute | solution.py:431
  14.4 11.0 %collective-permute-start.1 = (bf16[160,1024]{1,0:T(8,128)(2,1)}, bf16[160,1024]{1,0:T(8,128)(2,1)S(1)}, u32[]{:S(2)}, u32[]{:S(2)}) collective-permute-start(bf16[160,1024]{1,0:T(8,128)(2,1)} %slice.32), channel_id=1, source_target_pairs={{0,2},{2,0},{4,6},{6,4},{8,10},{10,8},{12,14},{14,12},{16,18},{18,... | collective-permute-start | bytes 983048 | tf_op jit(solution)/shard_map/ppermute | solution.py:431
  23.7 16.0 %collective-permute-start.3 = (bf16[2,1280,128]{2,1,0:T(8,128)(2,1)S(1)}, bf16[2,1280,128]{2,1,0:T(8,128)(2,1)}, u32[]{:S(2)}, u32[]{:S(2)}) collective-permute-start(bf16[2,1280,128]{2,1,0:T(8,128)(2,1)S(1)} %pad_maximum_fusion.refs_0_), channel_id=1, source_target_pairs={{0,1},{1,0},{2,3},{3,2},{4,5},{5,4},{6,7},{7,6},{8,9},{9,8},{10,11... | collective-permute-start | bytes 1966088 | tf_op jit(solution)/shard_map/ppermute | solution.py:431
  30.7 12.6 %collective-permute-start.8 = (bf16[1024,256]{1,0:T(8,128)(2,1)S(1)}, bf16[1024,256]{1,0:T(8,128)(2,1)S(1)}, u32[]{:S(2)}, u32[]{:S(2)}) collective-permute-start(bf16[1024,256]{1,0:T(8,128)(2,1)S(1)} %get-tuple-element.87.outs_ref), channel_id=1, source_target_pairs={{0,4},{2,6},{4,0},{6,2},{8,12},{10,14},{12,8},{14,10},{16,20},{18,... | collective-permute-start | bytes 1572872 | tf_op jit(solution)/shard_map/ppermute | solution.py:431
  33.5 12.0 %collective-permute-start.10 = (bf16[160,1536]{1,0:T(8,128)(2,1)S(1)}, bf16[160,1536]{1,0:T(8,128)(2,1)S(1)}, u32[]{:S(2)}, u32[]{:S(2)}) collective-permute-start(bf16[160,1536]{1,0:T(8,128)(2,1)S(1)} %collective-permute-done.4.refs_1_), channel_id=1, source_target_pairs={{0,8},{2,10},{4,12},{6,14},{8,0},{10,2},{12,4},{14,6},{16,24},{18,... | collective-permute-start | bytes 1474568 | tf_op jit(solution)/shard_map/ppermute | solution.py:431
  34.1 7.1 %collective-permute-start.5 = (bf16[160,1024]{1,0:T(8,128)(2,1)S(1)}, bf16[160,1024]{1,0:T(8,128)(2,1)S(1)}, u32[]{:S(2)}, u32[]{:S(2)}) collective-permute-start(bf16[160,1024]{1,0:T(8,128)(2,1)S(1)} %slice.25), channel_id=1, source_target_pairs={{0,2},{2,0},{4,6},{6,4},{8,10},{10,8},{12,14},{14,12},{16,18},{18,... | collective-permute-start | bytes 983048 | tf_op jit(solution)/shard_map/ppermute | solution.py:431
  34.2 6.9 %collective-permute-start.7 = (bf16[160,1024]{1,0:T(8,128)(2,1)S(1)}, bf16[160,1024]{1,0:T(8,128)(2,1)S(1)}, u32[]{:S(2)}, u32[]{:S(2)}) collective-permute-start(bf16[160,1024]{1,0:T(8,128)(2,1)S(1)} %slice.26), channel_id=1, source_target_pairs={{0,2},{2,0},{4,6},{6,4},{8,10},{10,8},{12,14},{14,12},{16,18},{18,... | collective-permute-start | bytes 983048 | tf_op jit(solution)/shard_map/ppermute | solution.py:431
  39.7 9.4 %collective-permute-start.11 = (bf16[3,128,512]{2,1,0:T(8,128)(2,1)S(1)}, bf16[3,128,512]{2,1,0:T(8,128)(2,1)S(1)}, u32[]{:S(2)}, u32[]{:S(2)}) collective-permute-start(bf16[3,128,512]{2,1,0:T(8,128)(2,1)S(1)} %copy-done.11), channel_id=1, source_target_pairs={{0,1},{1,0},{2,3},{3,2},{4,5},{5,4},{6,7},{7,6},{8,9},{9,8},{10,11... | collective-permute-start | bytes 1179656 | tf_op jit(solution)/shard_map/ppermute | solution.py:431
  43.8 2.3 %collective-permute-start.9 = (bf16[160,1024]{1,0:T(8,128)(2,1)S(1)}, bf16[160,1024]{1,0:T(8,128)(2,1)S(1)}, u32[]{:S(2)}, u32[]{:S(2)}) collective-permute-start(bf16[160,1024]{1,0:T(8,128)(2,1)S(1)} %columns_sum.11), channel_id=1, source_target_pairs={{0,2},{2,0},{4,6},{6,4},{8,10},{10,8},{12,14},{14,12},{16,18},{18,... | collective-permute-start | bytes 983048 | tf_op jit(solution)/shard_map/ppermute | solution.py:431
  44.4 4.7 %collective-permute-start.12 = (bf16[160,1024]{1,0:T(8,128)(2,1)S(1)}, bf16[160,1024]{1,0:T(8,128)(2,1)S(1)}, u32[]{:S(2)}, u32[]{:S(2)}) collective-permute-start(bf16[160,1024]{1,0:T(8,128)(2,1)S(1)} %columns_sum.12), channel_id=1, source_target_pairs={{0,2},{2,0},{4,6},{6,4},{8,10},{10,8},{12,14},{14,12},{16,18},{18,... | collective-permute-start | bytes 983048 | tf_op jit(solution)/shard_map/ppermute | solution.py:431
  45.5 5.6 %collective-permute-start.13 = (bf16[160,1024]{1,0:T(8,128)(2,1)S(1)}, bf16[160,1024]{1,0:T(8,128)(2,1)S(1)}, u32[]{:S(2)}, u32[]{:S(2)}) collective-permute-start(bf16[160,1024]{1,0:T(8,128)(2,1)S(1)} %slice.33), channel_id=1, source_target_pairs={{0,2},{2,0},{4,6},{6,4},{8,10},{10,8},{12,14},{14,12},{16,18},{18,... | collective-permute-start | bytes 983048 | tf_op jit(solution)/shard_map/ppermute | solution.py:431
  45.6 7.7 %collective-permute-start.18 = (bf16[160,512]{1,0:T(8,128)(2,1)S(1)}, bf16[160,512]{1,0:T(8,128)(2,1)S(1)}, u32[]{:S(2)}, u32[]{:S(2)}) collective-permute-start(bf16[160,512]{1,0:T(8,128)(2,1)S(1)} %slice.34), channel_id=1, source_target_pairs={{0,2},{2,0},{4,6},{6,4},{8,10},{10,8},{12,14},{14,12},{16,18},{18,... | collective-permute-start | bytes 491528 | tf_op jit(solution)/shard_map/ppermute | solution.py:431
  49.9 17.0 %collective-permute-start.14 = (bf16[320,1024]{1,0:T(8,128)(2,1)S(1)}, bf16[320,1024]{1,0:T(8,128)(2,1)S(1)}, u32[]{:S(2)}, u32[]{:S(2)}) collective-permute-start(bf16[320,1024]{1,0:T(8,128)(2,1)S(1)} %columns_sum.13), channel_id=1, source_target_pairs={{0,8},{2,10},{4,12},{6,14},{8,0},{10,2},{12,4},{14,6},{16,24},{18,... | collective-permute-start | bytes 1966088 | tf_op jit(solution)/shard_map/ppermute | solution.py:431
  53.2 14.4 %collective-permute-start.15 = (bf16[320,1024]{1,0:T(8,128)(2,1)S(1)}, bf16[320,1024]{1,0:T(8,128)(2,1)S(1)}, u32[]{:S(2)}, u32[]{:S(2)}) collective-permute-start(bf16[320,1024]{1,0:T(8,128)(2,1)S(1)} %columns_sum.14), channel_id=1, source_target_pairs={{0,2},{2,0},{4,6},{6,4},{8,10},{10,8},{12,14},{14,12},{16,18},{18,... | collective-permute-start | bytes 1966088 | tf_op jit(solution)/shard_map/ppermute | solution.py:431
  55.5 9.2 %collective-permute-start.19 = (bf16[512,256]{1,0:T(8,128)(2,1)S(1)}, bf16[512,256]{1,0:T(8,128)(2,1)S(1)}, u32[]{:S(2)}, u32[]{:S(2)}) collective-permute-start(bf16[512,256]{1,0:T(8,128)(2,1)S(1)} %get-tuple-element.88.outs_ref), channel_id=1, source_target_pairs={{0,4},{2,6},{4,0},{6,2},{8,12},{10,14},{12,8},{14,10},{16,20},{18,... | collective-permute-start | bytes 786440 | tf_op jit(solution)/shard_map/ppermute | solution.py:431
  57.1 18.8 %collective-permute-start.16 = (bf16[256,1024]{1,0:T(8,128)(2,1)S(1)}, bf16[256,1024]{1,0:T(8,128)(2,1)S(1)}, u32[]{:S(2)}, u32[]{:S(2)}) collective-permute-start(bf16[256,1024]{1,0:T(8,128)(2,1)S(1)} %get-tuple-element.69), channel_id=1, source_target_pairs={{0,4},{2,6},{4,0},{6,2},{8,12},{10,14},{12,8},{14,10},{16,20},{18,... | collective-permute-start | bytes 1572872 | tf_op jit(solution)/shard_map/ppermute | solution.py:431
  65.0 1.7 %collective-permute-start.20 = (bf16[320,512]{1,0:T(8,128)(2,1)S(1)}, bf16[320,512]{1,0:T(8,128)(2,1)S(1)}, u32[]{:S(2)}, u32[]{:S(2)}) collective-permute-start(bf16[320,512]{1,0:T(8,128)(2,1)S(1)} %columns_sum.16), channel_id=1, source_target_pairs={{0,2},{2,0},{4,6},{6,4},{8,10},{10,8},{12,14},{14,12},{16,18},{18,... | collective-permute-start | bytes 983048 | tf_op jit(solution)/shard_map/ppermute | solution.py:431
  65.1 3.9 %collective-permute-start.21 = (bf16[160,512]{1,0:T(8,128)(2,1)S(1)}, bf16[160,512]{1,0:T(8,128)(2,1)S(1)}, u32[]{:S(2)}, u32[]{:S(2)}) collective-permute-start(bf16[160,512]{1,0:T(8,128)(2,1)S(1)} %slice.35), channel_id=1, source_target_pairs={{0,2},{2,0},{4,6},{6,4},{8,10},{10,8},{12,14},{14,12},{16,18},{18,... | collective-permute-start | bytes 491528 | tf_op jit(solution)/shard_map/ppermute | solution.py:431
  66.7 4.6 %collective-permute-start.22 = (bf16[160,512]{1,0:T(8,128)(2,1)S(1)}, bf16[160,512]{1,0:T(8,128)(2,1)S(1)}, u32[]{:S(2)}, u32[]{:S(2)}) collective-permute-start(bf16[160,512]{1,0:T(8,128)(2,1)S(1)} %slice.36), channel_id=1, source_target_pairs={{0,2},{2,0},{4,6},{6,4},{8,10},{10,8},{12,14},{14,12},{16,18},{18,... | collective-permute-start | bytes 491528 | tf_op jit(solution)/shard_map/ppermute | solution.py:431
  66.9 4.5 %collective-permute-start.23 = (bf16[160,512]{1,0:T(8,128)(2,1)S(1)}, bf16[160,512]{1,0:T(8,128)(2,1)S(1)}, u32[]{:S(2)}, u32[]{:S(2)}) collective-permute-start(bf16[160,512]{1,0:T(8,128)(2,1)S(1)} %slice.37), channel_id=1, source_target_pairs={{0,2},{2,0},{4,6},{6,4},{8,10},{10,8},{12,14},{14,12},{16,18},{18,... | collective-permute-start | bytes 491528 | tf_op jit(solution)/shard_map/ppermute | solution.py:431
  67.6 16.8 %collective-permute-start.24 = (bf16[320,512]{1,0:T(8,128)(2,1)S(1)}, bf16[320,512]{1,0:T(8,128)(2,1)S(1)}, u32[]{:S(2)}, u32[]{:S(2)}) collective-permute-start(bf16[320,512]{1,0:T(8,128)(2,1)S(1)} %columns_sum.17), channel_id=1, source_target_pairs={{0,8},{2,10},{4,12},{6,14},{8,0},{10,2},{12,4},{14,6},{16,24},{18,... | collective-permute-start | bytes 983048 | tf_op jit(solution)/shard_map/ppermute | solution.py:431
  69.1 18.3 %collective-permute-start.27 = (bf16[160,1024]{1,0:T(8,128)(2,1)S(1)}, bf16[160,1024]{1,0:T(8,128)(2,1)S(1)}, u32[]{:S(2)}, u32[]{:S(2)}) collective-permute-start(bf16[160,1024]{1,0:T(8,128)(2,1)S(1)} %columns_sum.15), channel_id=1, source_target_pairs={{0,16},{2,18},{4,20},{6,22},{8,24},{10,26},{12,28},{14,30},{16,0},... | collective-permute-start | bytes 983048 | tf_op jit(solution)/shard_map/ppermute | solution.py:431
  72.2 12.3 %collective-permute-start.25 = (bf16[256,512]{1,0:T(8,128)(2,1)S(1)}, bf16[256,512]{1,0:T(8,128)(2,1)S(1)}, u32[]{:S(2)}, u32[]{:S(2)}) collective-permute-start(bf16[256,512]{1,0:T(8,128)(2,1)S(1)} %get-tuple-element.79), channel_id=1, source_target_pairs={{0,4},{2,6},{4,0},{6,2},{8,12},{10,14},{12,8},{14,10},{16,20},{18,... | collective-permute-start | bytes 786440 | tf_op jit(solution)/shard_map/ppermute | solution.py:431
  74.1 13.3 %collective-permute-start.28 = (bf16[320,512]{1,0:T(8,128)(2,1)S(1)}, bf16[320,512]{1,0:T(8,128)(2,1)S(1)}, u32[]{:S(2)}, u32[]{:S(2)}) collective-permute-start(bf16[320,512]{1,0:T(8,128)(2,1)S(1)} %columns_sum.18), channel_id=1, source_target_pairs={{0,2},{2,0},{4,6},{6,4},{8,10},{10,8},{12,14},{14,12},{16,18},{18,... | collective-permute-start | bytes 983048 | tf_op jit(solution)/shard_map/ppermute | solution.py:431
  79.6 18.8 %collective-permute-start.17 = (bf16[2,128,1024]{2,1,0:T(8,128)(2,1)S(1)}, bf16[2,128,1024]{2,1,0:T(8,128)(2,1)S(1)}, u32[]{:S(2)}, u32[]{:S(2)}) collective-permute-start(bf16[2,128,1024]{2,1,0:T(8,128)(2,1)S(1)} %get-tuple-element.71), channel_id=1, source_target_pairs={{0,1},{1,0},{2,3},{3,2},{4,5},{5,4},{6,7},{7,6},{8,9},{9,8},{10,11... | collective-permute-start | bytes 1572872 | tf_op jit(solution)/shard_map/ppermute | solution.py:431
  85.8 12.6 %collective-permute-start.26 = (bf16[2,128,512]{2,1,0:T(8,128)(2,1)S(1)}, bf16[2,128,512]{2,1,0:T(8,128)(2,1)S(1)}, u32[]{:S(2)}, u32[]{:S(2)}) collective-permute-start(bf16[2,128,512]{2,1,0:T(8,128)(2,1)S(1)} %get-tuple-element.81), channel_id=1, source_target_pairs={{0,1},{1,0},{2,3},{3,2},{4,5},{5,4},{6,7},{7,6},{8,9},{9,8},{10,11... | collective-permute-start | bytes 786440 | tf_op jit(solution)/shard_map/ppermute | solution.py:431
  87.7 9.4 %collective-permute-start.29 = (bf16[160,512]{1,0:T(8,128)(2,1)S(1)}, bf16[160,512]{1,0:T(8,128)(2,1)S(1)}, u32[]{:S(2)}, u32[]{:S(2)}) collective-permute-start(bf16[160,512]{1,0:T(8,128)(2,1)S(1)} %columns_sum.19), channel_id=1, source_target_pairs={{0,16},{2,18},{4,20},{6,22},{8,24},{10,26},{12,28},{14,30},{16,0},... | collective-permute-start | bytes 491528 | tf_op jit(solution)/shard_map/ppermute | solution.py:431
  (12 other events, 66.7 us)

commit v6 on v5

--- a/solution.py
+++ b/solution.py
@@ -362,13 +362,11 @@
     )(wide, outs, outs_x, *[piece for piece, _ in arrived])
 
 
-def assemble_kernel(local_heads, firsts, pos_ref, *refs):
-    part_refs, (query_ref, key_ref, sems) = refs[:-3], refs[-3:]
-    sections = len(part_refs) // len(firsts)
+def assemble_kernel(local_heads, places, pos_ref, *refs):
+    part_refs, (query_ref, key_ref, sems) = refs[: len(places)], refs[-3:]
     copies = []
-    for index, part_ref in enumerate(part_refs):
-        distance, part = index % sections, index // sections
-        start = pl.multiple_of(((pos_ref[0] ^ distance) * local_heads + firsts[part]) * HD, HD)
+    for (distance, first), part_ref in zip(places, part_refs):
+        start = pl.multiple_of(((pos_ref[0] ^ distance) * local_heads + first) * HD, HD)
         columns = pl.ds(start, part_ref.shape[2])
         for slot, out_ref in enumerate((query_ref, key_ref)):
             copies.append(
@@ -382,18 +380,19 @@
         copy.wait()
 
 
-def assemble(pos, parts, local_heads, firsts):
+def assemble(pos, parts, local_heads, places, written):
     tokens = parts[0].shape[1]
     return pl.pallas_call(
-        functools.partial(assemble_kernel, local_heads, firsts),
-        in_specs=whole(1, pltpu.SMEM) + whole(len(parts)),
+        functools.partial(assemble_kernel, local_heads, places),
+        in_specs=whole(1, pltpu.SMEM) + whole(len(parts)) + whole(len(written), pltpu.HBM),
         out_specs=whole(2, pltpu.HBM),
         out_shape=[jax.ShapeDtypeStruct((tokens, HEADS * HD), jnp.bfloat16)] * 2,
         scratch_shapes=[pltpu.SemaphoreType.DMA((2 * len(parts),))],
+        input_output_aliases={1 + len(parts) + index: index for index in range(len(written))},
         compiler_params=pltpu.CompilerParams(vmem_limit_bytes=VMEM_LIMIT),
         cost_estimate=SMALL_COST,
         name="assemble",
-    )(pos, *parts)
+    )(pos, *parts, *written)
 
 
 def add_kernel(*refs):
@@ -607,8 +606,16 @@
         back_parts += [swap_with(backs[k], "seq", k) for k in others]
         if part:
             last = next_sums(last + [arrived[0][-1][0]])
-    back_parts[-1] = after(back_parts[-1], *last)
-    grad_queries, grad_keys = assemble(pos, back_parts, local_heads, firsts)
+    places = [(k, first) for first in firsts for k in range(seq_size)]
+    grads = assemble(
+        pos, back_parts[::seq_size], local_heads, [(0, first) for first in firsts], []
+    )
+    last = last + [grads[0]]
+    back_parts[-1] = after(back_parts[-1], *last[:-1])
+    far = [index for index, (k, _) in enumerate(places) if k]
+    grad_queries, grad_keys = assemble(
+        pos, [back_parts[i] for i in far], local_heads, [places[i] for i in far], grads
+    )
     for part in range(len(counts)):
         final, _ = arrived[part].pop()
         base = columns_of(part, 0, cols, jnp.float32, *last)

time: 100 us -> 99.8 us (level)
  waiting for transfers between devices: 38.8 us -> 37.8 us
  transfers between devices with their start and end apart: 30 -> 30, of which waited for: 13 -> 13; matrix products, arithmetic and copies ran while one was open for 1% -> 1% of each run, Pallas kernels for 23% -> 24%
where the time goes in v6:
time: 99.8 us; the launch traced here: 99.4 us
  waiting for transfers between devices  37.8 us (38%)
  starting transfers between devices  28.5 us (29%)
  Pallas kernels  26.4 us (26%)
  local copies, waits for them, and re-layouts  5.52 us (6%)
  between operations  1.04 us (1%)
    ppermute x30, waiting for transfers between devices, swap_with(): lax.ppermute(array_in, axis_name, [(i, i ^ distance) for i in range(size)])  37.8 us
    ppermute x30, starting transfers between devices, swap_with(): lax.ppermute(array_in, axis_name, [(i, i ^ distance) for i in range(size)])  28.5 us
    pallas_call x2, Pallas kernels, attend_forward(): pl.pallas_call(functools.partial(forward_kernel, first, count, local_head...  6.34 us
    pallas_call x11, Pallas kernels, columns_sum(): pl.pallas_call(functools.partial(columns_kernel, start, stop, [first for...  5.07 us
    pallas_call x2, Pallas kernels, attend_backward(): pl.pallas_call(functools.partial(backward_kernel, count, len(pieces)), in...  5.03 us
    unnamed x28, local copies, waits for them, and re-layouts  4.53 us
    pallas_call x2, Pallas kernels, partial_heads(): pl.pallas_call(functools.partial(partial_kernel, first), in_specs=whole(1...  2.35 us
    pallas_call x1, Pallas kernels, collect_columns(): pl.pallas_call(functools.partial(collect_kernel, local_heads, pieces), in...  2.07 us
  transfers between devices with their start and end apart: 30, of which 13 were waited for; matrix products, arithmetic and copies ran while one was open for 1% of the time, Pallas kernels for 24%

profile of v6, /device:TPU:0, one launch (start us, length us, event | category | flops | bytes accessed | tf_op | source)
XLA Modules:
  0.0 99.4 jit_solution(7113859576750398515)
XLA Ops:
  0.7 2.1 %collect_columns.1 = bf16[3,128,1024]{2,1,0:T(8,128)(2,1)} custom-call(s32[1]{0:T(128)} %bitcast.pos_ref, bf16[128,3072]{1,0:T(8,128)(2,1)} %refs_0_.3, bf16[128,3072]{1,0:T(8,128)(2,1)} %refs_1_.3, bf16[128,3072]{1,0:T(8,128)(2,1)} %refs_2_.3), custom_call_target="tpu_custom_call" | custom-call | tf_op jit(solution)/shard_map/collect_columns/pallas_call | solution.py:219
  2.8 3.0 %collective-permute-start = (bf16[3,128,1024]{2,1,0:T(8,128)(2,1)}, bf16[3,128,1024]{2,1,0:T(8,128)(2,1)}, u32[]{:S(2)}, u32[]{:S(2)}) collective-permute-start(bf16[3,128,1024]{2,1,0:T(8,128)(2,1)} %collect_columns.1), channel_id=1, source_target_pairs={{0,1},{1,0},{2,3},{3,2},{4,5},{5,4},{6,7},{7,6},{8,9},{9,8},{10,11... | collective-permute-start | bytes 2359304 | tf_op jit(solution)/shard_map/ppermute | solution.py:430
  5.8 1.1 %copy-done.7 = bf16[128,2560]{1,0:T(8,128)(2,1)S(1)} copy-done((bf16[128,2560]{1,0:T(8,128)(2,1)S(1)}, bf16[128,2560]{1,0:T(8,128)(2,1)}, u32[]{:S(2)}) %copy-start.7) | copy-done | bytes 655384
  8.0 1.6 %collective-permute-start.2 = (bf16[1280,128]{1,0:T(8,128)(2,1)S(1)}, bf16[1280,128]{1,0:T(8,128)(2,1)S(1)}, u32[]{:S(2)}, u32[]{:S(2)}) collective-permute-start(bf16[1280,128]{1,0:T(8,128)(2,1)S(1)} %get-tuple-element.55), channel_id=1, source_target_pairs={{0,4},{2,6},{4,0},{6,2},{8,12},{10,14},{12,8},{14,10},{16,20},{18,... | collective-permute-start | bytes 983048 | tf_op jit(solution)/shard_map/ppermute | solution.py:430
  9.5 2.6 %collective-permute-start.4 = (bf16[160,1536]{1,0:T(8,128)(2,1)S(1)}, bf16[160,1536]{1,0:T(8,128)(2,1)S(1)}, u32[]{:S(2)}, u32[]{:S(2)}) collective-permute-start(bf16[160,1536]{1,0:T(8,128)(2,1)S(1)} %bitcast.6), channel_id=1, source_target_pairs={{0,16},{2,18},{4,20},{6,22},{8,24},{10,26},{12,28},{14,30},{16,0},... | collective-permute-start | bytes 1474568 | tf_op jit(solution)/shard_map/ppermute | solution.py:430
  12.1 1.6 %collective-permute-start.6 = (bf16[160,1536]{1,0:T(8,128)(2,1)S(1)}, bf16[160,1536]{1,0:T(8,128)(2,1)S(1)}, u32[]{:S(2)}, u32[]{:S(2)}) collective-permute-start(bf16[160,1536]{1,0:T(8,128)(2,1)S(1)} %bitcast.7), channel_id=1, source_target_pairs={{0,8},{2,10},{4,12},{6,14},{8,0},{10,2},{12,4},{14,6},{16,24},{18,... | collective-permute-start | bytes 1474568 | tf_op jit(solution)/shard_map/ppermute | solution.py:430
  14.5 1.1 %copy-done.2 = bf16[128,3072]{1,0:T(8,128)(2,1)S(1)} copy-done((bf16[128,3072]{1,0:T(8,128)(2,1)S(1)}, bf16[128,3072]{1,0:T(8,128)(2,1)}, u32[]{:S(2)}) %copy-start.2) | copy-done | bytes 786456
  15.6 1.1 %copy-done.3 = bf16[128,3072]{1,0:T(8,128)(2,1)S(1)} copy-done((bf16[128,3072]{1,0:T(8,128)(2,1)S(1)}, bf16[128,3072]{1,0:T(8,128)(2,1)}, u32[]{:S(2)}) %copy-start.3) | copy-done | bytes 786456
  17.3 6.4 %collective-permute-done.refs_1_ = bf16[3,128,1024]{2,1,0:T(8,128)(2,1)} collective-permute-done((bf16[3,128,1024]{2,1,0:T(8,128)(2,1)}, bf16[3,128,1024]{2,1,0:T(8,128)(2,1)}, u32[]{:S(2)}, u32[]{:S(2)}) %collective-permute-start) | collective-permute-done | bytes 786464 | tf_op jit(solution)/shard_map/ppermute | solution.py:430
  23.7 1.7 %collective-permute-start.3 = (bf16[2,1280,128]{2,1,0:T(8,128)(2,1)S(1)}, bf16[2,1280,128]{2,1,0:T(8,128)(2,1)}, u32[]{:S(2)}, u32[]{:S(2)}) collective-permute-start(bf16[2,1280,128]{2,1,0:T(8,128)(2,1)S(1)} %pad_maximum_fusion.refs_0_), channel_id=1, source_target_pairs={{0,1},{1,0},{2,3},{3,2},{4,5},{5,4},{6,7},{7,6},{8,9},{9,8},{10,11... | collective-permute-start | bytes 1966088 | tf_op jit(solution)/shard_map/ppermute | solution.py:430
  25.5 1.1 %copy-done.5 = bf16[3,128,1024]{2,1,0:T(8,128)(2,1)S(1)} copy-done((bf16[3,128,1024]{2,1,0:T(8,128)(2,1)S(1)}, bf16[3,128,1024]{2,1,0:T(8,128)(2,1)}, u32[]{:S(2)}) %copy-start.5) | copy-done | bytes 786456
  26.6 4.1 %attend_forward.2 = (bf16[1024,256]{1,0:T(8,128)(2,1)S(1)}, f32[8,256,256]{2,1,0:T(8,128)S(1)}) custom-call(s32[1]{0:T(128)} %bitcast.pos_ref, s32[24,4]{1,0:T(8,128)S(1)} %copy.12.mask_ref, bf16[3,128,1024]{2,1,0:T(8,128)(2,1)S(1)} %copy-done.5, bf16[3,128,1024]{2,1,0:T(8,128)(2,1)} %collective-permute-done.refs_1_), custom_call_target="tpu_custom_call" | custom-call | tf_op jit(solution)/shard_map/attend_forward/pallas_call | solution.py:146
  30.7 1.6 %collective-permute-start.8 = (bf16[1024,256]{1,0:T(8,128)(2,1)S(1)}, bf16[1024,256]{1,0:T(8,128)(2,1)S(1)}, u32[]{:S(2)}, u32[]{:S(2)}) collective-permute-start(bf16[1024,256]{1,0:T(8,128)(2,1)S(1)} %get-tuple-element.91.outs_ref), channel_id=1, source_target_pairs={{0,4},{2,6},{4,0},{6,2},{8,12},{10,14},{12,8},{14,10},{16,20},{18,... | collective-permute-start | bytes 1572872 | tf_op jit(solution)/shard_map/ppermute | solution.py:430
  32.3 1.1 %collective-permute-done.4.refs_1_ = bf16[160,1536]{1,0:T(8,128)(2,1)S(1)} collective-permute-done((bf16[160,1536]{1,0:T(8,128)(2,1)S(1)}, bf16[160,1536]{1,0:T(8,128)(2,1)S(1)}, u32[]{:S(2)}, u32[]{:S(2)}) %collective-permute-start.4) | collective-permute-done | bytes 491552 | tf_op jit(solution)/shard_map/ppermute | solution.py:430
  34.7 4.9 %collective-permute-done.3.refs_1_ = bf16[2,1280,128]{2,1,0:T(8,128)(2,1)} collective-permute-done((bf16[2,1280,128]{2,1,0:T(8,128)(2,1)S(1)}, bf16[2,1280,128]{2,1,0:T(8,128)(2,1)}, u32[]{:S(2)}, u32[]{:S(2)}) %collective-permute-start.3) | collective-permute-done | bytes 655392 | tf_op jit(solution)/shard_map/ppermute | solution.py:430
  39.7 1.4 %collective-permute-start.11 = (bf16[3,128,512]{2,1,0:T(8,128)(2,1)S(1)}, bf16[3,128,512]{2,1,0:T(8,128)(2,1)S(1)}, u32[]{:S(2)}, u32[]{:S(2)}) collective-permute-start(bf16[3,128,512]{2,1,0:T(8,128)(2,1)S(1)} %copy-done.11), channel_id=1, source_target_pairs={{0,1},{1,0},{2,3},{3,2},{4,5},{5,4},{6,7},{7,6},{8,9},{9,8},{10,11... | collective-permute-start | bytes 1179656 | tf_op jit(solution)/shard_map/ppermute | solution.py:430
  41.1 1.5 %join_pieces.1 = (bf16[1280,512]{1,0:T(8,128)(2,1)S(1)}, bf16[512,1280]{1,0:T(8,128)(2,1)S(1)}) custom-call(bf16[2,1280,128]{2,1,0:T(8,128)(2,1)S(1)} %pad_maximum_fusion.refs_0_, bf16[2,1280,128]{2,1,0:T(8,128)(2,1)} %collective-permute-done.3.refs_1_), custom_call_target="tpu_custom_call" | custom-call | tf_op jit(solution)/shard_map/join_pieces/pallas_call | solution.py:280
  46.2 2.9 %collective-permute-done.11.refs_1_ = bf16[3,128,512]{2,1,0:T(8,128)(2,1)S(1)} collective-permute-done((bf16[3,128,512]{2,1,0:T(8,128)(2,1)S(1)}, bf16[3,128,512]{2,1,0:T(8,128)(2,1)S(1)}, u32[]{:S(2)}, u32[]{:S(2)}) %collective-permute-start.11) | collective-permute-done | bytes 393248 | tf_op jit(solution)/shard_map/ppermute | solution.py:430
  49.9 1.2 %collective-permute-start.14 = (bf16[320,1024]{1,0:T(8,128)(2,1)S(1)}, bf16[320,1024]{1,0:T(8,128)(2,1)S(1)}, u32[]{:S(2)}, u32[]{:S(2)}) collective-permute-start(bf16[320,1024]{1,0:T(8,128)(2,1)S(1)} %columns_sum.13), channel_id=1, source_target_pairs={{0,8},{2,10},{4,12},{6,14},{8,0},{10,2},{12,4},{14,6},{16,24},{18,... | collective-permute-start | bytes 1966088 | tf_op jit(solution)/shard_map/ppermute | solution.py:430
  51.1 1.5 %partial_heads.2 = (f32[256,1024]{1,0:T(8,128)S(1)}, bf16[256,1024]{1,0:T(8,128)(2,1)S(1)}) custom-call(bf16[512,1280]{1,0:T(8,128)(2,1)S(1)} %get-tuple-element.77.grad_ref, bf16[160,1536]{1,0:T(8,128)(2,1)S(1)} %bitcast.10, bf16[160,1536]{1,0:T(8,128)(2,1)S(1)} %collective-permute-done.4.refs_1_, bf16[160,1536]{1,0:T(8,128)(2,1)S(1)} %collective-permute-done.6.refs_2_, ...), custom_call_target="tpu_custom_call" | custom-call | tf_op jit(solution)/shard_map/partial_heads/pallas_call | solution.py:313
  53.3 2.2 %attend_forward.3 = (bf16[512,256]{1,0:T(8,128)(2,1)S(1)}, f32[4,256,256]{2,1,0:T(8,128)S(1)}) custom-call(s32[1]{0:T(128)} %bitcast.pos_ref, s32[24,4]{1,0:T(8,128)S(1)} %copy.12.mask_ref, bf16[3,128,512]{2,1,0:T(8,128)(2,1)S(1)} %get-tuple-element.73.refs_0_, bf16[3,128,512]{2,1,0:T(8,128)(2,1)S(1)} %collective-permute-done.11.refs_1_), custom_call_target="tpu_custom_call" | custom-call | tf_op jit(solution)/shard_map/attend_forward/pallas_call | solution.py:146
  55.5 1.6 %collective-permute-start.19 = (bf16[512,256]{1,0:T(8,128)(2,1)S(1)}, bf16[512,256]{1,0:T(8,128)(2,1)S(1)}, u32[]{:S(2)}, u32[]{:S(2)}) collective-permute-start(bf16[512,256]{1,0:T(8,128)(2,1)S(1)} %get-tuple-element.92.outs_ref), channel_id=1, source_target_pairs={{0,4},{2,6},{4,0},{6,2},{8,12},{10,14},{12,8},{14,10},{16,20},{18,... | collective-permute-start | bytes 786440 | tf_op jit(solution)/shard_map/ppermute | solution.py:430
  57.6 7.1 %collective-permute-done.19.outs_x_ref = bf16[512,256]{1,0:T(8,128)(2,1)S(1)} collective-permute-done((bf16[512,256]{1,0:T(8,128)(2,1)S(1)}, bf16[512,256]{1,0:T(8,128)(2,1)S(1)}, u32[]{:S(2)}, u32[]{:S(2)}) %collective-permute-start.19) | collective-permute-done | bytes 262176 | tf_op jit(solution)/shard_map/ppermute | solution.py:430
  69.1 2.3 %collective-permute-start.27 = (bf16[160,1024]{1,0:T(8,128)(2,1)S(1)}, bf16[160,1024]{1,0:T(8,128)(2,1)S(1)}, u32[]{:S(2)}, u32[]{:S(2)}) collective-permute-start(bf16[160,1024]{1,0:T(8,128)(2,1)S(1)} %columns_sum.15), channel_id=1, source_target_pairs={{0,16},{2,18},{4,20},{6,22},{8,24},{10,26},{12,28},{14,30},{16,0},... | collective-permute-start | bytes 983048 | tf_op jit(solution)/shard_map/ppermute | solution.py:430
  72.2 1.5 %collective-permute-start.25 = (bf16[256,512]{1,0:T(8,128)(2,1)S(1)}, bf16[256,512]{1,0:T(8,128)(2,1)S(1)}, u32[]{:S(2)}, u32[]{:S(2)}) collective-permute-start(bf16[256,512]{1,0:T(8,128)(2,1)S(1)} %get-tuple-element.81), channel_id=1, source_target_pairs={{0,4},{2,6},{4,0},{6,2},{8,12},{10,14},{12,8},{14,10},{16,20},{18,... | collective-permute-start | bytes 786440 | tf_op jit(solution)/shard_map/ppermute | solution.py:430
  74.2 1.7 %collective-permute-done.16.refs_4_ = bf16[256,1024]{1,0:T(8,128)(2,1)S(1)} collective-permute-done((bf16[256,1024]{1,0:T(8,128)(2,1)S(1)}, bf16[256,1024]{1,0:T(8,128)(2,1)S(1)}, u32[]{:S(2)}, u32[]{:S(2)}) %collective-permute-start.16) | collective-permute-done | bytes 524320 | tf_op jit(solution)/shard_map/ppermute | solution.py:430
  75.9 3.7 %attend_backward.2 = (bf16[2,128,1024]{2,1,0:T(8,128)(2,1)S(1)}, bf16[2,128,1024]{2,1,0:T(8,128)(2,1)S(1)}) custom-call(bf16[3,128,1024]{2,1,0:T(8,128)(2,1)S(1)} %copy-done.6, bf16[3,128,1024]{2,1,0:T(8,128)(2,1)} %collective-permute-done.refs_1_, f32[8,256,256]{2,1,0:T(8,128)S(1)} %get-tuple-element.54.refs_2_, f32[256,1024]{1,0:T(8,128)S(1)} %get-tuple-element.70.refs_3_, ...), custom_call_target="tpu_custom_call" | custom-call | flops 3500000000 | tf_op jit(solution)/shard_map/attend_backward/pallas_call | solution.py:162
  79.6 1.6 %collective-permute-start.17 = (bf16[2,128,1024]{2,1,0:T(8,128)(2,1)S(1)}, bf16[2,128,1024]{2,1,0:T(8,128)(2,1)S(1)}, u32[]{:S(2)}, u32[]{:S(2)}) collective-permute-start(bf16[2,128,1024]{2,1,0:T(8,128)(2,1)S(1)} %get-tuple-element.72), channel_id=1, source_target_pairs={{0,1},{1,0},{2,3},{3,2},{4,5},{5,4},{6,7},{7,6},{8,9},{9,8},{10,11... | collective-permute-start | bytes 1572872 | tf_op jit(solution)/shard_map/ppermute | solution.py:430
  81.2 3.3 %collective-permute-done.24.refs_0_ = bf16[320,512]{1,0:T(8,128)(2,1)S(1)} collective-permute-done((bf16[320,512]{1,0:T(8,128)(2,1)S(1)}, bf16[320,512]{1,0:T(8,128)(2,1)S(1)}, u32[]{:S(2)}, u32[]{:S(2)}) %collective-permute-start.24) | collective-permute-done | bytes 327712 | tf_op jit(solution)/shard_map/ppermute | solution.py:430
  84.5 1.3 %attend_backward.3 = (bf16[2,128,512]{2,1,0:T(8,128)(2,1)S(1)}, bf16[2,128,512]{2,1,0:T(8,128)(2,1)S(1)}) custom-call(bf16[3,128,512]{2,1,0:T(8,128)(2,1)S(1)} %get-tuple-element.73.refs_0_, bf16[3,128,512]{2,1,0:T(8,128)(2,1)S(1)} %collective-permute-done.11.refs_1_, f32[4,256,256]{2,1,0:T(8,128)S(1)} %get-tuple-element.74.refs_2_, ...), custom_call_target="tpu_custom_call" | custom-call | tf_op jit(solution)/shard_map/attend_backward/pallas_call | solution.py:162
  85.8 1.6 %collective-permute-start.26 = (bf16[2,128,512]{2,1,0:T(8,128)(2,1)S(1)}, bf16[2,128,512]{2,1,0:T(8,128)(2,1)S(1)}, u32[]{:S(2)}, u32[]{:S(2)}) collective-permute-start(bf16[2,128,512]{2,1,0:T(8,128)(2,1)S(1)} %get-tuple-element.82), channel_id=1, source_target_pairs={{0,1},{1,0},{2,3},{3,2},{4,5},{5,4},{6,7},{7,6},{8,9},{9,8},{10,11... | collective-permute-start | bytes 786440 | tf_op jit(solution)/shard_map/ppermute | solution.py:430
  89.6 7.8 %collective-permute-done.29.refs_3_ = bf16[160,512]{1,0:T(8,128)(2,1)S(1)} collective-permute-done((bf16[160,512]{1,0:T(8,128)(2,1)S(1)}, bf16[160,512]{1,0:T(8,128)(2,1)S(1)}, u32[]{:S(2)}, u32[]{:S(2)}) %collective-permute-start.29) | collective-permute-done | bytes 163872 | tf_op jit(solution)/shard_map/ppermute | solution.py:430
  (91 shorter events, 19.0 us)
Async XLA Ops:
  0.6 13.8 %copy-start.12 = (s32[24,4,4]{0,2,1:T(4,128)S(1)}, s32[24,4,4]{0,2,1:T(4,128)}, u32[]{:S(2)}) copy-start(s32[24,4,4]{0,2,1:T(4,128)} %param.12) | copy-start | bytes 4612
  0.7 13.8 %copy-start.13 = (s32[24,4]{0,1:T(4,128)S(1)}, s32[24,4]{0,1:T(4,128)}, u32[]{:S(2)}) copy-start(s32[24,4]{0,1:T(4,128)} %param.13) | copy-start | bytes 1156
  2.8 20.9 %collective-permute-start = (bf16[3,128,1024]{2,1,0:T(8,128)(2,1)}, bf16[3,128,1024]{2,1,0:T(8,128)(2,1)}, u32[]{:S(2)}, u32[]{:S(2)}) collective-permute-start(bf16[3,128,1024]{2,1,0:T(8,128)(2,1)} %collect_columns.1), channel_id=1, source_target_pairs={{0,1},{1,0},{2,3},{3,2},{4,5},{5,4},{6,7},{7,6},{8,9},{9,8},{10,11... | collective-permute-start | bytes 2359304 | tf_op jit(solution)/shard_map/ppermute | solution.py:430
  8.0 9.2 %collective-permute-start.2 = (bf16[1280,128]{1,0:T(8,128)(2,1)S(1)}, bf16[1280,128]{1,0:T(8,128)(2,1)S(1)}, u32[]{:S(2)}, u32[]{:S(2)}) collective-permute-start(bf16[1280,128]{1,0:T(8,128)(2,1)S(1)} %get-tuple-element.55), channel_id=1, source_target_pairs={{0,4},{2,6},{4,0},{6,2},{8,12},{10,14},{12,8},{14,10},{16,20},{18,... | collective-permute-start | bytes 983048 | tf_op jit(solution)/shard_map/ppermute | solution.py:430
  9.5 23.9 %collective-permute-start.4 = (bf16[160,1536]{1,0:T(8,128)(2,1)S(1)}, bf16[160,1536]{1,0:T(8,128)(2,1)S(1)}, u32[]{:S(2)}, u32[]{:S(2)}) collective-permute-start(bf16[160,1536]{1,0:T(8,128)(2,1)S(1)} %bitcast.6), channel_id=1, source_target_pairs={{0,16},{2,18},{4,20},{6,22},{8,24},{10,26},{12,28},{14,30},{16,0},... | collective-permute-start | bytes 1474568 | tf_op jit(solution)/shard_map/ppermute | solution.py:430
  12.1 22.0 %collective-permute-start.6 = (bf16[160,1536]{1,0:T(8,128)(2,1)S(1)}, bf16[160,1536]{1,0:T(8,128)(2,1)S(1)}, u32[]{:S(2)}, u32[]{:S(2)}) collective-permute-start(bf16[160,1536]{1,0:T(8,128)(2,1)S(1)} %bitcast.7), channel_id=1, source_target_pairs={{0,8},{2,10},{4,12},{6,14},{8,0},{10,2},{12,4},{14,6},{16,24},{18,... | collective-permute-start | bytes 1474568 | tf_op jit(solution)/shard_map/ppermute | solution.py:430
  14.5 11.0 %collective-permute-start.1 = (bf16[160,1024]{1,0:T(8,128)(2,1)}, bf16[160,1024]{1,0:T(8,128)(2,1)S(1)}, u32[]{:S(2)}, u32[]{:S(2)}) collective-permute-start(bf16[160,1024]{1,0:T(8,128)(2,1)} %slice.32), channel_id=1, source_target_pairs={{0,2},{2,0},{4,6},{6,4},{8,10},{10,8},{12,14},{14,12},{16,18},{18,... | collective-permute-start | bytes 983048 | tf_op jit(solution)/shard_map/ppermute | solution.py:430
  23.7 16.0 %collective-permute-start.3 = (bf16[2,1280,128]{2,1,0:T(8,128)(2,1)S(1)}, bf16[2,1280,128]{2,1,0:T(8,128)(2,1)}, u32[]{:S(2)}, u32[]{:S(2)}) collective-permute-start(bf16[2,1280,128]{2,1,0:T(8,128)(2,1)S(1)} %pad_maximum_fusion.refs_0_), channel_id=1, source_target_pairs={{0,1},{1,0},{2,3},{3,2},{4,5},{5,4},{6,7},{7,6},{8,9},{9,8},{10,11... | collective-permute-start | bytes 1966088 | tf_op jit(solution)/shard_map/ppermute | solution.py:430
  30.7 12.6 %collective-permute-start.8 = (bf16[1024,256]{1,0:T(8,128)(2,1)S(1)}, bf16[1024,256]{1,0:T(8,128)(2,1)S(1)}, u32[]{:S(2)}, u32[]{:S(2)}) collective-permute-start(bf16[1024,256]{1,0:T(8,128)(2,1)S(1)} %get-tuple-element.91.outs_ref), channel_id=1, source_target_pairs={{0,4},{2,6},{4,0},{6,2},{8,12},{10,14},{12,8},{14,10},{16,20},{18,... | collective-permute-start | bytes 1572872 | tf_op jit(solution)/shard_map/ppermute | solution.py:430
  33.5 12.0 %collective-permute-start.10 = (bf16[160,1536]{1,0:T(8,128)(2,1)S(1)}, bf16[160,1536]{1,0:T(8,128)(2,1)S(1)}, u32[]{:S(2)}, u32[]{:S(2)}) collective-permute-start(bf16[160,1536]{1,0:T(8,128)(2,1)S(1)} %collective-permute-done.4.refs_1_), channel_id=1, source_target_pairs={{0,8},{2,10},{4,12},{6,14},{8,0},{10,2},{12,4},{14,6},{16,24},{18,... | collective-permute-start | bytes 1474568 | tf_op jit(solution)/shard_map/ppermute | solution.py:430
  34.1 7.1 %collective-permute-start.5 = (bf16[160,1024]{1,0:T(8,128)(2,1)S(1)}, bf16[160,1024]{1,0:T(8,128)(2,1)S(1)}, u32[]{:S(2)}, u32[]{:S(2)}) collective-permute-start(bf16[160,1024]{1,0:T(8,128)(2,1)S(1)} %slice.25), channel_id=1, source_target_pairs={{0,2},{2,0},{4,6},{6,4},{8,10},{10,8},{12,14},{14,12},{16,18},{18,... | collective-permute-start | bytes 983048 | tf_op jit(solution)/shard_map/ppermute | solution.py:430
  34.2 6.9 %collective-permute-start.7 = (bf16[160,1024]{1,0:T(8,128)(2,1)S(1)}, bf16[160,1024]{1,0:T(8,128)(2,1)S(1)}, u32[]{:S(2)}, u32[]{:S(2)}) collective-permute-start(bf16[160,1024]{1,0:T(8,128)(2,1)S(1)} %slice.26), channel_id=1, source_target_pairs={{0,2},{2,0},{4,6},{6,4},{8,10},{10,8},{12,14},{14,12},{16,18},{18,... | collective-permute-start | bytes 983048 | tf_op jit(solution)/shard_map/ppermute | solution.py:430
  39.7 9.4 %collective-permute-start.11 = (bf16[3,128,512]{2,1,0:T(8,128)(2,1)S(1)}, bf16[3,128,512]{2,1,0:T(8,128)(2,1)S(1)}, u32[]{:S(2)}, u32[]{:S(2)}) collective-permute-start(bf16[3,128,512]{2,1,0:T(8,128)(2,1)S(1)} %copy-done.11), channel_id=1, source_target_pairs={{0,1},{1,0},{2,3},{3,2},{4,5},{5,4},{6,7},{7,6},{8,9},{9,8},{10,11... | collective-permute-start | bytes 1179656 | tf_op jit(solution)/shard_map/ppermute | solution.py:430
  43.8 2.3 %collective-permute-start.9 = (bf16[160,1024]{1,0:T(8,128)(2,1)S(1)}, bf16[160,1024]{1,0:T(8,128)(2,1)S(1)}, u32[]{:S(2)}, u32[]{:S(2)}) collective-permute-start(bf16[160,1024]{1,0:T(8,128)(2,1)S(1)} %columns_sum.11), channel_id=1, source_target_pairs={{0,2},{2,0},{4,6},{6,4},{8,10},{10,8},{12,14},{14,12},{16,18},{18,... | collective-permute-start | bytes 983048 | tf_op jit(solution)/shard_map/ppermute | solution.py:430
  44.4 4.7 %collective-permute-start.12 = (bf16[160,1024]{1,0:T(8,128)(2,1)S(1)}, bf16[160,1024]{1,0:T(8,128)(2,1)S(1)}, u32[]{:S(2)}, u32[]{:S(2)}) collective-permute-start(bf16[160,1024]{1,0:T(8,128)(2,1)S(1)} %columns_sum.12), channel_id=1, source_target_pairs={{0,2},{2,0},{4,6},{6,4},{8,10},{10,8},{12,14},{14,12},{16,18},{18,... | collective-permute-start | bytes 983048 | tf_op jit(solution)/shard_map/ppermute | solution.py:430
  45.5 5.6 %collective-permute-start.13 = (bf16[160,1024]{1,0:T(8,128)(2,1)S(1)}, bf16[160,1024]{1,0:T(8,128)(2,1)S(1)}, u32[]{:S(2)}, u32[]{:S(2)}) collective-permute-start(bf16[160,1024]{1,0:T(8,128)(2,1)S(1)} %slice.33), channel_id=1, source_target_pairs={{0,2},{2,0},{4,6},{6,4},{8,10},{10,8},{12,14},{14,12},{16,18},{18,... | collective-permute-start | bytes 983048 | tf_op jit(solution)/shard_map/ppermute | solution.py:430
  45.6 7.7 %collective-permute-start.18 = (bf16[160,512]{1,0:T(8,128)(2,1)S(1)}, bf16[160,512]{1,0:T(8,128)(2,1)S(1)}, u32[]{:S(2)}, u32[]{:S(2)}) collective-permute-start(bf16[160,512]{1,0:T(8,128)(2,1)S(1)} %slice.34), channel_id=1, source_target_pairs={{0,2},{2,0},{4,6},{6,4},{8,10},{10,8},{12,14},{14,12},{16,18},{18,... | collective-permute-start | bytes 491528 | tf_op jit(solution)/shard_map/ppermute | solution.py:430
  49.9 17.0 %collective-permute-start.14 = (bf16[320,1024]{1,0:T(8,128)(2,1)S(1)}, bf16[320,1024]{1,0:T(8,128)(2,1)S(1)}, u32[]{:S(2)}, u32[]{:S(2)}) collective-permute-start(bf16[320,1024]{1,0:T(8,128)(2,1)S(1)} %columns_sum.13), channel_id=1, source_target_pairs={{0,8},{2,10},{4,12},{6,14},{8,0},{10,2},{12,4},{14,6},{16,24},{18,... | collective-permute-start | bytes 1966088 | tf_op jit(solution)/shard_map/ppermute | solution.py:430
  53.2 14.4 %collective-permute-start.15 = (bf16[320,1024]{1,0:T(8,128)(2,1)S(1)}, bf16[320,1024]{1,0:T(8,128)(2,1)S(1)}, u32[]{:S(2)}, u32[]{:S(2)}) collective-permute-start(bf16[320,1024]{1,0:T(8,128)(2,1)S(1)} %columns_sum.14), channel_id=1, source_target_pairs={{0,2},{2,0},{4,6},{6,4},{8,10},{10,8},{12,14},{14,12},{16,18},{18,... | collective-permute-start | bytes 1966088 | tf_op jit(solution)/shard_map/ppermute | solution.py:430
  55.5 9.2 %collective-permute-start.19 = (bf16[512,256]{1,0:T(8,128)(2,1)S(1)}, bf16[512,256]{1,0:T(8,128)(2,1)S(1)}, u32[]{:S(2)}, u32[]{:S(2)}) collective-permute-start(bf16[512,256]{1,0:T(8,128)(2,1)S(1)} %get-tuple-element.92.outs_ref), channel_id=1, source_target_pairs={{0,4},{2,6},{4,0},{6,2},{8,12},{10,14},{12,8},{14,10},{16,20},{18,... | collective-permute-start | bytes 786440 | tf_op jit(solution)/shard_map/ppermute | solution.py:430
  57.1 18.8 %collective-permute-start.16 = (bf16[256,1024]{1,0:T(8,128)(2,1)S(1)}, bf16[256,1024]{1,0:T(8,128)(2,1)S(1)}, u32[]{:S(2)}, u32[]{:S(2)}) collective-permute-start(bf16[256,1024]{1,0:T(8,128)(2,1)S(1)} %get-tuple-element.71), channel_id=1, source_target_pairs={{0,4},{2,6},{4,0},{6,2},{8,12},{10,14},{12,8},{14,10},{16,20},{18,... | collective-permute-start | bytes 1572872 | tf_op jit(solution)/shard_map/ppermute | solution.py:430
  65.0 1.7 %collective-permute-start.20 = (bf16[320,512]{1,0:T(8,128)(2,1)S(1)}, bf16[320,512]{1,0:T(8,128)(2,1)S(1)}, u32[]{:S(2)}, u32[]{:S(2)}) collective-permute-start(bf16[320,512]{1,0:T(8,128)(2,1)S(1)} %columns_sum.16), channel_id=1, source_target_pairs={{0,2},{2,0},{4,6},{6,4},{8,10},{10,8},{12,14},{14,12},{16,18},{18,... | collective-permute-start | bytes 983048 | tf_op jit(solution)/shard_map/ppermute | solution.py:430
  65.1 3.9 %collective-permute-start.21 = (bf16[160,512]{1,0:T(8,128)(2,1)S(1)}, bf16[160,512]{1,0:T(8,128)(2,1)S(1)}, u32[]{:S(2)}, u32[]{:S(2)}) collective-permute-start(bf16[160,512]{1,0:T(8,128)(2,1)S(1)} %slice.35), channel_id=1, source_target_pairs={{0,2},{2,0},{4,6},{6,4},{8,10},{10,8},{12,14},{14,12},{16,18},{18,... | collective-permute-start | bytes 491528 | tf_op jit(solution)/shard_map/ppermute | solution.py:430
  66.7 4.6 %collective-permute-start.22 = (bf16[160,512]{1,0:T(8,128)(2,1)S(1)}, bf16[160,512]{1,0:T(8,128)(2,1)S(1)}, u32[]{:S(2)}, u32[]{:S(2)}) collective-permute-start(bf16[160,512]{1,0:T(8,128)(2,1)S(1)} %slice.36), channel_id=1, source_target_pairs={{0,2},{2,0},{4,6},{6,4},{8,10},{10,8},{12,14},{14,12},{16,18},{18,... | collective-permute-start | bytes 491528 | tf_op jit(solution)/shard_map/ppermute | solution.py:430
  66.9 4.5 %collective-permute-start.23 = (bf16[160,512]{1,0:T(8,128)(2,1)S(1)}, bf16[160,512]{1,0:T(8,128)(2,1)S(1)}, u32[]{:S(2)}, u32[]{:S(2)}) collective-permute-start(bf16[160,512]{1,0:T(8,128)(2,1)S(1)} %slice.37), channel_id=1, source_target_pairs={{0,2},{2,0},{4,6},{6,4},{8,10},{10,8},{12,14},{14,12},{16,18},{18,... | collective-permute-start | bytes 491528 | tf_op jit(solution)/shard_map/ppermute | solution.py:430
  67.6 16.8 %collective-permute-start.24 = (bf16[320,512]{1,0:T(8,128)(2,1)S(1)}, bf16[320,512]{1,0:T(8,128)(2,1)S(1)}, u32[]{:S(2)}, u32[]{:S(2)}) collective-permute-start(bf16[320,512]{1,0:T(8,128)(2,1)S(1)} %columns_sum.17), channel_id=1, source_target_pairs={{0,8},{2,10},{4,12},{6,14},{8,0},{10,2},{12,4},{14,6},{16,24},{18,... | collective-permute-start | bytes 983048 | tf_op jit(solution)/shard_map/ppermute | solution.py:430
  69.1 16.7 %collective-permute-start.27 = (bf16[160,1024]{1,0:T(8,128)(2,1)S(1)}, bf16[160,1024]{1,0:T(8,128)(2,1)S(1)}, u32[]{:S(2)}, u32[]{:S(2)}) collective-permute-start(bf16[160,1024]{1,0:T(8,128)(2,1)S(1)} %columns_sum.15), channel_id=1, source_target_pairs={{0,16},{2,18},{4,20},{6,22},{8,24},{10,26},{12,28},{14,30},{16,0},... | collective-permute-start | bytes 983048 | tf_op jit(solution)/shard_map/ppermute | solution.py:430
  72.2 12.3 %collective-permute-start.25 = (bf16[256,512]{1,0:T(8,128)(2,1)S(1)}, bf16[256,512]{1,0:T(8,128)(2,1)S(1)}, u32[]{:S(2)}, u32[]{:S(2)}) collective-permute-start(bf16[256,512]{1,0:T(8,128)(2,1)S(1)} %get-tuple-element.81), channel_id=1, source_target_pairs={{0,4},{2,6},{4,0},{6,2},{8,12},{10,14},{12,8},{14,10},{16,20},{18,... | collective-permute-start | bytes 786440 | tf_op jit(solution)/shard_map/ppermute | solution.py:430
  74.1 13.3 %collective-permute-start.28 = (bf16[320,512]{1,0:T(8,128)(2,1)S(1)}, bf16[320,512]{1,0:T(8,128)(2,1)S(1)}, u32[]{:S(2)}, u32[]{:S(2)}) collective-permute-start(bf16[320,512]{1,0:T(8,128)(2,1)S(1)} %columns_sum.18), channel_id=1, source_target_pairs={{0,2},{2,0},{4,6},{6,4},{8,10},{10,8},{12,14},{14,12},{16,18},{18,... | collective-permute-start | bytes 983048 | tf_op jit(solution)/shard_map/ppermute | solution.py:430
  79.6 18.8 %collective-permute-start.17 = (bf16[2,128,1024]{2,1,0:T(8,128)(2,1)S(1)}, bf16[2,128,1024]{2,1,0:T(8,128)(2,1)S(1)}, u32[]{:S(2)}, u32[]{:S(2)}) collective-permute-start(bf16[2,128,1024]{2,1,0:T(8,128)(2,1)S(1)} %get-tuple-element.72), channel_id=1, source_target_pairs={{0,1},{1,0},{2,3},{3,2},{4,5},{5,4},{6,7},{7,6},{8,9},{9,8},{10,11... | collective-permute-start | bytes 1572872 | tf_op jit(solution)/shard_map/ppermute | solution.py:430
  85.8 12.6 %collective-permute-start.26 = (bf16[2,128,512]{2,1,0:T(8,128)(2,1)S(1)}, bf16[2,128,512]{2,1,0:T(8,128)(2,1)S(1)}, u32[]{:S(2)}, u32[]{:S(2)}) collective-permute-start(bf16[2,128,512]{2,1,0:T(8,128)(2,1)S(1)} %get-tuple-element.82), channel_id=1, source_target_pairs={{0,1},{1,0},{2,3},{3,2},{4,5},{5,4},{6,7},{7,6},{8,9},{9,8},{10,11... | collective-permute-start | bytes 786440 | tf_op jit(solution)/shard_map/ppermute | solution.py:430
  87.7 9.6 %collective-permute-start.29 = (bf16[160,512]{1,0:T(8,128)(2,1)S(1)}, bf16[160,512]{1,0:T(8,128)(2,1)S(1)}, u32[]{:S(2)}, u32[]{:S(2)}) collective-permute-start(bf16[160,512]{1,0:T(8,128)(2,1)S(1)} %columns_sum.19), channel_id=1, source_target_pairs={{0,16},{2,18},{4,20},{6,22},{8,24},{10,26},{12,28},{14,30},{16,0},... | collective-permute-start | bytes 491528 | tf_op jit(solution)/shard_map/ppermute | solution.py:430
  (12 other events, 66.7 us)
